TPU v7x, 32 devices: a whole 2x2x4 slice. The times are simulated.
32 devices in a mesh: gx: 2 (over y), gy: 4 (over z), gz: 4 (over x, core).
Axes of the slice: x: 2, y: 2, z: 4, core: 2. Of those that a mesh axis runs over, the one named last changes fastest.
Arguments:
- tokens: bfloat16 [256, 8192], P('gx', 'gz'), may hold values from -6 to 6
- gate_weight: bfloat16 [8192, 14336], P('gz', ('gx', 'gy')), may hold values from -0.0625 to 0.0625
- up_weight: bfloat16 [8192, 14336], P('gz', ('gx', 'gy')), may hold values from -0.0625 to 0.0625
- down_weight: bfloat16 [14336, 8192], P(('gx', 'gy'), 'gz'), may hold values from -0.046875 to 0.046875
- out_grad: bfloat16 [256, 8192], P('gx', 'gz'), may hold values from -6 to 6
Outputs:
- output: bfloat16 [256, 8192], P('gx', 'gz')
- input_grad: bfloat16 [256, 8192], P('gx', 'gz')
- gate_grad: bfloat16 [8192, 14336], P('gz', ('gx', 'gy'))
- up_grad: bfloat16 [8192, 14336], P('gz', ('gx', 'gy'))
- down_grad: bfloat16 [14336, 8192], P(('gx', 'gy'), 'gz')
All inputs are finite; a program needn't handle non-finite values.
Results may differ from a plain program's by a relative error of at most 0.025.
Values may be sent and summed in bfloat16 or wider, within the bound.
A program may use at most 128 MiB of HBM per device.

v0:
```python
import jax
import jax.numpy as jnp
from jax import lax
from jax.sharding import PartitionSpec as P


def contract_rows(left, right):
    return lax.dot_general(
        left, right, (((0,), (0,)), ((), ())), preferred_element_type=jnp.float32
    )


def contract_cols(left, right):
    return lax.dot_general(
        left, right, (((1,), (1,)), ((), ())), preferred_element_type=jnp.float32
    )


def activate(gate, upward):
    sigmoid = jax.nn.sigmoid(gate)
    hidden = (gate * sigmoid * upward).astype(jnp.bfloat16)
    return (hidden, sigmoid)


def backward_gates(dhidden, gate, upward, sigmoid):
    dgate = (dhidden * upward * sigmoid * (1.0 + gate * (1.0 - sigmoid))).astype(jnp.bfloat16)
    dupward = (dhidden * gate * sigmoid).astype(jnp.bfloat16)
    return (dgate, dupward)


def body(tokens, gate_weight, up_weight, down_weight, out_grad):
    all_tokens = lax.all_gather(tokens, "gx", axis=0, tiled=True)
    gate_part = jnp.dot(all_tokens, gate_weight, preferred_element_type=jnp.float32)
    up_part = jnp.dot(all_tokens, up_weight, preferred_element_type=jnp.float32)
    gate, upward = (
        lax.psum_scatter(
            gate_part.astype(jnp.bfloat16), "gz", scatter_dimension=0, tiled=True
        ).astype(jnp.float32),
        lax.psum_scatter(
            up_part.astype(jnp.bfloat16), "gz", scatter_dimension=0, tiled=True
        ).astype(jnp.float32),
    )
    hidden_own, sigmoid = activate(gate, upward)
    hidden_all = lax.all_gather(hidden_own, "gz", axis=0, tiled=True)
    hidden_mine = lax.all_to_all(hidden_all, "gx", split_axis=0, concat_axis=1, tiled=True)
    output_part = jnp.dot(
        hidden_mine,
        lax.all_gather(down_weight, "gx", axis=0, tiled=True),
        preferred_element_type=jnp.float32,
    )
    output = lax.psum(output_part.astype(jnp.bfloat16), "gy")
    all_grad = lax.all_gather(out_grad, "gx", axis=0, tiled=True)
    dhidden_part = contract_cols(all_grad, down_weight)
    dhidden = lax.psum_scatter(
        dhidden_part.astype(jnp.bfloat16), "gz", scatter_dimension=0, tiled=True
    ).astype(jnp.float32)
    dgate_own, dup_own = backward_gates(dhidden, gate, upward, sigmoid)
    dgate_all, dup_all = (
        lax.all_gather(dgate_own, "gz", axis=0, tiled=True),
        lax.all_gather(dup_own, "gz", axis=0, tiled=True),
    )
    input_part = lax.psum_scatter(
        (contract_cols(dgate_all, gate_weight) + contract_cols(dup_all, up_weight)).astype(
            jnp.bfloat16
        ),
        "gx",
        scatter_dimension=0,
        tiled=True,
    )
    input_grad = lax.psum(input_part, "gy")
    gate_grad = contract_rows(all_tokens, dgate_all).astype(jnp.bfloat16)
    up_grad = contract_rows(all_tokens, dup_all).astype(jnp.bfloat16)
    down_grad = contract_rows(hidden_all, all_grad).astype(jnp.bfloat16)
    return (output, input_grad, gate_grad, up_grad, down_grad)


def solution(mesh):
    return jax.shard_map(
        body,
        mesh=mesh,
        in_specs=(
            P("gx", "gz"),
            P("gz", ("gx", "gy")),
            P("gz", ("gx", "gy")),
            P(("gx", "gy"), "gz"),
            P("gx", "gz"),
        ),
        out_specs=(
            P("gx", "gz"),
            P("gx", "gz"),
            P("gz", ("gx", "gy")),
            P("gz", ("gx", "gy")),
            P(("gx", "gy"), "gz"),
        ),
        check_vma=False,
    )
```

profile of v0, /device:TPU:0, one launch (start us, length us, event | category | flops | bytes accessed | tf_op | source)
XLA Modules:
  0.0 414.0 jit_solution(18516077754030057)
XLA Ops:
  7.2 0.0 all-gather.4.cloned.1.call-start
  7.2 0.7 all-gather.4.cloned.1.call-update
  7.9 0.0 all-gather.8.cloned.1.call-start
  7.9 0.7 all-gather.8.cloned.1.call-update
  8.6 0.0 reduce-scatter.5.cloned.1.call-start
  8.7 24.9 %all-gather.4.cloned.1.call-done = bf16[256,2048]{1,0:T(8,128)(2,1)} async-done(((bf16[128,2048]{1,0:T(8,128)(2,1)}), bf16[256,2048]{1,0:T(8,128)(2,1)}) %all-gather.4.cloned.1.call-update) | async-done | bytes 1048592 | tf_op jit(solution)/shard_map/all_gather | solution.py:32
  33.6 6.5 %convolution_convert_fusion.5 = bf16[256,1792]{1,0:T(8,128)(2,1)} fusion(bf16[256,2048]{1,0:T(8,128)(2,1)} %all-gather.4.cloned.1.call-done, bf16[2048,1792]{1,0:T(8,128)(2,1)} %param.6), kind=kOutput, calls=%fused_computation.8 | convolution fusion | flops 1879506944 | bytes 9306112 | tf_op jit(solution)/shard_map/dot_general | solution.py:33
  40.1 0.0 reduce-scatter.5.cloned.1.call-update
  40.1 0.0 reduce-scatter.7.cloned.1.call-start
  40.1 0.0 copy-done.1
  40.1 6.4 %convolution_convert_fusion.4 = bf16[256,1792]{1,0:T(8,128)(2,1)} fusion(bf16[256,2048]{1,0:T(8,128)(2,1)S(1)} %copy-done.1, bf16[2048,1792]{1,0:T(8,128)(2,1)} %param.7), kind=kOutput, calls=%fused_computation.7 | convolution fusion | flops 1879506944 | bytes 9306112 | tf_op jit(solution)/shard_map/dot_general | solution.py:34
  46.6 0.0 reduce-scatter.7.cloned.1.call-update
  46.6 0.0 reduce-scatter.9.cloned.1.call-start
  46.7 9.8 %all-gather.8.cloned.1.call-done = bf16[256,2048]{1,0:T(8,128)(2,1)} async-done(((bf16[128,2048]{1,0:T(8,128)(2,1)}), bf16[256,2048]{1,0:T(8,128)(2,1)}) %all-gather.8.cloned.1.call-update) | async-done | bytes 1048592 | tf_op jit(solution)/shard_map/all_gather | solution.py:52
  56.5 6.4 %convolution_convert_fusion.3 = bf16[256,1792]{1,0:T(8,128)(2,1)} fusion(bf16[256,2048]{1,0:T(8,128)(2,1)} %all-gather.8.cloned.1.call-done, bf16[1792,2048]{1,0:T(8,128)(2,1)} %param.8), kind=kOutput, calls=%fused_computation.6 | convolution fusion | flops 1879506944 | bytes 9306112 | tf_op jit(solution)/shard_map/dot_general | solution.py:14
  62.9 0.0 reduce-scatter.9.cloned.1.call-update
  62.9 0.0 all-gather.6.cloned.1.call-start
  63.0 0.5 all-gather.6.cloned.1.call-update
  63.5 0.0 reduce-scatter.11.cloned.1.call-start
  63.6 20.1 %reduce-scatter.5.cloned.1.call-done = bf16[64,1792]{1,0:T(8,128)(2,1)} async-done(((bf16[256,1792]{1,0:T(8,128)(2,1)}), bf16[64,1792]{1,0:T(8,128)(2,1)}) %reduce-scatter.5.cloned.1.call-update) | async-done | bytes 229392 | tf_op jit(solution)/shard_map/reduce_scatter | solution.py:36
  83.7 27.3 %reduce-scatter.7.cloned.1.call-done = bf16[64,1792]{1,0:T(8,128)(2,1)} async-done(((bf16[256,1792]{1,0:T(8,128)(2,1)}), bf16[64,1792]{1,0:T(8,128)(2,1)}) %reduce-scatter.7.cloned.1.call-update) | async-done | bytes 229392 | tf_op jit(solution)/shard_map/reduce_scatter | solution.py:39
  111.0 27.1 %reduce-scatter.9.cloned.1.call-done = bf16[64,1792]{1,0:T(8,128)(2,1)} async-done(((bf16[256,1792]{1,0:T(8,128)(2,1)}), bf16[64,1792]{1,0:T(8,128)(2,1)}) %reduce-scatter.9.cloned.1.call-update) | async-done | bytes 229392 | tf_op jit(solution)/shard_map/reduce_scatter | solution.py:54
  138.1 1.4 fusion.12
  139.5 0.0 slice-start
  139.5 9.1 %all_gather.22 = bf16[256,1792]{1,0:T(8,128)(2,1)S(1)} all-gather(bf16[64,1792]{1,0:T(8,128)(2,1)S(1)} %get-tuple-element.18), channel_id=1, replica_groups=mesh['gx'=2,'gy'=4,'gz'=4] {'gz'}, dimensions={0}, use_global_device_ids=true | all-gather | bytes 1146880 | tf_op jit(solution)/shard_map/all_gather | solution.py:59
  148.6 9.4 %all_gather.23 = bf16[256,1792]{1,0:T(8,128)(2,1)S(1)} all-gather(bf16[64,1792]{1,0:T(8,128)(2,1)S(1)} %get-tuple-element.17), channel_id=1, replica_groups=mesh['gx'=2,'gy'=4,'gz'=4] {'gz'}, dimensions={0}, use_global_device_ids=true | all-gather | bytes 1146880 | tf_op jit(solution)/shard_map/all_gather | solution.py:60
  158.0 0.0 copy-done
  158.0 6.0 %fusion.13 = f32[256,2048]{1,0:T(8,128)S(1)} fusion(bf16[256,1792]{1,0:T(8,128)(2,1)S(1)} %all_gather.22, bf16[2048,1792]{1,0:T(8,128)(2,1)} %param.6), kind=kOutput, calls=%fused_computation.27 | convolution fusion | flops 1879048192 | bytes 10354688 | tf_op jit(solution)/shard_map/dot_general | solution.py:14
  164.0 0.0 slice-done
  164.0 0.0 slice-done.1
  164.1 3.1 fusion.2
  167.1 0.0 reduce-scatter.11.cloned.1.call-update
  167.2 0.0 all-reduce.3.cloned.1.call-start
  167.2 9.4 %all_gather.19 = bf16[256,1792]{1,0:T(8,128)(2,1)S(1)} all-gather(bf16[64,1792]{1,0:T(8,128)(2,1)S(1)} %get-tuple-element.19), channel_id=1, replica_groups=mesh['gx'=2,'gy'=4,'gz'=4] {'gz'}, dimensions={0}, use_global_device_ids=true | all-gather | bytes 1146880 | tf_op jit(solution)/shard_map/all_gather | solution.py:44
  176.6 1.3 copy.12
  177.9 26.7 %all_to_all.19 = bf16[2,128,1792]{1,2,0:T(8,128)(2,1)S(1)} all-to-all(bf16[2,128,1792]{1,2,0:T(8,128)(2,1)} %copy.12), channel_id=1, replica_groups=mesh['gx'=2,'gy'=4,'gz'=4] {'gx'}, dimensions={0} | all-to-all | bytes 1835008 | tf_op jit(solution)/shard_map/all_to_all | solution.py:45
  204.6 120.3 %all-gather.6.cloned.1.call-done = bf16[3584,2048]{1,0:T(8,128)(2,1)} async-done(((bf16[1792,2048]{1,0:T(8,128)(2,1)}), bf16[3584,2048]{1,0:T(8,128)(2,1)}) %all-gather.6.cloned.1.call-update) | async-done | bytes 14680080 | tf_op jit(solution)/shard_map/all_gather | solution.py:48
  325.0 8.1 %convolution_convert_fusion.6 = bf16[128,2048]{1,0:T(8,128)(2,1)} fusion(bf16[128,3584]{0,1:T(8,128)(2,1)S(1)} %bitcast.27, bf16[3584,2048]{1,0:T(8,128)(2,1)} %all-gather.6.cloned.1.call-done), kind=kOutput, calls=%fused_computation.10 | convolution fusion | flops 1879310336 | bytes 16121856 | tf_op jit(solution)/shard_map/dot_general | solution.py:46
  333.0 15.2 %reduce-scatter.11.cloned.1.call-done = bf16[128,2048]{1,0:T(8,128)(2,1)} async-done(((bf16[256,2048]{1,0:T(8,128)(2,1)}), bf16[128,2048]{1,0:T(8,128)(2,1)}) %reduce-scatter.11.cloned.1.call-update) | async-done | bytes 524304 | tf_op jit(solution)/shard_map/reduce_scatter | solution.py:62
  348.2 0.0 all-reduce.3.cloned.1.call-update
  348.2 6.7 %fusion = bf16[2048,1792]{0,1:T(8,128)(2,1)} fusion(bf16[256,1792]{1,0:T(8,128)(2,1)} %copy-done, bf16[256,2048]{1,0:T(8,128)(2,1)} %all-gather.4.cloned.1.call-done), kind=kOutput, calls=%fused_computation.3 | convolution fusion | flops 1882718208 | bytes 9306112 | tf_op jit(solution)/shard_map/dot_general | solution.py:8
  354.9 10.0 %copy.13 = bf16[2048,1792]{1,0:T(8,128)(2,1)} copy(bf16[2048,1792]{0,1:T(8,128)(2,1)} %fusion) | data formatting | bytes 14680064
  364.8 6.4 %fusion.1 = bf16[2048,1792]{0,1:T(8,128)(2,1)} fusion(bf16[256,1792]{1,0:T(8,128)(2,1)S(1)} %all_gather.23, bf16[256,2048]{1,0:T(8,128)(2,1)} %all-gather.4.cloned.1.call-done), kind=kOutput, calls=%fused_computation.4 | convolution fusion | flops 1882718208 | bytes 9306112 | tf_op jit(solution)/shard_map/dot_general | solution.py:8
  371.2 10.0 %copy.14 = bf16[2048,1792]{1,0:T(8,128)(2,1)} copy(bf16[2048,1792]{0,1:T(8,128)(2,1)} %fusion.1) | data formatting | bytes 14680064
  381.3 5.1 %convolution_convert_fusion = bf16[1792,2048]{1,0:T(8,128)(2,1)} fusion(bf16[256,1792]{1,0:T(8,128)(2,1)S(1)} %all_gather.19, bf16[256,2048]{1,0:T(8,128)(2,1)S(1)} %copy-done.2), kind=kOutput, calls=%fused_computation | convolution fusion | flops 1882718208 | bytes 9306112 | tf_op jit(solution)/shard_map/dot_general | solution.py:8
  386.4 17.0 %all-reduce.3.cloned.1.call-done = (bf16[128,2048]{1,0:T(8,128)(2,1)}, bf16[128,2048]{1,0:T(8,128)(2,1)}) async-done(((bf16[128,2048]{1,0:T(8,128)(2,1)}, bf16[128,2048]{1,0:T(8,128)(2,1)}), (bf16[128,2048]{1,0:T(8,128)(2,1)}, bf16[128,2048]{1,0:T(8,128)(2,1)})) %all-reduce.3.cloned.1.call-update) | async-done | bytes 1048592 | tf_op jit(solution)/shard_map/psum | solution.py:51
  403.4 1.9 copy.17
  405.3 1.9 copy.18
  (6 shorter events, 0.0 us)
Async XLA Ops:
  7.2 26.4 %all-gather.4.cloned.1.call-start = ((), (), s32[]{:S(2)}) async-start(), calls=%async_computation.5 | async-start | bytes 1572864 | tf_op jit(solution)/shard_map/all_gather | solution.py:32
  7.9 48.6 %all-gather.8.cloned.1.call-start = ((), (), s32[]{:S(2)}) async-start(), calls=%async_computation.9 | async-start | bytes 1572864 | tf_op jit(solution)/shard_map/all_gather | solution.py:52
  8.6 75.0 %reduce-scatter.5.cloned.1.call-start = ((), (), s32[]{:S(2)}) async-start(), calls=%async_computation.6 | async-start | bytes 1146880 | tf_op jit(solution)/shard_map/reduce_scatter | solution.py:36
  33.6 6.5 %copy-start.1 = (bf16[256,2048]{1,0:T(8,128)(2,1)S(1)}, bf16[256,2048]{1,0:T(8,128)(2,1)}, u32[]{:S(2)}) copy-start(bf16[256,2048]{1,0:T(8,128)(2,1)} %all-gather.4.cloned.1.call-done) | copy-start | bytes 3145732
  40.1 70.9 %reduce-scatter.7.cloned.1.call-start = ((), (), s32[]{:S(2)}) async-start(), calls=%async_computation.7 | async-start | bytes 1146880 | tf_op jit(solution)/shard_map/reduce_scatter | solution.py:39
  46.6 91.5 %reduce-scatter.9.cloned.1.call-start = ((), (), s32[]{:S(2)}) async-start(), calls=%async_computation.10 | async-start | bytes 1146880 | tf_op jit(solution)/shard_map/reduce_scatter | solution.py:54
  62.9 262.0 %all-gather.6.cloned.1.call-start = ((), (), s32[]{:S(2)}) async-start(), calls=%async_computation.8 | async-start | bytes 22020096 | tf_op jit(solution)/shard_map/all_gather | solution.py:48
  63.5 284.7 %reduce-scatter.11.cloned.1.call-start = ((), (), s32[]{:S(2)}) async-start(), calls=%async_computation.11 | async-start | bytes 1572864 | tf_op jit(solution)/shard_map/reduce_scatter | solution.py:62
  139.5 24.5 %slice-start = ((s8[7340032]{0:T(1024)(128)(4,1)}), s8[4194304]{0:T(1024)(128)(4,1)S(1)}, s32[]{:S(2)}) async-start(s8[7340032]{0:T(1024)(128)(4,1)} %bitcast.28), calls=%async_computation.13 | async-start | bytes 8388608
  148.6 9.4 %copy-start = (bf16[256,1792]{1,0:T(8,128)(2,1)}, bf16[256,1792]{1,0:T(8,128)(2,1)S(1)}, u32[]{:S(2)}) copy-start(bf16[256,1792]{1,0:T(8,128)(2,1)S(1)} %all_gather.22) | copy-start | bytes 2752516
  158.0 6.0 %slice-start.1 = ((s8[7340032]{0:T(1024)(128)(4,1)}), s8[3145728]{0:T(1024)(128)(4,1)S(1)}, s32[]{:S(2)}) async-start(s8[7340032]{0:T(1024)(128)(4,1)} %bitcast.28), calls=%async_computation.14 | async-start | bytes 6291456
  167.2 236.2 %all-reduce.3.cloned.1.call-start = ((), (), s32[]{:S(2)}) async-start(), calls=%async_computation.12 | async-start | bytes 2097152 | tf_op jit(solution)/shard_map/psum | solution.py:51
  371.2 10.0 %copy-start.2 = (bf16[256,2048]{1,0:T(8,128)(2,1)S(1)}, bf16[256,2048]{1,0:T(8,128)(2,1)}, u32[]{:S(2)}) copy-start(bf16[256,2048]{1,0:T(8,128)(2,1)} %all-gather.8.cloned.1.call-done) | copy-start | bytes 3145732
Sparse Core Ops, SparseCore 0:
  9.5 23.9 all-gather.3
  35.1 21.2 all-gather.7
  59.6 24.0 reduce-scatter.4
  86.9 24.0 reduce-scatter.6
  114.0 24.0 reduce-scatter.8
  139.5 185.3 all-gather.5
  327.9 20.3 reduce-scatter.10
  351.2 52.1 all-reduce.2
where the time goes:
time: 415 us; the launch traced here: 414 us
  waiting for transfers between devices  264 us (64%)
  matrix products  54.7 us (13%)
  blocking collectives  54.6 us (13%)
  local copies, waits for them, and re-layouts  25 us (6%)
  between operations  14.2 us (3%)
    all_gather x1, waiting for transfers between devices, body(): lax.all_gather(down_weight, 'gx', axis=0, tiled=True)  120 us
    reduce_scatter x1, waiting for transfers between devices, body(): lax.psum_scatter(up_part.astype(jnp.bfloat16), 'gz', scatter_dimension=0,...  27.3 us
    reduce_scatter x1, waiting for transfers between devices, body(): lax.psum_scatter(dhidden_part.astype(jnp.bfloat16), 'gz', scatter_dimensi...  27.1 us
    all_to_all x1, blocking collectives, body(): lax.all_to_all(hidden_all, 'gx', split_axis=0, concat_axis=1, tiled=True)  26.7 us
    all_gather x1, waiting for transfers between devices, body(): all_tokens = lax.all_gather(tokens, 'gx', axis=0, tiled=True)  24.9 us
    unnamed x14, local copies, waits for them, and re-layouts  23.8 us
    reduce_scatter x1, waiting for transfers between devices, body(): lax.psum_scatter(gate_part.astype(jnp.bfloat16), 'gz', scatter_dimension=...  20.1 us
    dot_general x3, matrix products, contract_rows(): lax.dot_general(left, right, (((0,), (0,)), ((), ())), preferred_element_...  18.2 us
  transfers between devices with their start and end apart: 8, of which 8 were waited for; matrix products, arithmetic and copies ran while one was open for 19% of the time, Pallas kernels for 0%

commit v1 on v0

v1 whole, which is shorter than its diff:
```python
import jax
import jax.numpy as jnp
from jax import lax
from jax.experimental import pallas as pl
from jax.experimental.pallas import tpu as pltpu
from jax.sharding import PartitionSpec as P

BF16 = jnp.bfloat16
F32 = jnp.float32
CORES = 2


def dot(left, right):
    return jnp.dot(left, right, preferred_element_type=F32)


def contract_cols(left, right):
    return lax.dot_general(
        left, right, (((1,), (1,)), ((), ())), preferred_element_type=F32
    )


def tile_of(extent):
    for tile in (256, 128):
        if extent % tile == 0:
            return tile
    return extent


def weight_grad_kernel(left_ref, right_ref, out_ref):
    out_ref[...] = lax.dot_general(
        left_ref[...], right_ref[...], (((0,), (0,)), ((), ())), preferred_element_type=F32
    ).astype(BF16)


def weight_grad(left, right):
    rows, height = left.shape
    width = right.shape[1]
    tile = tile_of(height)
    return pl.pallas_call(
        weight_grad_kernel,
        out_shape=jax.ShapeDtypeStruct((height, width), BF16),
        grid=(height // tile,),
        in_specs=[
            pl.BlockSpec((rows, tile), lambda i: (0, i)),
            pl.BlockSpec((rows, width), lambda i: (0, 0)),
        ],
        out_specs=pl.BlockSpec((tile, width), lambda i: (i, 0)),
        compiler_params=pltpu.CompilerParams(vmem_limit_bytes=24 * 2**20),
        cost_estimate=pl.CostEstimate(
            flops=2 * rows * height * width,
            bytes_accessed=2 * (height * width + rows * (height + width)),
            transcendentals=0,
        ),
    )(left, right)


def shift(x, axis, step):
    n = lax.axis_size(axis)
    return lax.ppermute(x, axis, [(i, (i + step) % n) for i in range(n)])


def other_core(x):
    n = lax.axis_size("gz")
    return lax.ppermute(x, "gz", [(i, i ^ 1) for i in range(n)])


def shift_chip(x, step):
    n = lax.axis_size("gz")
    chips = n // CORES
    return lax.ppermute(
        x, "gz", [(i, (i // CORES + step) % chips * CORES + i % CORES) for i in range(n)]
    )


def gather_gx(own):
    return [own] + [shift(own, "gx", k) for k in range(1, lax.axis_size("gx"))]


def reduce_gz(part):
    half = part.shape[0] // CORES
    total = part[:half].astype(F32) + other_core(part[half:]).astype(F32)
    sent = total.astype(BF16)
    for k in range(1, lax.axis_size("gz") // CORES):
        total = total + shift_chip(sent, k).astype(F32)
    return total


def join_cores(own):
    return jnp.concatenate([own, other_core(own)], axis=0)


def reduce_terms(terms):
    total = terms[0].astype(F32)
    for k in range(1, len(terms)):
        total = total + shift(terms[k], "gx", -k).astype(F32)
    rows, width = total.shape
    n = lax.axis_size("gy")
    me = lax.axis_index("gy")
    core = lax.rem(lax.axis_index("gz"), CORES)
    piece = rows // n
    total = total.astype(BF16)

    def slot(k):
        return lax.rem(me + k, n) * piece

    mine = lax.dynamic_slice_in_dim(total, slot(0), piece, 0).astype(F32)
    for k in range(1, n):
        mine = mine + shift(lax.dynamic_slice_in_dim(total, slot(k), piece, 0), "gy", k).astype(F32)
    mine = mine.astype(BF16)
    result = jnp.zeros((rows, width), BF16)
    for k in range(n):
        got = mine if k == 0 else shift(mine, "gy", k)
        at = lax.rem(slot(n - k) + core * (rows // CORES), rows)
        result = lax.dynamic_update_slice_in_dim(result, got, at, 0)
    return result


def body(tokens, gate_weight, up_weight, down_weight, out_grad):
    core = lax.rem(lax.axis_index("gz"), CORES)
    rows = tokens.shape[0]

    def own_half_first(x):
        return lax.dynamic_slice_in_dim(
            jnp.concatenate([x, x], axis=0), core * (rows // CORES), rows, 0
        )

    toks = gather_gx(own_half_first(tokens))
    grads = gather_gx(own_half_first(out_grad))
    hiddens, dgates, dups, acts = [], [], [], []
    for tok in toks:
        gate = reduce_gz(dot(tok, gate_weight).astype(BF16))
        upward = reduce_gz(dot(tok, up_weight).astype(BF16))
        sig = jax.nn.sigmoid(gate)
        hiddens.append(join_cores((gate * sig * upward).astype(BF16)))
        acts.append((gate, upward, sig))
    output = reduce_terms([dot(h, down_weight).astype(BF16) for h in hiddens])
    for grad, (gate, upward, sig) in zip(grads, acts):
        dhidden = reduce_gz(contract_cols(grad, down_weight).astype(BF16))
        dgates.append(
            join_cores((dhidden * upward * sig * (1.0 + gate * (1.0 - sig))).astype(BF16))
        )
        dups.append(join_cores((dhidden * gate * sig).astype(BF16)))
    input_grad = reduce_terms(
        [
            (contract_cols(dg, gate_weight) + contract_cols(du, up_weight)).astype(BF16)
            for dg, du in zip(dgates, dups)
        ]
    )
    all_tokens = jnp.concatenate(toks, axis=0)
    down_grad = weight_grad(jnp.concatenate(hiddens, axis=0), jnp.concatenate(grads, axis=0))
    gate_grad = weight_grad(all_tokens, jnp.concatenate(dgates, axis=0))
    up_grad = weight_grad(all_tokens, jnp.concatenate(dups, axis=0))
    return (output, input_grad, gate_grad, up_grad, down_grad)


def solution(mesh):
    return jax.shard_map(
        body,
        mesh=mesh,
        in_specs=(
            P("gx", "gz"),
            P("gz", ("gx", "gy")),
            P("gz", ("gx", "gy")),
            P(("gx", "gy"), "gz"),
            P("gx", "gz"),
        ),
        out_specs=(
            P("gx", "gz"),
            P("gx", "gz"),
            P("gz", ("gx", "gy")),
            P("gz", ("gx", "gy")),
            P(("gx", "gy"), "gz"),
        ),
        check_vma=False,
    )
```

time: 415 us -> 153 us (0.37)
  waiting for transfers between devices: 264 us -> 51.7 us
  blocking collectives: 54.6 us -> 0 us
  starting transfers between devices: 0.32 us -> 34.2 us
  local copies, waits for them, and re-layouts: 25 us -> 2 us
  matrix products: 54.7 us -> 34.2 us
  Pallas kernels: 0 us -> 17.9 us
  between operations: 14.2 us -> 1.21 us
  other arithmetic: 1.45 us -> 11.2 us
    all_gather x3 -> x0, waiting for transfers between devices: 155 us -> none  [the longest x1 120 us: body(): lax.all_gather(down_weight, 'gx', axis=0, tiled=True)]
    reduce_scatter x4 -> x0, waiting for transfers between devices: 89.7 us -> none  [the longest x1 27.3 us: body(): lax.psum_scatter(up_part.astype(jnp.bfloat16), 'gz', scatter_dimension=0,...]
    ppermute x0 -> x34, waiting for transfers between devices: none -> 51.7 us  [the longest x16 27.5 us: shift(): return lax.ppermute(x, axis, [(i, (i + step) % n) for i in range(n)])]
    ppermute x0 -> x34, starting transfers between devices: none -> 34.2 us  [the longest x16 23.9 us: shift(): return lax.ppermute(x, axis, [(i, (i + step) % n) for i in range(n)])]
    all_gather x3 -> x0, blocking collectives: 27.9 us -> none  [the longest x1 9.43 us: body(): hidden_all = lax.all_gather(hidden_own, 'gz', axis=0, tiled=True)]
    all_to_all x1 -> x0, blocking collectives: 26.7 us -> none  [body(): lax.all_to_all(hidden_all, 'gx', split_axis=0, concat_axis=1, tiled=True)]
    dot_general x6, matrix products: 39.1 us -> 14.6 us  [dot(): return jnp.dot(left, right, preferred_element_type=F32)]
    unnamed x14 -> x36, local copies, waits for them, and re-layouts: 23.8 us -> 1.65 us
  transfers between devices with their start and end apart: 8 -> 34, of which waited for: 8 -> 12; matrix products, arithmetic and copies ran while one was open for 19% -> 26% of each run, Pallas kernels for 0% -> 12%
where the time goes in v1:
time: 153 us
  waiting for transfers between devices  51.7 us (34%)
  matrix products  34.2 us (22%)
  starting transfers between devices  34.2 us (22%)
  Pallas kernels  17.9 us (12%)
  other arithmetic  11.2 us (7%)
  local copies, waits for them, and re-layouts  2 us (1%)
    ppermute x16, waiting for transfers between devices, shift(): return lax.ppermute(x, axis, [(i, (i + step) % n) for i in range(n)])  27.5 us
    ppermute x6, waiting for transfers between devices, shift_chip(): lax.ppermute(x, 'gz', [(i, (i // CORES + step) % chips * CORES + i % CORE...  24.2 us
    ppermute x16, starting transfers between devices, shift(): return lax.ppermute(x, axis, [(i, (i + step) % n) for i in range(n)])  23.9 us
    dot_general x6, matrix products, contract_cols(): lax.dot_general(left, right, (((1,), (1,)), ((), ())), preferred_element_...  19.6 us
    pallas_call x3, Pallas kernels, weight_grad(): pl.pallas_call(weight_grad_kernel, out_shape=jax.ShapeDtypeStruct((height...  17.9 us
    dot_general x6, matrix products, dot(): return jnp.dot(left, right, preferred_element_type=F32)  14.6 us
    ppermute x6, starting transfers between devices, shift_chip(): lax.ppermute(x, 'gz', [(i, (i // CORES + step) % chips * CORES + i % CORE...  7.26 us
    concatenate x2, other arithmetic, own_half_first(): jnp.concatenate([x, x], axis=0)  3.34 us
  transfers between devices with their start and end apart: 34, of which 12 were waited for; matrix products, arithmetic and copies ran while one was open for 26% of the time, Pallas kernels for 12%

profile of v1, /device:TPU:0, one launch (start us, length us, event | category | flops | bytes accessed | tf_op | source)
XLA Modules:
  0.0 152.5 jit_solution(3437733121231492400)
XLA Ops:
  0.7 2.2 %fusion.9 = bf16[128,2048]{1,0:T(8,128)(2,1)} fusion(s32[]{:T(128)S(6)} %select_n.36, bf16[128,2048]{1,0:T(8,128)(2,1)} %param.5), kind=kLoop, calls=%fused_computation.28 | loop fusion | flops 1048576 | bytes 1048580 | tf_op jit(solution)/shard_map/concatenate | solution.py:125
  2.9 4.5 %convolution_convert_fusion.6 = bf16[128,1792]{1,0:T(8,128)(2,1)S(1)} fusion(bf16[128,2048]{1,0:T(8,128)(2,1)} %fusion.9, bf16[2048,1792]{1,0:T(8,128)(2,1)} %param.7), kind=kOutput, calls=%fused_computation.16 | convolution fusion | flops 939753472 | bytes 8323072 | tf_op jit(solution)/shard_map/dot_general | solution.py:14
  8.0 2.7 %convolution_convert_fusion.7 = bf16[128,1792]{1,0:T(8,128)(2,1)S(1)} fusion(bf16[128,2048]{1,0:T(8,128)(2,1)} %fusion.9, bf16[2048,1792]{1,0:T(8,128)(2,1)S(1)} %bitcast.21), kind=kOutput, calls=%fused_computation.17 | convolution fusion | flops 939753472 | bytes 8323072 | tf_op jit(solution)/shard_map/dot_general | solution.py:14
  10.8 1.1 fusion.8
  11.9 3.6 %convolution_convert_fusion.1 = bf16[128,1792]{1,0:T(8,128)(2,1)S(1)} fusion(bf16[128,2048]{1,0:T(8,128)(2,1)} %fusion.8, bf16[1792,2048]{1,0:T(8,128)(2,1)S(1)} %bitcast.25), kind=kOutput, calls=%fused_computation.8 | convolution fusion | flops 939753472 | bytes 8323072 | tf_op jit(solution)/shard_map/dot_general | solution.py:18
  16.1 0.8 fusion.31
  16.9 2.7 %collective-permute-start.3 = (bf16[64,1792]{1,0:T(8,128)(2,1)}, bf16[64,1792]{1,0:T(8,128)(2,1)}, u32[]{:S(2)}, u32[]{:S(2)}) collective-permute-start(bf16[64,1792]{1,0:T(8,128)(2,1)} %fusion.31), channel_id=1, source_target_pairs={{0,2},{1,3},{2,0},{3,1},{4,6},{5,7},{6,4},{7,5},{8,10},{9,11},{10,... | collective-permute-start | bytes 688136 | tf_op jit(solution)/shard_map/ppermute | solution.py:71
  19.5 0.8 fusion.30
  21.1 2.0 %collective-permute-start.19 = (bf16[64,1792]{1,0:T(8,128)(2,1)}, bf16[64,1792]{1,0:T(8,128)(2,1)}, u32[]{:S(2)}, u32[]{:S(2)}) collective-permute-start(bf16[64,1792]{1,0:T(8,128)(2,1)} %fusion.34), channel_id=1, source_target_pairs={{0,2},{1,3},{2,0},{3,1},{4,6},{5,7},{6,4},{7,5},{8,10},{9,11},{10,... | collective-permute-start | bytes 688136 | tf_op jit(solution)/shard_map/ppermute | solution.py:71
  23.1 1.5 collective-permute-start.22
  25.1 1.2 collective-permute-done.3
  26.3 4.9 %collective-permute-done.1 = bf16[64,1792]{1,0:T(8,128)(2,1)} collective-permute-done((bf16[64,1792]{1,0:T(8,128)(2,1)}, bf16[64,1792]{1,0:T(8,128)(2,1)}, u32[]{:S(2)}, u32[]{:S(2)}) %collective-permute-start.1) | collective-permute-done | bytes 229408 | tf_op jit(solution)/shard_map/ppermute | solution.py:71
  31.2 4.7 %collective-permute-done.19 = bf16[64,1792]{1,0:T(8,128)(2,1)} collective-permute-done((bf16[64,1792]{1,0:T(8,128)(2,1)}, bf16[64,1792]{1,0:T(8,128)(2,1)}, u32[]{:S(2)}, u32[]{:S(2)}) %collective-permute-start.19) | collective-permute-done | bytes 229408 | tf_op jit(solution)/shard_map/ppermute | solution.py:71
  35.9 2.0 %multiply_convert_fusion.3 = (bf16[64,1792]{1,0:T(8,128)(2,1)S(1)}, bf16[64,1792]{1,0:T(8,128)(2,1)S(1)}, bf16[64,1792]{1,0:T(8,128)(2,1)S(1)}) fusion(bf16[64,1792]{1,0:T(8,128)(2,1)} %collective-permute-done.3, bf16[64,1792]{1,0:T(8,128)(2,1)S(1)} %collective-permute-done.2, bf16[64,1792]{1,0:T(8,128)(2,1)} %collective-permute-done.19, ...), kind=kLoop, calls=%fused_computation.54 | loop fusion | flops 3555328 | bytes 2752512 | tf_op jit(solution)/shard_map/convert_element_type | solution.py:141
  38.5 6.0 %convolution_convert_fusion = bf16[128,1792]{1,0:T(8,128)(2,1)S(1)} fusion(bf16[128,2048]{1,0:T(8,128)(2,1)} %collective-permute-done.22, bf16[1792,2048]{1,0:T(8,128)(2,1)} %param.8), kind=kOutput, calls=%fused_computation.7 | convolution fusion | flops 939753472 | bytes 8323072 | tf_op jit(solution)/shard_map/dot_general | solution.py:18
  44.6 3.5 %collective-permute-done.5 = bf16[128,2048]{1,0:T(8,128)(2,1)} collective-permute-done((bf16[128,2048]{1,0:T(8,128)(2,1)}, bf16[128,2048]{1,0:T(8,128)(2,1)}, u32[]{:S(2)}, u32[]{:S(2)}) %collective-permute-start.5) | collective-permute-done | bytes 524320 | tf_op jit(solution)/shard_map/ppermute | solution.py:60
  48.1 2.2 %convolution_convert_fusion.3 = bf16[128,1792]{1,0:T(8,128)(2,1)S(1)} fusion(bf16[128,2048]{1,0:T(8,128)(2,1)} %collective-permute-done.5, bf16[2048,1792]{1,0:T(8,128)(2,1)S(1)} %bitcast.19), kind=kOutput, calls=%fused_computation.10 | convolution fusion | flops 939753472 | bytes 8323072 | tf_op jit(solution)/shard_map/dot_general | solution.py:14
  50.4 2.2 %convolution_convert_fusion.4 = bf16[128,1792]{1,0:T(8,128)(2,1)S(1)} fusion(bf16[128,2048]{1,0:T(8,128)(2,1)} %collective-permute-done.5, bf16[2048,1792]{1,0:T(8,128)(2,1)S(1)} %bitcast.23), kind=kOutput, calls=%fused_computation.11 | convolution fusion | flops 939753472 | bytes 8323072 | tf_op jit(solution)/shard_map/dot_general | solution.py:14
  53.2 1.3 pad_maximum_fusion.1.right_ref
  55.1 1.7 %collective-permute-start.9 = (bf16[64,1792]{1,0:T(8,128)(2,1)S(1)}, bf16[64,1792]{1,0:T(8,128)(2,1)S(1)}, u32[]{:S(2)}, u32[]{:S(2)}) collective-permute-start(bf16[64,1792]{1,0:T(8,128)(2,1)S(1)} %fusion.33), channel_id=1, source_target_pairs={{0,2},{1,3},{2,0},{3,1},{4,6},{5,7},{6,4},{7,5},{8,10},{9,11},{10,... | collective-permute-start | bytes 688136 | tf_op jit(solution)/shard_map/ppermute | solution.py:71
  57.3 1.3 pad_maximum_fusion.left_ref
  58.6 4.5 %collective-permute-done.24 = bf16[64,1792]{1,0:T(8,128)(2,1)S(1)} collective-permute-done((bf16[64,1792]{1,0:T(8,128)(2,1)S(1)}, bf16[64,1792]{1,0:T(8,128)(2,1)S(1)}, u32[]{:S(2)}, u32[]{:S(2)}) %collective-permute-start.24) | collective-permute-done | bytes 229408 | tf_op jit(solution)/shard_map/ppermute | solution.py:71
  63.1 4.9 %collective-permute-done.9 = bf16[64,1792]{1,0:T(8,128)(2,1)S(1)} collective-permute-done((bf16[64,1792]{1,0:T(8,128)(2,1)S(1)}, bf16[64,1792]{1,0:T(8,128)(2,1)S(1)}, u32[]{:S(2)}, u32[]{:S(2)}) %collective-permute-start.9) | collective-permute-done | bytes 229408 | tf_op jit(solution)/shard_map/ppermute | solution.py:71
  68.0 4.0 %collective-permute-done.7 = bf16[64,1792]{1,0:T(8,128)(2,1)S(1)} collective-permute-done((bf16[64,1792]{1,0:T(8,128)(2,1)S(1)}, bf16[64,1792]{1,0:T(8,128)(2,1)S(1)}, u32[]{:S(2)}, u32[]{:S(2)}) %collective-permute-start.7) | collective-permute-done | bytes 229408 | tf_op jit(solution)/shard_map/ppermute | solution.py:71
  72.6 2.6 %fusion.19 = f32[128,2048]{1,0:T(8,128)S(1)} fusion(bf16[2048,1792]{1,0:T(8,128)(2,1)S(1)} %bitcast.19, bf16[64,1792]{1,0:T(8,128)(2,1)S(1)} %collective-permute-done.21, bf16[64,1792]{1,0:T(8,128)(2,1)S(1)} %get-tuple-element.10), kind=kOutput, calls=%fused_computation.38 | convolution fusion | flops 940441600 | bytes 8847360 | tf_op jit(solution)/shard_map/dot_general | solution.py:18
  75.9 1.9 %convolution_convert_fusion.2 = bf16[128,2048]{1,0:T(8,128)(2,1)} fusion(bf16[1792,2048]{1,0:T(8,128)(2,1)S(1)} %bitcast.27, bf16[64,1792]{1,0:T(8,128)(2,1)S(1)} %collective-permute-done.10, bf16[64,1792]{1,0:T(8,128)(2,1)S(1)} %get-tuple-element.14), kind=kOutput, calls=%fused_computation.9 | convolution fusion | flops 940703744 | bytes 8323072 | tf_op jit(solution)/shard_map/dot_general | solution.py:14
  77.8 1.5 collective-permute-start.11
  79.3 2.5 %fusion.26 = f32[128,2048]{1,0:T(8,128)S(1)} fusion(bf16[2048,1792]{1,0:T(8,128)(2,1)S(1)} %bitcast.19, bf16[64,1792]{1,0:T(8,128)(2,1)S(1)} %collective-permute-done.26, bf16[64,1792]{1,0:T(8,128)(2,1)S(1)} %get-tuple-element.13), kind=kOutput, calls=%fused_computation.45 | convolution fusion | flops 940441600 | bytes 8847360 | tf_op jit(solution)/shard_map/dot_general | solution.py:18
  81.8 2.5 %fusion.3 = bf16[128,2048]{1,0:T(8,128)(2,1)S(1)} fusion(f32[128,2048]{1,0:T(8,128)S(1)} %fusion.26, bf16[2048,1792]{1,0:T(8,128)(2,1)S(1)} %bitcast.23, bf16[64,1792]{1,0:T(8,128)(2,1)S(1)} %collective-permute-done.25, bf16[64,1792]{1,0:T(8,128)(2,1)S(1)} %get-tuple-element.12), kind=kOutput, calls=%fused_computation.5 | convolution fusion | flops 940965888 | bytes 9371648 | tf_op jit(solution)/shard_map/dot_general | solution.py:18
  85.0 6.1 %shard_map.92 = bf16[2048,1792]{1,0:T(8,128)(2,1)} custom-call(bf16[256,2048]{1,0:T(8,128)(2,1)S(1)} %pad_maximum_fusion.left_ref, bf16[256,1792]{1,0:T(8,128)(2,1)S(1)} %pad_maximum_fusion.2.right_ref), custom_call_target="tpu_custom_call" | custom-call | flops 1879048192 | bytes 9306112 | tf_op jit(solution)/shard_map/pallas_call | solution.py:40
  91.1 6.1 %shard_map.93 = bf16[2048,1792]{1,0:T(8,128)(2,1)} custom-call(bf16[256,2048]{1,0:T(8,128)(2,1)S(1)} %pad_maximum_fusion.left_ref, bf16[256,1792]{1,0:T(8,128)(2,1)S(1)} %pad_maximum_fusion.3.right_ref), custom_call_target="tpu_custom_call" | custom-call | flops 1879048192 | bytes 9306112 | tf_op jit(solution)/shard_map/pallas_call | solution.py:40
  97.2 5.8 %shard_map.94 = bf16[1792,2048]{1,0:T(8,128)(2,1)} custom-call(bf16[256,1792]{1,0:T(8,128)(2,1)S(1)} %pad_maximum_fusion.4.left_ref, bf16[256,2048]{1,0:T(8,128)(2,1)S(1)} %pad_maximum_fusion.1.right_ref), custom_call_target="tpu_custom_call" | custom-call | flops 1879048192 | bytes 9306112 | tf_op jit(solution)/shard_map/pallas_call | solution.py:40
  103.0 1.1 fusion.7
  104.2 1.6 %collective-permute-start.12 = (bf16[32,2048]{1,0:T(8,128)(2,1)S(1)}, bf16[32,2048]{1,0:T(8,128)(2,1)S(1)}, u32[]{:S(2)}, u32[]{:S(2)}) collective-permute-start(bf16[32,2048]{1,0:T(8,128)(2,1)S(1)} %get-tuple-element.18), channel_id=1, source_target_pairs={{0,4},{4,8},{8,12},{12,0},{1,5},{5,9},{9,13},{13,1},{2,6},{6,10},{... | collective-permute-start | bytes 393224 | tf_op jit(solution)/shard_map/ppermute | solution.py:60
  105.8 2.2 %collective-permute-start.14 = (bf16[32,2048]{1,0:T(8,128)(2,1)S(1)}, bf16[32,2048]{1,0:T(8,128)(2,1)S(1)}, u32[]{:S(2)}, u32[]{:S(2)}) collective-permute-start(bf16[32,2048]{1,0:T(8,128)(2,1)S(1)} %get-tuple-element.19), channel_id=1, source_target_pairs={{0,12},{4,0},{8,4},{12,8},{1,13},{5,1},{9,5},{13,9},{2,14},{6,2},{... | collective-permute-start | bytes 393224 | tf_op jit(solution)/shard_map/ppermute | solution.py:60
  108.0 0.8 collective-permute-start.13
  108.8 2.5 %fusion.4 = bf16[128,2048]{1,0:T(8,128)(2,1)S(1)} fusion(f32[128,2048]{1,0:T(8,128)S(1)} %fusion.19, bf16[2048,1792]{1,0:T(8,128)(2,1)S(1)} %bitcast.23, bf16[128,2048]{1,0:T(8,128)(2,1)S(1)} %collective-permute-done.27, bf16[64,1792]{1,0:T(8,128)(2,1)S(1)} %collective-permute-done.20, bf16[64,1792]{1,0:T(8,128)(2,1)S(1)} %get-tuple-element.9), kind=kOutput, calls=%fused_computation.6 | convolution fusion | flops 942014464 | bytes 9895936 | tf_op jit(solution)/shard_map/dot_general | solution.py:18
  111.4 1.6 %collective-permute-start.28 = (bf16[32,2048]{1,0:T(8,128)(2,1)S(1)}, bf16[32,2048]{1,0:T(8,128)(2,1)S(1)}, u32[]{:S(2)}, u32[]{:S(2)}) collective-permute-start(bf16[32,2048]{1,0:T(8,128)(2,1)S(1)} %get-tuple-element.15), channel_id=1, source_target_pairs={{0,4},{4,8},{8,12},{12,0},{1,5},{5,9},{9,13},{13,1},{2,6},{6,10},{... | collective-permute-start | bytes 393224 | tf_op jit(solution)/shard_map/ppermute | solution.py:60
  113.0 2.2 %collective-permute-start.30 = (bf16[32,2048]{1,0:T(8,128)(2,1)S(1)}, bf16[32,2048]{1,0:T(8,128)(2,1)S(1)}, u32[]{:S(2)}, u32[]{:S(2)}) collective-permute-start(bf16[32,2048]{1,0:T(8,128)(2,1)S(1)} %get-tuple-element.16), channel_id=1, source_target_pairs={{0,12},{4,0},{8,4},{12,8},{1,13},{5,1},{9,5},{13,9},{2,14},{6,2},{... | collective-permute-start | bytes 393224 | tf_op jit(solution)/shard_map/ppermute | solution.py:60
  115.3 2.8 %collective-permute-start.29 = (bf16[32,2048]{1,0:T(8,128)(2,1)S(1)}, bf16[32,2048]{1,0:T(8,128)(2,1)S(1)}, u32[]{:S(2)}, u32[]{:S(2)}) collective-permute-start(bf16[32,2048]{1,0:T(8,128)(2,1)S(1)} %get-tuple-element.17), channel_id=1, source_target_pairs={{0,8},{4,12},{8,0},{12,4},{1,9},{5,13},{9,1},{13,5},{2,10},{6,14},... | collective-permute-start | bytes 393224 | tf_op jit(solution)/shard_map/ppermute | solution.py:60
  118.1 5.7 %collective-permute-done.13 = bf16[32,2048]{1,0:T(8,128)(2,1)S(1)} collective-permute-done((bf16[32,2048]{1,0:T(8,128)(2,1)S(1)}, bf16[32,2048]{1,0:T(8,128)(2,1)S(1)}, u32[]{:S(2)}, u32[]{:S(2)}) %collective-permute-start.13) | collective-permute-done | bytes 131104 | tf_op jit(solution)/shard_map/ppermute | solution.py:60
  124.0 4.4 %collective-permute-start.15 = (bf16[32,2048]{1,0:T(8,128)(2,1)S(1)}, bf16[32,2048]{1,0:T(8,128)(2,1)S(1)}, u32[]{:S(2)}, u32[]{:S(2)}) collective-permute-start(bf16[32,2048]{1,0:T(8,128)(2,1)S(1)} %get-tuple-element.8), channel_id=1, source_target_pairs={{0,4},{4,8},{8,12},{12,0},{1,5},{5,9},{9,13},{13,1},{2,6},{6,10},{... | collective-permute-start | bytes 393224 | tf_op jit(solution)/shard_map/ppermute | solution.py:60
  128.4 8.5 %collective-permute-done.29 = bf16[32,2048]{1,0:T(8,128)(2,1)S(1)} collective-permute-done((bf16[32,2048]{1,0:T(8,128)(2,1)S(1)}, bf16[32,2048]{1,0:T(8,128)(2,1)S(1)}, u32[]{:S(2)}, u32[]{:S(2)}) %collective-permute-start.29) | collective-permute-done | bytes 131104 | tf_op jit(solution)/shard_map/ppermute | solution.py:60
  137.1 2.6 %collective-permute-start.31 = (bf16[32,2048]{1,0:T(8,128)(2,1)S(1)}, bf16[32,2048]{1,0:T(8,128)(2,1)S(1)}, u32[]{:S(2)}, u32[]{:S(2)}) collective-permute-start(bf16[32,2048]{1,0:T(8,128)(2,1)S(1)} %get-tuple-element.6), channel_id=1, source_target_pairs={{0,4},{4,8},{8,12},{12,0},{1,5},{5,9},{9,13},{13,1},{2,6},{6,10},{... | collective-permute-start | bytes 393224 | tf_op jit(solution)/shard_map/ppermute | solution.py:60
  139.7 1.3 collective-permute-start.33
  141.0 3.9 %collective-permute-done.31 = bf16[32,2048]{1,0:T(8,128)(2,1)S(1)} collective-permute-done((bf16[32,2048]{1,0:T(8,128)(2,1)S(1)}, bf16[32,2048]{1,0:T(8,128)(2,1)S(1)}, u32[]{:S(2)}, u32[]{:S(2)}) %collective-permute-start.31) | collective-permute-done | bytes 131104 | tf_op jit(solution)/shard_map/ppermute | solution.py:60
  145.3 5.6 %collective-permute-done.32 = bf16[32,2048]{1,0:T(8,128)(2,1)S(1)} collective-permute-done((bf16[32,2048]{1,0:T(8,128)(2,1)S(1)}, bf16[32,2048]{1,0:T(8,128)(2,1)S(1)}, u32[]{:S(2)}, u32[]{:S(2)}) %collective-permute-start.32) | collective-permute-done | bytes 131104 | tf_op jit(solution)/shard_map/ppermute | solution.py:60
  151.7 0.8 copy-done.5
  (109 shorter events, 8.5 us)
Async XLA Ops:
  0.6 7.4 %slice-start.2 = ((s8[7340032]{0:T(1024)(128)(4,1)}), s8[4194304]{0:T(1024)(128)(4,1)S(1)}, s32[]{:S(2)}) async-start(s8[7340032]{0:T(1024)(128)(4,1)} %bitcast.20), calls=%async_computation.2 | async-start | bytes 8388608
  2.9 5.1 %slice-start.3 = ((s8[7340032]{0:T(1024)(128)(4,1)}), s8[3145728]{0:T(1024)(128)(4,1)S(1)}, s32[]{:S(2)}) async-start(s8[7340032]{0:T(1024)(128)(4,1)} %bitcast.20), calls=%async_computation.3 | async-start | bytes 6291456
  7.4 13.7 %copy-start.1 = (bf16[128,1792]{1,0:T(8,128)(2,1)}, bf16[128,1792]{1,0:T(8,128)(2,1)S(1)}, u32[]{:S(2)}) copy-start(bf16[128,1792]{1,0:T(8,128)(2,1)S(1)} %convolution_convert_fusion.6) | copy-start | bytes 1376260
  7.4 4.5 %slice-start.6 = ((s8[7340032]{0:T(1024)(128)(4,1)}), s8[4194304]{0:T(1024)(128)(4,1)S(1)}, s32[]{:S(2)}) async-start(s8[7340032]{0:T(1024)(128)(4,1)} %bitcast.24), calls=%async_computation.6 | async-start | bytes 8388608
  7.5 4.4 %slice-start.7 = ((s8[7340032]{0:T(1024)(128)(4,1)}), s8[3145728]{0:T(1024)(128)(4,1)S(1)}, s32[]{:S(2)}) async-start(s8[7340032]{0:T(1024)(128)(4,1)} %bitcast.24), calls=%async_computation.7 | async-start | bytes 6291456
  7.5 8.6 %collective-permute-start.2 = (bf16[64,1792]{1,0:T(8,128)(2,1)S(1)}, bf16[64,1792]{1,0:T(8,128)(2,1)S(1)}, u32[]{:S(2)}, u32[]{:S(2)}) collective-permute-start(bf16[64,1792]{1,0:T(8,128)(2,1)S(1)} %slice.51), channel_id=1, source_target_pairs={{0,1},{1,0},{2,3},{3,2},{4,5},{5,4},{6,7},{7,6},{8,9},{9,8},{10,11... | collective-permute-start | bytes 688136 | tf_op jit(solution)/shard_map/ppermute | solution.py:65
  10.7 12.4 %copy-start.2 = (bf16[128,1792]{1,0:T(8,128)(2,1)}, bf16[128,1792]{1,0:T(8,128)(2,1)S(1)}, u32[]{:S(2)}) copy-start(bf16[128,1792]{1,0:T(8,128)(2,1)S(1)} %convolution_convert_fusion.7) | copy-start | bytes 1376260
  10.7 8.8 %collective-permute-start = (bf16[64,1792]{1,0:T(8,128)(2,1)S(1)}, bf16[64,1792]{1,0:T(8,128)(2,1)S(1)}, u32[]{:S(2)}, u32[]{:S(2)}) collective-permute-start(bf16[64,1792]{1,0:T(8,128)(2,1)S(1)} %slice.49), channel_id=1, source_target_pairs={{0,1},{1,0},{2,3},{3,2},{4,5},{5,4},{6,7},{7,6},{8,9},{9,8},{10,11... | collective-permute-start | bytes 688136 | tf_op jit(solution)/shard_map/ppermute | solution.py:65
  15.5 4.8 %copy-start = (bf16[128,1792]{1,0:T(8,128)(2,1)}, bf16[128,1792]{1,0:T(8,128)(2,1)S(1)}, u32[]{:S(2)}) copy-start(bf16[128,1792]{1,0:T(8,128)(2,1)S(1)} %convolution_convert_fusion.1) | copy-start | bytes 1376260
  15.5 32.6 %slice-start = ((s8[7340032]{0:T(1024)(128)(4,1)}), s8[3145728]{0:T(1024)(128)(4,1)S(1)}, s32[]{:S(2)}) async-start(s8[7340032]{0:T(1024)(128)(4,1)} %bitcast.18), calls=%async_computation | async-start | bytes 6291456
  15.6 4.7 %collective-permute-start.18 = (bf16[64,1792]{1,0:T(8,128)(2,1)S(1)}, bf16[64,1792]{1,0:T(8,128)(2,1)S(1)}, u32[]{:S(2)}, u32[]{:S(2)}) collective-permute-start(bf16[64,1792]{1,0:T(8,128)(2,1)S(1)} %slice.57), channel_id=1, source_target_pairs={{0,1},{1,0},{2,3},{3,2},{4,5},{5,4},{6,7},{7,6},{8,9},{9,8},{10,11... | collective-permute-start | bytes 688136 | tf_op jit(solution)/shard_map/ppermute | solution.py:65
  16.9 9.4 %collective-permute-start.3 = (bf16[64,1792]{1,0:T(8,128)(2,1)}, bf16[64,1792]{1,0:T(8,128)(2,1)}, u32[]{:S(2)}, u32[]{:S(2)}) collective-permute-start(bf16[64,1792]{1,0:T(8,128)(2,1)} %fusion.31), channel_id=1, source_target_pairs={{0,2},{1,3},{2,0},{3,1},{4,6},{5,7},{6,4},{7,5},{8,10},{9,11},{10,... | collective-permute-start | bytes 688136 | tf_op jit(solution)/shard_map/ppermute | solution.py:71
  19.5 5.1 %copy-start.3 = (bf16[64,1792]{1,0:T(8,128)(2,1)}, bf16[64,1792]{1,0:T(8,128)(2,1)S(1)}, u32[]{:S(2)}) copy-start(bf16[64,1792]{1,0:T(8,128)(2,1)S(1)} %collective-permute-done) | copy-start | bytes 688132
  20.3 10.9 %collective-permute-start.1 = (bf16[64,1792]{1,0:T(8,128)(2,1)}, bf16[64,1792]{1,0:T(8,128)(2,1)}, u32[]{:S(2)}, u32[]{:S(2)}) collective-permute-start(bf16[64,1792]{1,0:T(8,128)(2,1)} %fusion.30), channel_id=1, source_target_pairs={{0,2},{1,3},{2,0},{3,1},{4,6},{5,7},{6,4},{7,5},{8,10},{9,11},{10,... | collective-permute-start | bytes 688136 | tf_op jit(solution)/shard_map/ppermute | solution.py:71
  20.3 4.3 %copy-start.4 = (bf16[64,1792]{1,0:T(8,128)(2,1)}, bf16[64,1792]{1,0:T(8,128)(2,1)S(1)}, u32[]{:S(2)}) copy-start(bf16[64,1792]{1,0:T(8,128)(2,1)S(1)} %collective-permute-done.18) | copy-start | bytes 688132
  21.1 14.8 %collective-permute-start.19 = (bf16[64,1792]{1,0:T(8,128)(2,1)}, bf16[64,1792]{1,0:T(8,128)(2,1)}, u32[]{:S(2)}, u32[]{:S(2)}) collective-permute-start(bf16[64,1792]{1,0:T(8,128)(2,1)} %fusion.34), channel_id=1, source_target_pairs={{0,2},{1,3},{2,0},{3,1},{4,6},{5,7},{6,4},{7,5},{8,10},{9,11},{10,... | collective-permute-start | bytes 688136 | tf_op jit(solution)/shard_map/ppermute | solution.py:71
  23.1 15.4 %collective-permute-start.22 = (bf16[128,2048]{1,0:T(8,128)(2,1)}, bf16[128,2048]{1,0:T(8,128)(2,1)}, u32[]{:S(2)}, u32[]{:S(2)}) collective-permute-start(bf16[128,2048]{1,0:T(8,128)(2,1)} %fusion.8), channel_id=1, source_target_pairs={{0,16},{16,0},{1,17},{17,1},{2,18},{18,2},{3,19},{19,3},{4,20},{20... | collective-permute-start | bytes 1572872 | tf_op jit(solution)/shard_map/ppermute | solution.py:60
  24.6 23.5 %collective-permute-start.5 = (bf16[128,2048]{1,0:T(8,128)(2,1)}, bf16[128,2048]{1,0:T(8,128)(2,1)}, u32[]{:S(2)}, u32[]{:S(2)}) collective-permute-start(bf16[128,2048]{1,0:T(8,128)(2,1)} %fusion.9), channel_id=1, source_target_pairs={{0,16},{16,0},{1,17},{17,1},{2,18},{18,2},{3,19},{19,3},{4,20},{20... | collective-permute-start | bytes 1572872 | tf_op jit(solution)/shard_map/ppermute | solution.py:60
  37.9 47.0 %collective-permute-start.20 = (bf16[64,1792]{1,0:T(8,128)(2,1)S(1)}, bf16[64,1792]{1,0:T(8,128)(2,1)S(1)}, u32[]{:S(2)}, u32[]{:S(2)}) collective-permute-start(bf16[64,1792]{1,0:T(8,128)(2,1)S(1)} %get-tuple-element.9), channel_id=1, source_target_pairs={{0,1},{1,0},{2,3},{3,2},{4,5},{5,4},{6,7},{7,6},{8,9},{9,8},{10,11... | collective-permute-start | bytes 688136 | tf_op jit(solution)/shard_map/ppermute | solution.py:65
  38.0 10.1 %slice-start.1 = ((s8[7340032]{0:T(1024)(128)(4,1)}), s8[4194304]{0:T(1024)(128)(4,1)S(1)}, s32[]{:S(2)}) async-start(s8[7340032]{0:T(1024)(128)(4,1)} %bitcast.18), calls=%async_computation.1 | async-start | bytes 8388608
  38.0 34.6 %collective-permute-start.21 = (bf16[64,1792]{1,0:T(8,128)(2,1)S(1)}, bf16[64,1792]{1,0:T(8,128)(2,1)S(1)}, u32[]{:S(2)}, u32[]{:S(2)}) collective-permute-start(bf16[64,1792]{1,0:T(8,128)(2,1)S(1)} %get-tuple-element.10), channel_id=1, source_target_pairs={{0,1},{1,0},{2,3},{3,2},{4,5},{5,4},{6,7},{7,6},{8,9},{9,8},{10,11... | collective-permute-start | bytes 688136 | tf_op jit(solution)/shard_map/ppermute | solution.py:65
  44.5 5.9 %slice-start.4 = ((s8[7340032]{0:T(1024)(128)(4,1)}), s8[4194304]{0:T(1024)(128)(4,1)S(1)}, s32[]{:S(2)}) async-start(s8[7340032]{0:T(1024)(128)(4,1)} %bitcast.22), calls=%async_computation.4 | async-start | bytes 8388608
  44.6 5.8 %slice-start.5 = ((s8[7340032]{0:T(1024)(128)(4,1)}), s8[3145728]{0:T(1024)(128)(4,1)S(1)}, s32[]{:S(2)}) async-start(s8[7340032]{0:T(1024)(128)(4,1)} %bitcast.22), calls=%async_computation.5 | async-start | bytes 6291456
  44.6 9.9 %collective-permute-start.23 = (bf16[64,1792]{1,0:T(8,128)(2,1)S(1)}, bf16[64,1792]{1,0:T(8,128)(2,1)S(1)}, u32[]{:S(2)}, u32[]{:S(2)}) collective-permute-start(bf16[64,1792]{1,0:T(8,128)(2,1)S(1)} %slice.59), channel_id=1, source_target_pairs={{0,1},{1,0},{2,3},{3,2},{4,5},{5,4},{6,7},{7,6},{8,9},{9,8},{10,11... | collective-permute-start | bytes 688136 | tf_op jit(solution)/shard_map/ppermute | solution.py:65
  50.3 4.7 %collective-permute-start.8 = (bf16[64,1792]{1,0:T(8,128)(2,1)S(1)}, bf16[64,1792]{1,0:T(8,128)(2,1)S(1)}, u32[]{:S(2)}, u32[]{:S(2)}) collective-permute-start(bf16[64,1792]{1,0:T(8,128)(2,1)S(1)} %slice.55), channel_id=1, source_target_pairs={{0,1},{1,0},{2,3},{3,2},{4,5},{5,4},{6,7},{7,6},{8,9},{9,8},{10,11... | collective-permute-start | bytes 688136 | tf_op jit(solution)/shard_map/ppermute | solution.py:65
  52.6 4.2 %collective-permute-start.6 = (bf16[64,1792]{1,0:T(8,128)(2,1)S(1)}, bf16[64,1792]{1,0:T(8,128)(2,1)S(1)}, u32[]{:S(2)}, u32[]{:S(2)}) collective-permute-start(bf16[64,1792]{1,0:T(8,128)(2,1)S(1)} %slice.53), channel_id=1, source_target_pairs={{0,1},{1,0},{2,3},{3,2},{4,5},{5,4},{6,7},{7,6},{8,9},{9,8},{10,11... | collective-permute-start | bytes 688136 | tf_op jit(solution)/shard_map/ppermute | solution.py:65
  54.6 8.5 %collective-permute-start.24 = (bf16[64,1792]{1,0:T(8,128)(2,1)S(1)}, bf16[64,1792]{1,0:T(8,128)(2,1)S(1)}, u32[]{:S(2)}, u32[]{:S(2)}) collective-permute-start(bf16[64,1792]{1,0:T(8,128)(2,1)S(1)} %fusion.35), channel_id=1, source_target_pairs={{0,2},{1,3},{2,0},{3,1},{4,6},{5,7},{6,4},{7,5},{8,10},{9,11},{10,... | collective-permute-start | bytes 688136 | tf_op jit(solution)/shard_map/ppermute | solution.py:71
  55.1 20.8 %slice-start.8 = ((s8[7340032]{0:T(1024)(128)(4,1)}), s8[4194304]{0:T(1024)(128)(4,1)S(1)}, s32[]{:S(2)}) async-start(s8[7340032]{0:T(1024)(128)(4,1)} %bitcast.26), calls=%async_computation.8 | async-start | bytes 8388608
  55.1 12.9 %collective-permute-start.9 = (bf16[64,1792]{1,0:T(8,128)(2,1)S(1)}, bf16[64,1792]{1,0:T(8,128)(2,1)S(1)}, u32[]{:S(2)}, u32[]{:S(2)}) collective-permute-start(bf16[64,1792]{1,0:T(8,128)(2,1)S(1)} %fusion.33), channel_id=1, source_target_pairs={{0,2},{1,3},{2,0},{3,1},{4,6},{5,7},{6,4},{7,5},{8,10},{9,11},{10,... | collective-permute-start | bytes 688136 | tf_op jit(solution)/shard_map/ppermute | solution.py:71
  56.9 15.1 %collective-permute-start.7 = (bf16[64,1792]{1,0:T(8,128)(2,1)S(1)}, bf16[64,1792]{1,0:T(8,128)(2,1)S(1)}, u32[]{:S(2)}, u32[]{:S(2)}) collective-permute-start(bf16[64,1792]{1,0:T(8,128)(2,1)S(1)} %fusion.32), channel_id=1, source_target_pairs={{0,2},{1,3},{2,0},{3,1},{4,6},{5,7},{6,4},{7,5},{8,10},{9,11},{10,... | collective-permute-start | bytes 688136 | tf_op jit(solution)/shard_map/ppermute | solution.py:71
  63.1 34.0 %collective-permute-start.4 = (bf16[64,1792]{1,0:T(8,128)(2,1)S(1)}, bf16[64,1792]{1,0:T(8,128)(2,1)S(1)}, u32[]{:S(2)}, u32[]{:S(2)}) collective-permute-start(bf16[64,1792]{1,0:T(8,128)(2,1)S(1)} %get-tuple-element.11), channel_id=1, source_target_pairs={{0,1},{1,0},{2,3},{3,2},{4,5},{5,4},{6,7},{7,6},{8,9},{9,8},{10,11... | collective-permute-start | bytes 688136 | tf_op jit(solution)/shard_map/ppermute | solution.py:65
  72.5 3.4 %collective-permute-start.10 = (bf16[64,1792]{1,0:T(8,128)(2,1)S(1)}, bf16[64,1792]{1,0:T(8,128)(2,1)S(1)}, u32[]{:S(2)}, u32[]{:S(2)}) collective-permute-start(bf16[64,1792]{1,0:T(8,128)(2,1)S(1)} %get-tuple-element.14), channel_id=1, source_target_pairs={{0,1},{1,0},{2,3},{3,2},{4,5},{5,4},{6,7},{7,6},{8,9},{9,8},{10,11... | collective-permute-start | bytes 688136 | tf_op jit(solution)/shard_map/ppermute | solution.py:65
  75.2 6.6 %collective-permute-start.25 = (bf16[64,1792]{1,0:T(8,128)(2,1)S(1)}, bf16[64,1792]{1,0:T(8,128)(2,1)S(1)}, u32[]{:S(2)}, u32[]{:S(2)}) collective-permute-start(bf16[64,1792]{1,0:T(8,128)(2,1)S(1)} %get-tuple-element.12), channel_id=1, source_target_pairs={{0,1},{1,0},{2,3},{3,2},{4,5},{5,4},{6,7},{7,6},{8,9},{9,8},{10,11... | collective-permute-start | bytes 688136 | tf_op jit(solution)/shard_map/ppermute | solution.py:65
  75.8 3.5 %collective-permute-start.26 = (bf16[64,1792]{1,0:T(8,128)(2,1)S(1)}, bf16[64,1792]{1,0:T(8,128)(2,1)S(1)}, u32[]{:S(2)}, u32[]{:S(2)}) collective-permute-start(bf16[64,1792]{1,0:T(8,128)(2,1)S(1)} %get-tuple-element.13), channel_id=1, source_target_pairs={{0,1},{1,0},{2,3},{3,2},{4,5},{5,4},{6,7},{7,6},{8,9},{9,8},{10,11... | collective-permute-start | bytes 688136 | tf_op jit(solution)/shard_map/ppermute | solution.py:65
  77.8 25.2 %collective-permute-start.11 = (bf16[128,2048]{1,0:T(8,128)(2,1)}, bf16[128,2048]{1,0:T(8,128)(2,1)S(1)}, u32[]{:S(2)}, u32[]{:S(2)}) collective-permute-start(bf16[128,2048]{1,0:T(8,128)(2,1)} %convolution_convert_fusion.2), channel_id=1, source_target_pairs={{0,16},{16,0},{1,17},{17,1},{2,18},{18,2},{3,19},{19,3},{4,20},{20... | collective-permute-start | bytes 1572872 | tf_op jit(solution)/shard_map/ppermute | solution.py:60
  84.3 24.6 %collective-permute-start.27 = (bf16[128,2048]{1,0:T(8,128)(2,1)S(1)}, bf16[128,2048]{1,0:T(8,128)(2,1)S(1)}, u32[]{:S(2)}, u32[]{:S(2)}) collective-permute-start(bf16[128,2048]{1,0:T(8,128)(2,1)S(1)} %fusion.3), channel_id=1, source_target_pairs={{0,16},{16,0},{1,17},{17,1},{2,18},{18,2},{3,19},{19,3},{4,20},{20... | collective-permute-start | bytes 1572872 | tf_op jit(solution)/shard_map/ppermute | solution.py:60
  104.2 11.1 %collective-permute-start.12 = (bf16[32,2048]{1,0:T(8,128)(2,1)S(1)}, bf16[32,2048]{1,0:T(8,128)(2,1)S(1)}, u32[]{:S(2)}, u32[]{:S(2)}) collective-permute-start(bf16[32,2048]{1,0:T(8,128)(2,1)S(1)} %get-tuple-element.18), channel_id=1, source_target_pairs={{0,4},{4,8},{8,12},{12,0},{1,5},{5,9},{9,13},{13,1},{2,6},{6,10},{... | collective-permute-start | bytes 393224 | tf_op jit(solution)/shard_map/ppermute | solution.py:60
  105.8 12.3 %collective-permute-start.14 = (bf16[32,2048]{1,0:T(8,128)(2,1)S(1)}, bf16[32,2048]{1,0:T(8,128)(2,1)S(1)}, u32[]{:S(2)}, u32[]{:S(2)}) collective-permute-start(bf16[32,2048]{1,0:T(8,128)(2,1)S(1)} %get-tuple-element.19), channel_id=1, source_target_pairs={{0,12},{4,0},{8,4},{12,8},{1,13},{5,1},{9,5},{13,9},{2,14},{6,2},{... | collective-permute-start | bytes 393224 | tf_op jit(solution)/shard_map/ppermute | solution.py:60
  108.0 15.7 %collective-permute-start.13 = (bf16[32,2048]{1,0:T(8,128)(2,1)S(1)}, bf16[32,2048]{1,0:T(8,128)(2,1)S(1)}, u32[]{:S(2)}, u32[]{:S(2)}) collective-permute-start(bf16[32,2048]{1,0:T(8,128)(2,1)S(1)} %get-tuple-element.20), channel_id=1, source_target_pairs={{0,8},{4,12},{8,0},{12,4},{1,9},{5,13},{9,1},{13,5},{2,10},{6,14},... | collective-permute-start | bytes 393224 | tf_op jit(solution)/shard_map/ppermute | solution.py:60
  111.4 17.0 %collective-permute-start.28 = (bf16[32,2048]{1,0:T(8,128)(2,1)S(1)}, bf16[32,2048]{1,0:T(8,128)(2,1)S(1)}, u32[]{:S(2)}, u32[]{:S(2)}) collective-permute-start(bf16[32,2048]{1,0:T(8,128)(2,1)S(1)} %get-tuple-element.15), channel_id=1, source_target_pairs={{0,4},{4,8},{8,12},{12,0},{1,5},{5,9},{9,13},{13,1},{2,6},{6,10},{... | collective-permute-start | bytes 393224 | tf_op jit(solution)/shard_map/ppermute | solution.py:60
  113.0 15.4 %collective-permute-start.30 = (bf16[32,2048]{1,0:T(8,128)(2,1)S(1)}, bf16[32,2048]{1,0:T(8,128)(2,1)S(1)}, u32[]{:S(2)}, u32[]{:S(2)}) collective-permute-start(bf16[32,2048]{1,0:T(8,128)(2,1)S(1)} %get-tuple-element.16), channel_id=1, source_target_pairs={{0,12},{4,0},{8,4},{12,8},{1,13},{5,1},{9,5},{13,9},{2,14},{6,2},{... | collective-permute-start | bytes 393224 | tf_op jit(solution)/shard_map/ppermute | solution.py:60
  115.3 21.6 %collective-permute-start.29 = (bf16[32,2048]{1,0:T(8,128)(2,1)S(1)}, bf16[32,2048]{1,0:T(8,128)(2,1)S(1)}, u32[]{:S(2)}, u32[]{:S(2)}) collective-permute-start(bf16[32,2048]{1,0:T(8,128)(2,1)S(1)} %get-tuple-element.17), channel_id=1, source_target_pairs={{0,8},{4,12},{8,0},{12,4},{1,9},{5,13},{9,1},{13,5},{2,10},{6,14},... | collective-permute-start | bytes 393224 | tf_op jit(solution)/shard_map/ppermute | solution.py:60
  123.9 21.4 %collective-permute-start.16 = (bf16[32,2048]{1,0:T(8,128)(2,1)S(1)}, bf16[32,2048]{1,0:T(8,128)(2,1)S(1)}, u32[]{:S(2)}, u32[]{:S(2)}) collective-permute-start(bf16[32,2048]{1,0:T(8,128)(2,1)S(1)} %get-tuple-element.8), channel_id=1, source_target_pairs={{0,8},{4,12},{8,0},{12,4},{1,9},{5,13},{9,1},{13,5},{2,10},{6,14},... | collective-permute-start | bytes 393224 | tf_op jit(solution)/shard_map/ppermute | solution.py:60
  124.0 15.7 %collective-permute-start.15 = (bf16[32,2048]{1,0:T(8,128)(2,1)S(1)}, bf16[32,2048]{1,0:T(8,128)(2,1)S(1)}, u32[]{:S(2)}, u32[]{:S(2)}) collective-permute-start(bf16[32,2048]{1,0:T(8,128)(2,1)S(1)} %get-tuple-element.8), channel_id=1, source_target_pairs={{0,4},{4,8},{8,12},{12,0},{1,5},{5,9},{9,13},{13,1},{2,6},{6,10},{... | collective-permute-start | bytes 393224 | tf_op jit(solution)/shard_map/ppermute | solution.py:60
  128.4 22.5 %collective-permute-start.17 = (bf16[32,2048]{1,0:T(8,128)(2,1)S(1)}, bf16[32,2048]{1,0:T(8,128)(2,1)S(1)}, u32[]{:S(2)}, u32[]{:S(2)}) collective-permute-start(bf16[32,2048]{1,0:T(8,128)(2,1)S(1)} %get-tuple-element.8), channel_id=1, source_target_pairs={{0,12},{4,0},{8,4},{12,8},{1,13},{5,1},{9,5},{13,9},{2,14},{6,2},{... | collective-permute-start | bytes 393224 | tf_op jit(solution)/shard_map/ppermute | solution.py:60
  137.0 13.9 %collective-permute-start.32 = (bf16[32,2048]{1,0:T(8,128)(2,1)S(1)}, bf16[32,2048]{1,0:T(8,128)(2,1)S(1)}, u32[]{:S(2)}, u32[]{:S(2)}) collective-permute-start(bf16[32,2048]{1,0:T(8,128)(2,1)S(1)} %get-tuple-element.6), channel_id=1, source_target_pairs={{0,8},{4,12},{8,0},{12,4},{1,9},{5,13},{9,1},{13,5},{2,10},{6,14},... | collective-permute-start | bytes 393224 | tf_op jit(solution)/shard_map/ppermute | solution.py:60
  137.1 7.8 %collective-permute-start.31 = (bf16[32,2048]{1,0:T(8,128)(2,1)S(1)}, bf16[32,2048]{1,0:T(8,128)(2,1)S(1)}, u32[]{:S(2)}, u32[]{:S(2)}) collective-permute-start(bf16[32,2048]{1,0:T(8,128)(2,1)S(1)} %get-tuple-element.6), channel_id=1, source_target_pairs={{0,4},{4,8},{8,12},{12,0},{1,5},{5,9},{9,13},{13,1},{2,6},{6,10},{... | collective-permute-start | bytes 393224 | tf_op jit(solution)/shard_map/ppermute | solution.py:60
  139.7 11.3 %collective-permute-start.33 = (bf16[32,2048]{1,0:T(8,128)(2,1)S(1)}, bf16[32,2048]{1,0:T(8,128)(2,1)S(1)}, u32[]{:S(2)}, u32[]{:S(2)}) collective-permute-start(bf16[32,2048]{1,0:T(8,128)(2,1)S(1)} %get-tuple-element.6), channel_id=1, source_target_pairs={{0,12},{4,0},{8,4},{12,8},{1,13},{5,1},{9,5},{13,9},{2,14},{6,2},{... | collective-permute-start | bytes 393224 | tf_op jit(solution)/shard_map/ppermute | solution.py:60
  (4 other events, 8.3 us)

commit v2 on v1

--- a/solution.py
+++ b/solution.py
@@ -73,21 +73,37 @@
     )
 
 
+def after(x, *earlier):
+    return lax.optimization_barrier((x,) + earlier)[0]
+
+
 def gather_gx(own):
     return [own] + [shift(own, "gx", k) for k in range(1, lax.axis_size("gx"))]
 
 
-def reduce_gz(part):
-    half = part.shape[0] // CORES
-    total = part[:half].astype(F32) + other_core(part[half:]).astype(F32)
+def halves(blocks, core):
+    half = blocks[0].shape[0] // CORES
+    return tuple(
+        jnp.concatenate(
+            [lax.dynamic_slice_in_dim(x, at * half, half, 0) for x in blocks], axis=0
+        )
+        for at in (core, 1 - core)
+    )
+
+
+def reduce_gz(multiply, mine, other):
+    sent = multiply(other).astype(BF16)
+    kept = multiply(after(mine, sent)).astype(BF16)
+    total = kept.astype(F32) + other_core(sent).astype(F32)
     sent = total.astype(BF16)
     for k in range(1, lax.axis_size("gz") // CORES):
         total = total + shift_chip(sent, k).astype(F32)
-    return total
-
-
-def join_cores(own):
-    return jnp.concatenate([own, other_core(own)], axis=0)
+    return total, kept
+
+
+def block_rows(mine, other, k, n):
+    half = mine.shape[0] // n
+    return jnp.concatenate([mine[k * half : (k + 1) * half], other[k * half : (k + 1) * half]], axis=0)
 
 
 def reduce_terms(terms):
@@ -118,39 +134,49 @@
 
 def body(tokens, gate_weight, up_weight, down_weight, out_grad):
     core = lax.rem(lax.axis_index("gz"), CORES)
-    rows = tokens.shape[0]
-
-    def own_half_first(x):
-        return lax.dynamic_slice_in_dim(
-            jnp.concatenate([x, x], axis=0), core * (rows // CORES), rows, 0
-        )
-
-    toks = gather_gx(own_half_first(tokens))
-    grads = gather_gx(own_half_first(out_grad))
-    hiddens, dgates, dups, acts = [], [], [], []
-    for tok in toks:
-        gate = reduce_gz(dot(tok, gate_weight).astype(BF16))
-        upward = reduce_gz(dot(tok, up_weight).astype(BF16))
-        sig = jax.nn.sigmoid(gate)
-        hiddens.append(join_cores((gate * sig * upward).astype(BF16)))
-        acts.append((gate, upward, sig))
-    output = reduce_terms([dot(h, down_weight).astype(BF16) for h in hiddens])
-    for grad, (gate, upward, sig) in zip(grads, acts):
-        dhidden = reduce_gz(contract_cols(grad, down_weight).astype(BF16))
-        dgates.append(
-            join_cores((dhidden * upward * sig * (1.0 + gate * (1.0 - sig))).astype(BF16))
-        )
-        dups.append(join_cores((dhidden * gate * sig).astype(BF16)))
-    input_grad = reduce_terms(
-        [
-            (contract_cols(dg, gate_weight) + contract_cols(du, up_weight)).astype(BF16)
-            for dg, du in zip(dgates, dups)
-        ]
-    )
-    all_tokens = jnp.concatenate(toks, axis=0)
-    down_grad = weight_grad(jnp.concatenate(hiddens, axis=0), jnp.concatenate(grads, axis=0))
-    gate_grad = weight_grad(all_tokens, jnp.concatenate(dgates, axis=0))
-    up_grad = weight_grad(all_tokens, jnp.concatenate(dups, axis=0))
+    n = lax.axis_size("gx")
+
+    toks = gather_gx(tokens)
+    grads = gather_gx(after(out_grad, *toks[1:]))
+    tok_mine, tok_other = halves(toks, core)
+    gate, gate_part = reduce_gz(lambda x: dot(x, gate_weight), tok_mine, tok_other)
+    tok_next = after(tok_other, gate_part)
+    upward, up_part = reduce_gz(lambda x: dot(x, up_weight), tok_mine, tok_next)
+    grad_mine, grad_other = halves(grads, core)
+    grad_next = after(grad_other, up_part)
+    dhidden, _ = reduce_gz(lambda x: contract_cols(x, down_weight), grad_mine, grad_next)
+
+    sig = jax.nn.sigmoid(gate)
+    hid_mine = (gate * sig * upward).astype(BF16)
+    hid_other = other_core(hid_mine)
+
+    terms = [None] * n
+    ahead = ()
+    for k in list(range(1, n)) + [0]:
+        rows = after(block_rows(hid_mine, hid_other, k, n), *ahead)
+        terms[k] = dot(rows, down_weight).astype(BF16)
+        ahead = (terms[k],)
+    output = reduce_terms(terms)
+
+    dhidden = after(dhidden, *ahead)
+    dg_mine = (dhidden * upward * sig * (1.0 + gate * (1.0 - sig))).astype(BF16)
+    du_mine = (dhidden * gate * sig).astype(BF16)
+    dg_other, du_other = other_core(dg_mine), other_core(du_mine)
+    ahead = ()
+    for k in list(range(1, n)) + [0]:
+        dg = after(block_rows(dg_mine, dg_other, k, n), *ahead)
+        du = block_rows(du_mine, du_other, k, n)
+        terms[k] = (contract_cols(dg, gate_weight) + contract_cols(du, up_weight)).astype(BF16)
+        ahead = (terms[k],)
+    input_grad = reduce_terms(terms)
+
+    def join(mine, other):
+        return jnp.concatenate([mine, other], axis=0)
+
+    all_tokens = join(tok_mine, tok_other)
+    down_grad = weight_grad(join(hid_mine, hid_other), join(grad_mine, grad_other))
+    gate_grad = weight_grad(after(all_tokens, *ahead), join(dg_mine, dg_other))
+    up_grad = weight_grad(after(all_tokens, *ahead), join(du_mine, du_other))
     return (output, input_grad, gate_grad, up_grad, down_grad)
 
 

time: 153 us -> 163 us (1.065)
  waiting for transfers between devices: 51.7 us -> 82.1 us
  other arithmetic: 11.2 us -> 2.16 us
  matrix products: 34.2 us -> 25.2 us
  starting transfers between devices: 34.2 us -> 30.6 us
  local copies, waits for them, and re-layouts: 2 us -> 3.8 us
    ppermute x16, waiting for transfers between devices: 27.5 us -> 62.3 us  [shift(): return lax.ppermute(x, axis, [(i, (i + step) % n) for i in range(n)])]
    ppermute x6 -> x3, waiting for transfers between devices: 24.2 us -> 18.3 us  [shift_chip(): lax.ppermute(x, 'gz', [(i, (i // CORES + step) % chips * CORES + i % CORE...]
    concatenate x7 -> x13, other arithmetic: 6.12 us -> 0.65 us  [the longest x5 0.36 us: join(): return jnp.concatenate([mine, other], axis=0)]
    dot_general x6, matrix products: 19.6 us -> 15 us  [contract_cols(): lax.dot_general(left, right, (((1,), (1,)), ((), ())), preferred_element_...]
    dot_general x6, matrix products: 14.6 us -> 10.2 us  [dot(): return jnp.dot(left, right, preferred_element_type=F32)]
    convert_element_type x8 -> x2, other arithmetic: 4.95 us -> 1.21 us  [the longest x1 0.71 us: body(): dg_mine = (dhidden * upward * sig * (1.0 + gate * (1.0 - sig))).astype(BF16)]
    ppermute x6 -> x3, starting transfers between devices: 7.26 us -> 4.23 us  [shift_chip(): lax.ppermute(x, 'gz', [(i, (i // CORES + step) % chips * CORES + i % CORE...]
    dynamic_slice x0 -> x3, local copies, waits for them, and re-layouts: none -> 2.21 us  [halves(): lax.dynamic_slice_in_dim(x, at * half, half, 0)]
  transfers between devices with their start and end apart: 34 -> 25, of which waited for: 12 -> 15; matrix products, arithmetic and copies ran while one was open for 26% -> 9% of each run, Pallas kernels for 12% -> 11%
where the time goes in v2:
time: 163 us
  waiting for transfers between devices  82.1 us (50%)
  starting transfers between devices  30.6 us (19%)
  matrix products  25.2 us (15%)
  Pallas kernels  18.1 us (11%)
  local copies, waits for them, and re-layouts  3.8 us (2%)
  other arithmetic  2.16 us (1%)
    ppermute x16, waiting for transfers between devices, shift(): return lax.ppermute(x, axis, [(i, (i + step) % n) for i in range(n)])  62.3 us
    ppermute x16, starting transfers between devices, shift(): return lax.ppermute(x, axis, [(i, (i + step) % n) for i in range(n)])  25.4 us
    ppermute x3, waiting for transfers between devices, shift_chip(): lax.ppermute(x, 'gz', [(i, (i // CORES + step) % chips * CORES + i % CORE...  18.3 us
    pallas_call x3, Pallas kernels, weight_grad(): pl.pallas_call(weight_grad_kernel, out_shape=jax.ShapeDtypeStruct((height...  18.1 us
    dot_general x6, matrix products, contract_cols(): lax.dot_general(left, right, (((1,), (1,)), ((), ())), preferred_element_...  15 us
    dot_general x6, matrix products, dot(): return jnp.dot(left, right, preferred_element_type=F32)  10.2 us
    ppermute x3, starting transfers between devices, shift_chip(): lax.ppermute(x, 'gz', [(i, (i // CORES + step) % chips * CORES + i % CORE...  4.23 us
  transfers between devices with their start and end apart: 25, of which 15 were waited for; matrix products, arithmetic and copies ran while one was open for 9% of the time, Pallas kernels for 11%

profile of v2, /device:TPU:0, one launch (start us, length us, event | category | flops | bytes accessed | tf_op | source)
XLA Modules:
  0.0 163.1 jit_solution(18035511051160260297)
XLA Ops:
  0.6 3.0 %collective-permute-start = (bf16[128,2048]{1,0:T(8,128)(2,1)}, bf16[128,2048]{1,0:T(8,128)(2,1)S(1)}, u32[]{:S(2)}, u32[]{:S(2)}) collective-permute-start(bf16[128,2048]{1,0:T(8,128)(2,1)} %param.5), channel_id=1, source_target_pairs={{0,16},{16,0},{1,17},{17,1},{2,18},{18,2},{3,19},{19,3},{4,20},{20... | collective-permute-start | bytes 1572872 | tf_op jit(solution)/shard_map/ppermute | solution.py:60
  3.7 12.1 %collective-permute-done = bf16[128,2048]{1,0:T(8,128)(2,1)S(1)} collective-permute-done((bf16[128,2048]{1,0:T(8,128)(2,1)}, bf16[128,2048]{1,0:T(8,128)(2,1)S(1)}, u32[]{:S(2)}, u32[]{:S(2)}) %collective-permute-start) | collective-permute-done | bytes 524320 | tf_op jit(solution)/shard_map/ppermute | solution.py:60
  15.8 1.7 %collective-permute-start.13 = (bf16[128,2048]{1,0:T(8,128)(2,1)}, bf16[128,2048]{1,0:T(8,128)(2,1)S(1)}, u32[]{:S(2)}, u32[]{:S(2)}) collective-permute-start(bf16[128,2048]{1,0:T(8,128)(2,1)} %param.9), channel_id=1, source_target_pairs={{0,16},{16,0},{1,17},{17,1},{2,18},{18,2},{3,19},{19,3},{4,20},{20... | collective-permute-start | bytes 1572872 | tf_op jit(solution)/shard_map/ppermute | solution.py:60
  17.5 1.1 constant_dynamic-slice_fusion.13
  18.6 1.1 constant_dynamic-slice_fusion.4
  19.7 9.4 %collective-permute-done.13 = bf16[128,2048]{1,0:T(8,128)(2,1)S(1)} collective-permute-done((bf16[128,2048]{1,0:T(8,128)(2,1)}, bf16[128,2048]{1,0:T(8,128)(2,1)S(1)}, u32[]{:S(2)}, u32[]{:S(2)}) %collective-permute-start.13) | collective-permute-done | bytes 524320 | tf_op jit(solution)/shard_map/ppermute | solution.py:60
  29.3 4.4 %convolution_convert_fusion.7 = bf16[128,1792]{1,0:T(8,128)(2,1)S(1)} fusion(bf16[2048,1792]{1,0:T(8,128)(2,1)} %param.6, bf16[64,2048]{1,0:T(8,128)(2,1)S(1)} %get-tuple-element.67, bf16[64,2048]{1,0:T(8,128)(2,1)S(1)} %get-tuple-element.42), kind=kOutput, calls=%fused_computation.12 | convolution fusion | flops 940802048 | bytes 8323072 | tf_op jit(solution)/shard_map/dot_general | solution.py:14
  34.0 1.6 collective-permute-done.1
  35.5 1.2 fusion.3
  37.0 1.1 convolution_convert_fusion.5
  38.9 1.5 collective-permute-start.2
  40.3 1.2 fusion.4
  41.5 1.3 collective-permute-start.4
  42.8 2.5 %convolution_convert_fusion.1 = bf16[128,1792]{1,0:T(8,128)(2,1)S(1)} fusion(bf16[128,2048]{1,0:T(8,128)(2,1)S(1)} %pad_maximum_fusion.8, bf16[1792,2048]{1,0:T(8,128)(2,1)S(1)} %bitcast.24), kind=kOutput, calls=%fused_computation.6 | convolution fusion | flops 939753472 | bytes 8323072 | tf_op jit(solution)/shard_map/dot_general | solution.py:18
  45.5 6.8 %collective-permute-done.2 = bf16[128,1792]{1,0:T(8,128)(2,1)S(1)} collective-permute-done((bf16[128,1792]{1,0:T(8,128)(2,1)S(1)}, bf16[128,1792]{1,0:T(8,128)(2,1)S(1)}, u32[]{:S(2)}, u32[]{:S(2)}) %collective-permute-start.2) | collective-permute-done | bytes 458784 | tf_op jit(solution)/shard_map/ppermute | solution.py:71
  52.3 8.9 %collective-permute-done.4 = bf16[128,1792]{1,0:T(8,128)(2,1)S(1)} collective-permute-done((bf16[128,1792]{1,0:T(8,128)(2,1)S(1)}, bf16[128,1792]{1,0:T(8,128)(2,1)S(1)}, u32[]{:S(2)}, u32[]{:S(2)}) %collective-permute-start.4) | collective-permute-done | bytes 458784 | tf_op jit(solution)/shard_map/ppermute | solution.py:71
  61.8 2.5 %fusion.5 = (bf16[128,1792]{1,0:T(8,128)(2,1)S(1)}, f32[128,1792]{1,0:T(8,128)S(1)}) fusion(bf16[128,1792]{1,0:T(8,128)(2,1)S(1)} %collective-permute-done.14, bf16[128,2048]{1,0:T(8,128)(2,1)S(1)} %pad_maximum_fusion.7, bf16[1792,2048]{1,0:T(8,128)(2,1)S(1)} %bitcast.24), kind=kOutput, calls=%fused_computation.32 | convolution fusion | flops 940670976 | bytes 9699328 | tf_op jit(solution)/shard_map/dot_general | solution.py:18
  64.4 1.5 collective-permute-start.15
  66.0 1.2 convolution_convert_fusion.3
  67.2 1.6 collective-permute-start.6
  68.8 6.0 %shard_map.94 = bf16[1792,2048]{1,0:T(8,128)(2,1)} custom-call(bf16[256,1792]{1,0:T(8,128)(2,1)S(1)} %pad_maximum_fusion.4.left_ref, bf16[256,2048]{1,0:T(8,128)(2,1)S(1)} %pad_maximum_fusion.1.right_ref), custom_call_target="tpu_custom_call" | custom-call | flops 1879048192 | bytes 9306112 | tf_op jit(solution)/shard_map/pallas_call | solution.py:40
  74.8 2.5 %collective-permute-done.15 = bf16[128,1792]{1,0:T(8,128)(2,1)S(1)} collective-permute-done((bf16[128,1792]{1,0:T(8,128)(2,1)S(1)}, bf16[128,1792]{1,0:T(8,128)(2,1)S(1)}, u32[]{:S(2)}, u32[]{:S(2)}) %collective-permute-start.15) | collective-permute-done | bytes 458784 | tf_op jit(solution)/shard_map/ppermute | solution.py:71
  77.5 3.7 %collective-permute-done.6 = bf16[128,2048]{1,0:T(8,128)(2,1)S(1)} collective-permute-done((bf16[128,2048]{1,0:T(8,128)(2,1)S(1)}, bf16[128,2048]{1,0:T(8,128)(2,1)S(1)}, u32[]{:S(2)}, u32[]{:S(2)}) %collective-permute-start.6) | collective-permute-done | bytes 524320 | tf_op jit(solution)/shard_map/ppermute | solution.py:60
  81.3 1.2 add_convert_fusion.1
  82.5 1.6 collective-permute-start.7
  84.1 2.2 %collective-permute-start.9 = (bf16[32,2048]{1,0:T(8,128)(2,1)S(1)}, bf16[32,2048]{1,0:T(8,128)(2,1)S(1)}, u32[]{:S(2)}, u32[]{:S(2)}) collective-permute-start(bf16[32,2048]{1,0:T(8,128)(2,1)S(1)} %get-tuple-element.39), channel_id=1, source_target_pairs={{0,12},{4,0},{8,4},{12,8},{1,13},{5,1},{9,5},{13,9},{2,14},{6,2},{... | collective-permute-start | bytes 393224 | tf_op jit(solution)/shard_map/ppermute | solution.py:60
  86.4 0.8 collective-permute-start.8
  88.0 2.7 %collective-permute-done.7 = bf16[32,2048]{1,0:T(8,128)(2,1)S(1)} collective-permute-done((bf16[32,2048]{1,0:T(8,128)(2,1)S(1)}, bf16[32,2048]{1,0:T(8,128)(2,1)S(1)}, u32[]{:S(2)}, u32[]{:S(2)}) %collective-permute-start.7) | collective-permute-done | bytes 131104 | tf_op jit(solution)/shard_map/ppermute | solution.py:60
  91.5 6.2 %collective-permute-done.8 = bf16[32,2048]{1,0:T(8,128)(2,1)S(1)} collective-permute-done((bf16[32,2048]{1,0:T(8,128)(2,1)S(1)}, bf16[32,2048]{1,0:T(8,128)(2,1)S(1)}, u32[]{:S(2)}, u32[]{:S(2)}) %collective-permute-start.8) | collective-permute-done | bytes 131104 | tf_op jit(solution)/shard_map/ppermute | solution.py:60
  98.0 2.4 %collective-permute-start.11 = (bf16[32,2048]{1,0:T(8,128)(2,1)S(1)}, bf16[32,2048]{1,0:T(8,128)(2,1)S(1)}, u32[]{:S(2)}, u32[]{:S(2)}) collective-permute-start(bf16[32,2048]{1,0:T(8,128)(2,1)S(1)} %get-tuple-element.28), channel_id=1, source_target_pairs={{0,8},{4,12},{8,0},{12,4},{1,9},{5,13},{9,1},{13,5},{2,10},{6,14},... | collective-permute-start | bytes 393224 | tf_op jit(solution)/shard_map/ppermute | solution.py:60
  100.4 1.5 collective-permute-start.12
  101.9 4.3 %collective-permute-done.10 = bf16[32,2048]{1,0:T(8,128)(2,1)S(1)} collective-permute-done((bf16[32,2048]{1,0:T(8,128)(2,1)S(1)}, bf16[32,2048]{1,0:T(8,128)(2,1)S(1)}, u32[]{:S(2)}, u32[]{:S(2)}) %collective-permute-start.10) | collective-permute-done | bytes 131104 | tf_op jit(solution)/shard_map/ppermute | solution.py:60
  106.2 4.0 %collective-permute-done.11 = bf16[32,2048]{1,0:T(8,128)(2,1)S(1)} collective-permute-done((bf16[32,2048]{1,0:T(8,128)(2,1)S(1)}, bf16[32,2048]{1,0:T(8,128)(2,1)S(1)}, u32[]{:S(2)}, u32[]{:S(2)}) %collective-permute-start.11) | collective-permute-done | bytes 131104 | tf_op jit(solution)/shard_map/ppermute | solution.py:60
  110.5 2.4 %fusion.6 = f32[128,2048]{1,0:T(8,128)S(1)} fusion(bf16[2048,1792]{1,0:T(8,128)(2,1)S(1)} %bitcast.22, bf16[64,1792]{1,0:T(8,128)(2,1)S(1)} %get-tuple-element.48, bf16[64,1792]{1,0:T(8,128)(2,1)S(1)} %get-tuple-element.46), kind=kOutput, calls=%fused_computation.41 | convolution fusion | flops 940441600 | bytes 8847360 | tf_op jit(solution)/shard_map/dot_general | solution.py:18
  112.9 2.5 %fusion = bf16[128,2048]{1,0:T(8,128)(2,1)S(1)} fusion(f32[128,2048]{1,0:T(8,128)S(1)} %fusion.6, bf16[128,1792]{1,0:T(8,128)(2,1)S(1)} %pad_maximum_fusion.12, bf16[2048,1792]{1,0:T(8,128)(2,1)S(1)} %bitcast.26), kind=kOutput, calls=%fused_computation.2 | convolution fusion | flops 940048384 | bytes 9371648 | tf_op jit(solution)/shard_map/dot_general | solution.py:18
  115.4 1.6 collective-permute-start.18
  117.2 2.5 %fusion.21 = f32[128,2048]{1,0:T(8,128)S(1)} fusion(bf16[128,1792]{1,0:T(8,128)(2,1)S(1)} %pad_maximum_fusion.11, bf16[2048,1792]{1,0:T(8,128)(2,1)S(1)} %bitcast.26), kind=kOutput, calls=%fused_computation.80 | convolution fusion | flops 939524096 | bytes 8847360 | tf_op jit(solution)/shard_map/dot_general | solution.py:18
  119.6 9.7 %collective-permute-done.18 = bf16[128,2048]{1,0:T(8,128)(2,1)S(1)} collective-permute-done((bf16[128,2048]{1,0:T(8,128)(2,1)S(1)}, bf16[128,2048]{1,0:T(8,128)(2,1)S(1)}, u32[]{:S(2)}, u32[]{:S(2)}) %collective-permute-start.18) | collective-permute-done | bytes 524320 | tf_op jit(solution)/shard_map/ppermute | solution.py:60
  129.3 2.5 %add_convert_fusion = bf16[128,2048]{1,0:T(8,128)(2,1)S(1)} fusion(bf16[128,2048]{1,0:T(8,128)(2,1)S(1)} %collective-permute-done.18, f32[128,2048]{1,0:T(8,128)S(1)} %fusion.21, bf16[2048,1792]{1,0:T(8,128)(2,1)S(1)} %bitcast.22, bf16[64,1792]{1,0:T(8,128)(2,1)S(1)} %get-tuple-element.47, bf16[64,1792]{1,0:T(8,128)(2,1)S(1)} %get-tuple-element.45), kind=kOutput, calls=%fused_computation.15 | convolution fusion | flops 942014464 | bytes 9895936 | tf_op jit(solution)/shard_map/dot_general | solution.py:18
  131.8 3.4 %collective-permute-start.19 = (bf16[32,2048]{1,0:T(8,128)(2,1)S(1)}, bf16[32,2048]{1,0:T(8,128)(2,1)S(1)}, u32[]{:S(2)}, u32[]{:S(2)}) collective-permute-start(bf16[32,2048]{1,0:T(8,128)(2,1)S(1)} %get-tuple-element.31), channel_id=1, source_target_pairs={{0,4},{4,8},{8,12},{12,0},{1,5},{5,9},{9,13},{13,1},{2,6},{6,10},{... | collective-permute-start | bytes 393224 | tf_op jit(solution)/shard_map/ppermute | solution.py:60
  135.7 1.0 collective-permute-start.20
  136.7 6.1 %shard_map.93 = bf16[2048,1792]{1,0:T(8,128)(2,1)} custom-call(bf16[256,2048]{1,0:T(8,128)(2,1)S(1)} %pad_maximum_fusion.left_ref, bf16[256,1792]{1,0:T(8,128)(2,1)S(1)} %pad_maximum_fusion.3.right_ref), custom_call_target="tpu_custom_call" | custom-call | flops 1879048192 | bytes 9306112 | tf_op jit(solution)/shard_map/pallas_call | solution.py:40
  142.8 3.8 %collective-permute-done.20 = bf16[32,2048]{1,0:T(8,128)(2,1)S(1)} collective-permute-done((bf16[32,2048]{1,0:T(8,128)(2,1)S(1)}, bf16[32,2048]{1,0:T(8,128)(2,1)S(1)}, u32[]{:S(2)}, u32[]{:S(2)}) %collective-permute-start.20) | collective-permute-done | bytes 131104 | tf_op jit(solution)/shard_map/ppermute | solution.py:60
  146.9 6.1 %shard_map.92 = bf16[2048,1792]{1,0:T(8,128)(2,1)} custom-call(bf16[256,2048]{1,0:T(8,128)(2,1)S(1)} %pad_maximum_fusion.left_ref, bf16[256,1792]{1,0:T(8,128)(2,1)S(1)} %pad_maximum_fusion.2.right_ref), custom_call_target="tpu_custom_call" | custom-call | flops 1879048192 | bytes 9306112 | tf_op jit(solution)/shard_map/pallas_call | solution.py:40
  152.9 2.8 %collective-permute-start.23 = (bf16[32,2048]{1,0:T(8,128)(2,1)S(1)}, bf16[32,2048]{1,0:T(8,128)(2,1)S(1)}, u32[]{:S(2)}, u32[]{:S(2)}) collective-permute-start(bf16[32,2048]{1,0:T(8,128)(2,1)S(1)} %get-tuple-element.26), channel_id=1, source_target_pairs={{0,8},{4,12},{8,0},{12,4},{1,9},{5,13},{9,1},{13,5},{2,10},{6,14},... | collective-permute-start | bytes 393224 | tf_op jit(solution)/shard_map/ppermute | solution.py:60
  155.8 1.0 collective-permute-start.24
  156.7 5.5 %collective-permute-done.23 = bf16[32,2048]{1,0:T(8,128)(2,1)S(1)} collective-permute-done((bf16[32,2048]{1,0:T(8,128)(2,1)S(1)}, bf16[32,2048]{1,0:T(8,128)(2,1)S(1)}, u32[]{:S(2)}, u32[]{:S(2)}) %collective-permute-start.23) | collective-permute-done | bytes 131104 | tf_op jit(solution)/shard_map/ppermute | solution.py:60
  162.3 0.8 copy-done
  (73 shorter events, 5.4 us)
Async XLA Ops:
  0.6 15.2 %collective-permute-start = (bf16[128,2048]{1,0:T(8,128)(2,1)}, bf16[128,2048]{1,0:T(8,128)(2,1)S(1)}, u32[]{:S(2)}, u32[]{:S(2)}) collective-permute-start(bf16[128,2048]{1,0:T(8,128)(2,1)} %param.5), channel_id=1, source_target_pairs={{0,16},{16,0},{1,17},{17,1},{2,18},{18,2},{3,19},{19,3},{4,20},{20... | collective-permute-start | bytes 1572872 | tf_op jit(solution)/shard_map/ppermute | solution.py:60
  15.8 13.3 %collective-permute-start.13 = (bf16[128,2048]{1,0:T(8,128)(2,1)}, bf16[128,2048]{1,0:T(8,128)(2,1)S(1)}, u32[]{:S(2)}, u32[]{:S(2)}) collective-permute-start(bf16[128,2048]{1,0:T(8,128)(2,1)} %param.9), channel_id=1, source_target_pairs={{0,16},{16,0},{1,17},{17,1},{2,18},{18,2},{3,19},{19,3},{4,20},{20... | collective-permute-start | bytes 1572872 | tf_op jit(solution)/shard_map/ppermute | solution.py:60
  29.2 6.3 %slice-start.4 = ((s8[7340032]{0:T(1024)(128)(4,1)}), s8[4194304]{0:T(1024)(128)(4,1)S(1)}, s32[]{:S(2)}) async-start(s8[7340032]{0:T(1024)(128)(4,1)} %bitcast.25), calls=%async_computation.4 | async-start | bytes 8388608
  29.3 6.3 %slice-start.5 = ((s8[7340032]{0:T(1024)(128)(4,1)}), s8[3145728]{0:T(1024)(128)(4,1)S(1)}, s32[]{:S(2)}) async-start(s8[7340032]{0:T(1024)(128)(4,1)} %bitcast.25), calls=%async_computation.5 | async-start | bytes 6291456
  33.6 1.9 %collective-permute-start.1 = (bf16[128,1792]{1,0:T(8,128)(2,1)S(1)}, bf16[128,1792]{1,0:T(8,128)(2,1)S(1)}, u32[]{:S(2)}, u32[]{:S(2)}) collective-permute-start(bf16[128,1792]{1,0:T(8,128)(2,1)S(1)} %convolution_convert_fusion.7), channel_id=1, source_target_pairs={{0,1},{1,0},{2,3},{3,2},{4,5},{5,4},{6,7},{7,6},{8,9},{9,8},{10,11... | collective-permute-start | bytes 1376264 | tf_op jit(solution)/shard_map/ppermute | solution.py:65
  33.8 2.9 %slice-start = ((s8[7340032]{0:T(1024)(128)(4,1)}), s8[4194304]{0:T(1024)(128)(4,1)S(1)}, s32[]{:S(2)}) async-start(s8[7340032]{0:T(1024)(128)(4,1)} %bitcast.21), calls=%async_computation | async-start | bytes 8388608
  33.9 3.1 %slice-start.1 = ((s8[7340032]{0:T(1024)(128)(4,1)}), s8[3145728]{0:T(1024)(128)(4,1)S(1)}, s32[]{:S(2)}) async-start(s8[7340032]{0:T(1024)(128)(4,1)} %bitcast.21), calls=%async_computation.1 | async-start | bytes 6291456
  38.2 2.2 %collective-permute-start.3 = (bf16[128,1792]{1,0:T(8,128)(2,1)S(1)}, bf16[128,1792]{1,0:T(8,128)(2,1)S(1)}, u32[]{:S(2)}, u32[]{:S(2)}) collective-permute-start(bf16[128,1792]{1,0:T(8,128)(2,1)S(1)} %convolution_convert_fusion.5), channel_id=1, source_target_pairs={{0,1},{1,0},{2,3},{3,2},{4,5},{5,4},{6,7},{7,6},{8,9},{9,8},{10,11... | collective-permute-start | bytes 1376264 | tf_op jit(solution)/shard_map/ppermute | solution.py:65
  38.9 4.0 %slice-start.2 = ((s8[7340032]{0:T(1024)(128)(4,1)}), s8[4194304]{0:T(1024)(128)(4,1)S(1)}, s32[]{:S(2)}) async-start(s8[7340032]{0:T(1024)(128)(4,1)} %bitcast.23), calls=%async_computation.2 | async-start | bytes 8388608
  38.9 4.0 %slice-start.3 = ((s8[7340032]{0:T(1024)(128)(4,1)}), s8[3145728]{0:T(1024)(128)(4,1)S(1)}, s32[]{:S(2)}) async-start(s8[7340032]{0:T(1024)(128)(4,1)} %bitcast.23), calls=%async_computation.3 | async-start | bytes 6291456
  38.9 13.4 %collective-permute-start.2 = (bf16[128,1792]{1,0:T(8,128)(2,1)S(1)}, bf16[128,1792]{1,0:T(8,128)(2,1)S(1)}, u32[]{:S(2)}, u32[]{:S(2)}) collective-permute-start(bf16[128,1792]{1,0:T(8,128)(2,1)S(1)} %get-tuple-element.59), channel_id=1, source_target_pairs={{0,2},{1,3},{2,0},{3,1},{4,6},{5,7},{6,4},{7,5},{8,10},{9,11},{10,... | collective-permute-start | bytes 1376264 | tf_op jit(solution)/shard_map/ppermute | solution.py:71
  41.5 19.7 %collective-permute-start.4 = (bf16[128,1792]{1,0:T(8,128)(2,1)S(1)}, bf16[128,1792]{1,0:T(8,128)(2,1)S(1)}, u32[]{:S(2)}, u32[]{:S(2)}) collective-permute-start(bf16[128,1792]{1,0:T(8,128)(2,1)S(1)} %get-tuple-element.57), channel_id=1, source_target_pairs={{0,2},{1,3},{2,0},{3,1},{4,6},{5,7},{6,4},{7,5},{8,10},{9,11},{10,... | collective-permute-start | bytes 1376264 | tf_op jit(solution)/shard_map/ppermute | solution.py:71
  45.4 16.4 %collective-permute-start.14 = (bf16[128,1792]{1,0:T(8,128)(2,1)S(1)}, bf16[128,1792]{1,0:T(8,128)(2,1)S(1)}, u32[]{:S(2)}, u32[]{:S(2)}) collective-permute-start(bf16[128,1792]{1,0:T(8,128)(2,1)S(1)} %convolution_convert_fusion.1), channel_id=1, source_target_pairs={{0,1},{1,0},{2,3},{3,2},{4,5},{5,4},{6,7},{7,6},{8,9},{9,8},{10,11... | collective-permute-start | bytes 1376264 | tf_op jit(solution)/shard_map/ppermute | solution.py:65
  61.7 4.1 %collective-permute-start.5 = (bf16[128,1792]{1,0:T(8,128)(2,1)S(1)}, bf16[128,1792]{1,0:T(8,128)(2,1)S(1)}, u32[]{:S(2)}, u32[]{:S(2)}) collective-permute-start(bf16[128,1792]{1,0:T(8,128)(2,1)S(1)} %multiply_convert_fusion.2), channel_id=1, source_target_pairs={{0,1},{1,0},{2,3},{3,2},{4,5},{5,4},{6,7},{7,6},{8,9},{9,8},{10,11... | collective-permute-start | bytes 1376264 | tf_op jit(solution)/shard_map/ppermute | solution.py:65
  64.4 13.0 %collective-permute-start.15 = (bf16[128,1792]{1,0:T(8,128)(2,1)S(1)}, bf16[128,1792]{1,0:T(8,128)(2,1)S(1)}, u32[]{:S(2)}, u32[]{:S(2)}) collective-permute-start(bf16[128,1792]{1,0:T(8,128)(2,1)S(1)} %get-tuple-element.63), channel_id=1, source_target_pairs={{0,2},{1,3},{2,0},{3,1},{4,6},{5,7},{6,4},{7,5},{8,10},{9,11},{10,... | collective-permute-start | bytes 1376264 | tf_op jit(solution)/shard_map/ppermute | solution.py:71
  67.2 14.1 %collective-permute-start.6 = (bf16[128,2048]{1,0:T(8,128)(2,1)S(1)}, bf16[128,2048]{1,0:T(8,128)(2,1)S(1)}, u32[]{:S(2)}, u32[]{:S(2)}) collective-permute-start(bf16[128,2048]{1,0:T(8,128)(2,1)S(1)} %convolution_convert_fusion.3), channel_id=1, source_target_pairs={{0,16},{16,0},{1,17},{17,1},{2,18},{18,2},{3,19},{19,3},{4,20},{20... | collective-permute-start | bytes 1572872 | tf_op jit(solution)/shard_map/ppermute | solution.py:60
  82.5 8.2 %collective-permute-start.7 = (bf16[32,2048]{1,0:T(8,128)(2,1)S(1)}, bf16[32,2048]{1,0:T(8,128)(2,1)S(1)}, u32[]{:S(2)}, u32[]{:S(2)}) collective-permute-start(bf16[32,2048]{1,0:T(8,128)(2,1)S(1)} %get-tuple-element.38), channel_id=1, source_target_pairs={{0,4},{4,8},{8,12},{12,0},{1,5},{5,9},{9,13},{13,1},{2,6},{6,10},{... | collective-permute-start | bytes 393224 | tf_op jit(solution)/shard_map/ppermute | solution.py:60
  84.1 7.3 %collective-permute-start.9 = (bf16[32,2048]{1,0:T(8,128)(2,1)S(1)}, bf16[32,2048]{1,0:T(8,128)(2,1)S(1)}, u32[]{:S(2)}, u32[]{:S(2)}) collective-permute-start(bf16[32,2048]{1,0:T(8,128)(2,1)S(1)} %get-tuple-element.39), channel_id=1, source_target_pairs={{0,12},{4,0},{8,4},{12,8},{1,13},{5,1},{9,5},{13,9},{2,14},{6,2},{... | collective-permute-start | bytes 393224 | tf_op jit(solution)/shard_map/ppermute | solution.py:60
  86.4 11.3 %collective-permute-start.8 = (bf16[32,2048]{1,0:T(8,128)(2,1)S(1)}, bf16[32,2048]{1,0:T(8,128)(2,1)S(1)}, u32[]{:S(2)}, u32[]{:S(2)}) collective-permute-start(bf16[32,2048]{1,0:T(8,128)(2,1)S(1)} %get-tuple-element.40), channel_id=1, source_target_pairs={{0,8},{4,12},{8,0},{12,4},{1,9},{5,13},{9,1},{13,5},{2,10},{6,14},... | collective-permute-start | bytes 393224 | tf_op jit(solution)/shard_map/ppermute | solution.py:60
  87.9 22.4 %collective-permute-start.16 = (bf16[128,1792]{1,0:T(8,128)(2,1)S(1)}, bf16[128,1792]{1,0:T(8,128)(2,1)S(1)}, u32[]{:S(2)}, u32[]{:S(2)}) collective-permute-start(bf16[128,1792]{1,0:T(8,128)(2,1)S(1)} %get-tuple-element.29), channel_id=1, source_target_pairs={{0,1},{1,0},{2,3},{3,2},{4,5},{5,4},{6,7},{7,6},{8,9},{9,8},{10,11... | collective-permute-start | bytes 1376264 | tf_op jit(solution)/shard_map/ppermute | solution.py:65
  97.8 8.4 %collective-permute-start.10 = (bf16[32,2048]{1,0:T(8,128)(2,1)S(1)}, bf16[32,2048]{1,0:T(8,128)(2,1)S(1)}, u32[]{:S(2)}, u32[]{:S(2)}) collective-permute-start(bf16[32,2048]{1,0:T(8,128)(2,1)S(1)} %get-tuple-element.28), channel_id=1, source_target_pairs={{0,4},{4,8},{8,12},{12,0},{1,5},{5,9},{9,13},{13,1},{2,6},{6,10},{... | collective-permute-start | bytes 393224 | tf_op jit(solution)/shard_map/ppermute | solution.py:60
  97.9 12.5 %collective-permute-start.17 = (bf16[128,1792]{1,0:T(8,128)(2,1)S(1)}, bf16[128,1792]{1,0:T(8,128)(2,1)S(1)}, u32[]{:S(2)}, u32[]{:S(2)}) collective-permute-start(bf16[128,1792]{1,0:T(8,128)(2,1)S(1)} %get-tuple-element.30), channel_id=1, source_target_pairs={{0,1},{1,0},{2,3},{3,2},{4,5},{5,4},{6,7},{7,6},{8,9},{9,8},{10,11... | collective-permute-start | bytes 1376264 | tf_op jit(solution)/shard_map/ppermute | solution.py:65
  98.0 12.3 %collective-permute-start.11 = (bf16[32,2048]{1,0:T(8,128)(2,1)S(1)}, bf16[32,2048]{1,0:T(8,128)(2,1)S(1)}, u32[]{:S(2)}, u32[]{:S(2)}) collective-permute-start(bf16[32,2048]{1,0:T(8,128)(2,1)S(1)} %get-tuple-element.28), channel_id=1, source_target_pairs={{0,8},{4,12},{8,0},{12,4},{1,9},{5,13},{9,1},{13,5},{2,10},{6,14},... | collective-permute-start | bytes 393224 | tf_op jit(solution)/shard_map/ppermute | solution.py:60
  100.4 9.9 %collective-permute-start.12 = (bf16[32,2048]{1,0:T(8,128)(2,1)S(1)}, bf16[32,2048]{1,0:T(8,128)(2,1)S(1)}, u32[]{:S(2)}, u32[]{:S(2)}) collective-permute-start(bf16[32,2048]{1,0:T(8,128)(2,1)S(1)} %get-tuple-element.28), channel_id=1, source_target_pairs={{0,12},{4,0},{8,4},{12,8},{1,13},{5,1},{9,5},{13,9},{2,14},{6,2},{... | collective-permute-start | bytes 393224 | tf_op jit(solution)/shard_map/ppermute | solution.py:60
  110.3 5.1 %copy-start.1 = (bf16[128,2048]{1,0:T(8,128)(2,1)}, bf16[128,2048]{1,0:T(8,128)(2,1)S(1)}, u32[]{:S(2)}) copy-start(bf16[128,2048]{1,0:T(8,128)(2,1)S(1)} %constant_dynamic-update-slice_fusion.4) | copy-start | bytes 1572868
  115.4 13.9 %collective-permute-start.18 = (bf16[128,2048]{1,0:T(8,128)(2,1)S(1)}, bf16[128,2048]{1,0:T(8,128)(2,1)S(1)}, u32[]{:S(2)}, u32[]{:S(2)}) collective-permute-start(bf16[128,2048]{1,0:T(8,128)(2,1)S(1)} %fusion), channel_id=1, source_target_pairs={{0,16},{16,0},{1,17},{17,1},{2,18},{18,2},{3,19},{19,3},{4,20},{20... | collective-permute-start | bytes 1572872 | tf_op jit(solution)/shard_map/ppermute | solution.py:60
  131.8 11.0 %collective-permute-start.19 = (bf16[32,2048]{1,0:T(8,128)(2,1)S(1)}, bf16[32,2048]{1,0:T(8,128)(2,1)S(1)}, u32[]{:S(2)}, u32[]{:S(2)}) collective-permute-start(bf16[32,2048]{1,0:T(8,128)(2,1)S(1)} %get-tuple-element.31), channel_id=1, source_target_pairs={{0,4},{4,8},{8,12},{12,0},{1,5},{5,9},{9,13},{13,1},{2,6},{6,10},{... | collective-permute-start | bytes 393224 | tf_op jit(solution)/shard_map/ppermute | solution.py:60
  135.2 7.6 %collective-permute-start.21 = (bf16[32,2048]{1,0:T(8,128)(2,1)S(1)}, bf16[32,2048]{1,0:T(8,128)(2,1)S(1)}, u32[]{:S(2)}, u32[]{:S(2)}) collective-permute-start(bf16[32,2048]{1,0:T(8,128)(2,1)S(1)} %get-tuple-element.32), channel_id=1, source_target_pairs={{0,12},{4,0},{8,4},{12,8},{1,13},{5,1},{9,5},{13,9},{2,14},{6,2},{... | collective-permute-start | bytes 393224 | tf_op jit(solution)/shard_map/ppermute | solution.py:60
  135.7 11.0 %collective-permute-start.20 = (bf16[32,2048]{1,0:T(8,128)(2,1)S(1)}, bf16[32,2048]{1,0:T(8,128)(2,1)S(1)}, u32[]{:S(2)}, u32[]{:S(2)}) collective-permute-start(bf16[32,2048]{1,0:T(8,128)(2,1)S(1)} %get-tuple-element.33), channel_id=1, source_target_pairs={{0,8},{4,12},{8,0},{12,4},{1,9},{5,13},{9,1},{13,5},{2,10},{6,14},... | collective-permute-start | bytes 393224 | tf_op jit(solution)/shard_map/ppermute | solution.py:60
  146.8 9.9 %collective-permute-start.22 = (bf16[32,2048]{1,0:T(8,128)(2,1)S(1)}, bf16[32,2048]{1,0:T(8,128)(2,1)S(1)}, u32[]{:S(2)}, u32[]{:S(2)}) collective-permute-start(bf16[32,2048]{1,0:T(8,128)(2,1)S(1)} %get-tuple-element.26), channel_id=1, source_target_pairs={{0,4},{4,8},{8,12},{12,0},{1,5},{5,9},{9,13},{13,1},{2,6},{6,10},{... | collective-permute-start | bytes 393224 | tf_op jit(solution)/shard_map/ppermute | solution.py:60
  152.9 9.3 %collective-permute-start.23 = (bf16[32,2048]{1,0:T(8,128)(2,1)S(1)}, bf16[32,2048]{1,0:T(8,128)(2,1)S(1)}, u32[]{:S(2)}, u32[]{:S(2)}) collective-permute-start(bf16[32,2048]{1,0:T(8,128)(2,1)S(1)} %get-tuple-element.26), channel_id=1, source_target_pairs={{0,8},{4,12},{8,0},{12,4},{1,9},{5,13},{9,1},{13,5},{2,10},{6,14},... | collective-permute-start | bytes 393224 | tf_op jit(solution)/shard_map/ppermute | solution.py:60
  155.8 6.5 %collective-permute-start.24 = (bf16[32,2048]{1,0:T(8,128)(2,1)S(1)}, bf16[32,2048]{1,0:T(8,128)(2,1)S(1)}, u32[]{:S(2)}, u32[]{:S(2)}) collective-permute-start(bf16[32,2048]{1,0:T(8,128)(2,1)S(1)} %get-tuple-element.26), channel_id=1, source_target_pairs={{0,12},{4,0},{8,4},{12,8},{1,13},{5,1},{9,5},{13,9},{2,14},{6,2},{... | collective-permute-start | bytes 393224 | tf_op jit(solution)/shard_map/ppermute | solution.py:60
  162.3 0.8 copy-start

commit v3 on v2

--- a/solution.py
+++ b/solution.py
@@ -98,7 +98,7 @@
     sent = total.astype(BF16)
     for k in range(1, lax.axis_size("gz") // CORES):
         total = total + shift_chip(sent, k).astype(F32)
-    return total, kept
+    return total, kept, sent
 
 
 def block_rows(mine, other, k, n):
@@ -106,10 +106,10 @@
     return jnp.concatenate([mine[k * half : (k + 1) * half], other[k * half : (k + 1) * half]], axis=0)
 
 
-def reduce_terms(terms):
+def reduce_terms(terms, *earlier):
     total = terms[0].astype(F32)
     for k in range(1, len(terms)):
-        total = total + shift(terms[k], "gx", -k).astype(F32)
+        total = total + after(shift(terms[k], "gx", -k), *earlier).astype(F32)
     rows, width = total.shape
     n = lax.axis_size("gy")
     me = lax.axis_index("gy")
@@ -139,12 +139,12 @@
     toks = gather_gx(tokens)
     grads = gather_gx(after(out_grad, *toks[1:]))
     tok_mine, tok_other = halves(toks, core)
-    gate, gate_part = reduce_gz(lambda x: dot(x, gate_weight), tok_mine, tok_other)
+    gate, gate_part, _ = reduce_gz(lambda x: dot(x, gate_weight), tok_mine, tok_other)
     tok_next = after(tok_other, gate_part)
-    upward, up_part = reduce_gz(lambda x: dot(x, up_weight), tok_mine, tok_next)
+    upward, _, up_sent = reduce_gz(lambda x: dot(x, up_weight), tok_mine, tok_next)
+    grads = [after(x, up_sent) for x in grads]
     grad_mine, grad_other = halves(grads, core)
-    grad_next = after(grad_other, up_part)
-    dhidden, _ = reduce_gz(lambda x: contract_cols(x, down_weight), grad_mine, grad_next)
+    dhidden, _, _ = reduce_gz(lambda x: contract_cols(x, down_weight), grad_mine, grad_other)
 
     sig = jax.nn.sigmoid(gate)
     hid_mine = (gate * sig * upward).astype(BF16)
@@ -156,7 +156,7 @@
         rows = after(block_rows(hid_mine, hid_other, k, n), *ahead)
         terms[k] = dot(rows, down_weight).astype(BF16)
         ahead = (terms[k],)
-    output = reduce_terms(terms)
+    out_terms = list(terms)
 
     dhidden = after(dhidden, *ahead)
     dg_mine = (dhidden * upward * sig * (1.0 + gate * (1.0 - sig))).astype(BF16)
@@ -168,6 +168,7 @@
         du = block_rows(du_mine, du_other, k, n)
         terms[k] = (contract_cols(dg, gate_weight) + contract_cols(du, up_weight)).astype(BF16)
         ahead = (terms[k],)
+    output = reduce_terms(out_terms, *ahead)
     input_grad = reduce_terms(terms)
 
     def join(mine, other):

time: 163 us -> 144 us (0.88)
  waiting for transfers between devices: 82.1 us -> 62.1 us
  matrix products: 25.2 us -> 30.3 us
  starting transfers between devices: 30.6 us -> 26.9 us
    ppermute x16, waiting for transfers between devices: 62.3 us -> 44.7 us  [shift(): return lax.ppermute(x, axis, [(i, (i + step) % n) for i in range(n)])]
    dot_general x6, matrix products: 10.2 us -> 15.4 us  [dot(): return jnp.dot(left, right, preferred_element_type=F32)]
    ppermute x16, starting transfers between devices: 25.4 us -> 22.5 us  [shift(): return lax.ppermute(x, axis, [(i, (i + step) % n) for i in range(n)])]
    ppermute x3, waiting for transfers between devices: 18.3 us -> 15.7 us  [shift_chip(): lax.ppermute(x, 'gz', [(i, (i // CORES + step) % chips * CORES + i % CORE...]
  transfers between devices with their start and end apart: 25 -> 25, of which waited for: 15 -> 12; matrix products, arithmetic and copies ran while one was open for 9% -> 18% of each run, Pallas kernels for 11% -> 12%
where the time goes in v3:
time: 144 us
  waiting for transfers between devices  62.1 us (43%)
  matrix products  30.3 us (21%)
  starting transfers between devices  26.9 us (19%)
  Pallas kernels  17.9 us (12%)
  other arithmetic  2.54 us (2%)
  local copies, waits for them, and re-layouts  2.48 us (2%)
    ppermute x16, waiting for transfers between devices, shift(): return lax.ppermute(x, axis, [(i, (i + step) % n) for i in range(n)])  44.7 us
    ppermute x16, starting transfers between devices, shift(): return lax.ppermute(x, axis, [(i, (i + step) % n) for i in range(n)])  22.5 us
    pallas_call x3, Pallas kernels, weight_grad(): pl.pallas_call(weight_grad_kernel, out_shape=jax.ShapeDtypeStruct((height...  17.9 us
    ppermute x3, waiting for transfers between devices, shift_chip(): lax.ppermute(x, 'gz', [(i, (i // CORES + step) % chips * CORES + i % CORE...  15.7 us
    dot_general x6, matrix products, dot(): return jnp.dot(left, right, preferred_element_type=F32)  15.4 us
    dot_general x6, matrix products, contract_cols(): lax.dot_general(left, right, (((1,), (1,)), ((), ())), preferred_element_...  14.9 us
    ppermute x3, starting transfers between devices, shift_chip(): lax.ppermute(x, 'gz', [(i, (i // CORES + step) % chips * CORES + i % CORE...  3.43 us
  transfers between devices with their start and end apart: 25, of which 12 were waited for; matrix products, arithmetic and copies ran while one was open for 18% of the time, Pallas kernels for 12%

profile of v3, /device:TPU:0, one launch (start us, length us, event | category | flops | bytes accessed | tf_op | source)
XLA Modules:
  0.0 143.5 jit_solution(6180391618258585598)
XLA Ops:
  0.6 3.0 %collective-permute-start = (bf16[128,2048]{1,0:T(8,128)(2,1)}, bf16[128,2048]{1,0:T(8,128)(2,1)S(1)}, u32[]{:S(2)}, u32[]{:S(2)}) collective-permute-start(bf16[128,2048]{1,0:T(8,128)(2,1)} %param.5), channel_id=1, source_target_pairs={{0,16},{16,0},{1,17},{17,1},{2,18},{18,2},{3,19},{19,3},{4,20},{20... | collective-permute-start | bytes 1572872 | tf_op jit(solution)/shard_map/ppermute | solution.py:60
  3.7 1.1 constant_dynamic-slice_fusion.11
  4.7 11.1 %collective-permute-done = bf16[128,2048]{1,0:T(8,128)(2,1)S(1)} collective-permute-done((bf16[128,2048]{1,0:T(8,128)(2,1)}, bf16[128,2048]{1,0:T(8,128)(2,1)S(1)}, u32[]{:S(2)}, u32[]{:S(2)}) %collective-permute-start) | collective-permute-done | bytes 524320 | tf_op jit(solution)/shard_map/ppermute | solution.py:60
  15.9 4.4 %convolution_convert_fusion.7 = bf16[128,1792]{1,0:T(8,128)(2,1)S(1)} fusion(bf16[2048,1792]{1,0:T(8,128)(2,1)} %param.6, bf16[64,2048]{1,0:T(8,128)(2,1)S(1)} %get-tuple-element.47, bf16[64,2048]{1,0:T(8,128)(2,1)S(1)} %get-tuple-element.45), kind=kOutput, calls=%fused_computation.13 | convolution fusion | flops 940802048 | bytes 8323072 | tf_op jit(solution)/shard_map/dot_general | solution.py:14
  20.4 1.7 %collective-permute-done.1 = bf16[128,1792]{1,0:T(8,128)(2,1)S(1)} collective-permute-done((bf16[128,1792]{1,0:T(8,128)(2,1)S(1)}, bf16[128,1792]{1,0:T(8,128)(2,1)S(1)}, u32[]{:S(2)}, u32[]{:S(2)}) %collective-permute-start.1) | collective-permute-done | bytes 458784 | tf_op jit(solution)/shard_map/ppermute | solution.py:65
  22.1 2.0 %fusion.4 = (bf16[128,1792]{1,0:T(8,128)(2,1)}, bf16[128,1792]{1,0:T(8,128)(2,1)S(1)}) fusion(bf16[128,1792]{1,0:T(8,128)(2,1)S(1)} %collective-permute-done.1, bf16[128,2048]{1,0:T(8,128)(2,1)S(1)} %pad_maximum_fusion.5, bf16[2048,1792]{1,0:T(8,128)(2,1)S(1)} %bitcast.27), kind=kOutput, calls=%fused_computation.31 | convolution fusion | flops 940670976 | bytes 9240576 | tf_op jit(solution)/shard_map/dot_general | solution.py:14
  24.1 1.9 %convolution_convert_fusion.5 = bf16[128,1792]{1,0:T(8,128)(2,1)} fusion(bf16[128,2048]{1,0:T(8,128)(2,1)S(1)} %pad_maximum_fusion.6, bf16[2048,1792]{1,0:T(8,128)(2,1)S(1)} %bitcast.23), kind=kOutput, calls=%fused_computation.11 | convolution fusion | flops 939753472 | bytes 8323072 | tf_op jit(solution)/shard_map/dot_general | solution.py:14
  26.2 1.8 %collective-permute-start.7 = (bf16[128,2048]{1,0:T(8,128)(2,1)S(1)}, bf16[128,2048]{1,0:T(8,128)(2,1)S(1)}, u32[]{:S(2)}, u32[]{:S(2)}) collective-permute-start(bf16[128,2048]{1,0:T(8,128)(2,1)S(1)} %copy-done.2), channel_id=1, source_target_pairs={{0,16},{16,0},{1,17},{17,1},{2,18},{18,2},{3,19},{19,3},{4,20},{20... | collective-permute-start | bytes 1572872 | tf_op jit(solution)/shard_map/ppermute | solution.py:60
  28.1 1.6 %collective-permute-start.2 = (bf16[128,1792]{1,0:T(8,128)(2,1)}, bf16[128,1792]{1,0:T(8,128)(2,1)S(1)}, u32[]{:S(2)}, u32[]{:S(2)}) collective-permute-start(bf16[128,1792]{1,0:T(8,128)(2,1)} %get-tuple-element.63), channel_id=1, source_target_pairs={{0,2},{1,3},{2,0},{3,1},{4,6},{5,7},{6,4},{7,5},{8,10},{9,11},{10,... | collective-permute-start | bytes 1376264 | tf_op jit(solution)/shard_map/ppermute | solution.py:71
  29.6 4.8 %fusion.5 = (bf16[128,1792]{1,0:T(8,128)(2,1)S(1)}, f32[128,1792]{1,0:T(8,128)S(1)}) fusion(bf16[128,1792]{1,0:T(8,128)(2,1)S(1)} %collective-permute-done.3, bf16[128,2048]{1,0:T(8,128)(2,1)S(1)} %pad_maximum_fusion.5, bf16[2048,1792]{1,0:T(8,128)(2,1)} %param.7), kind=kOutput, calls=%fused_computation.32 | convolution fusion | flops 940670976 | bytes 9699328 | tf_op jit(solution)/shard_map/dot_general | solution.py:14
  34.4 0.3 collective-permute-start.4
  34.7 5.7 %collective-permute-done.7 = bf16[128,2048]{1,0:T(8,128)(2,1)S(1)} collective-permute-done((bf16[128,2048]{1,0:T(8,128)(2,1)S(1)}, bf16[128,2048]{1,0:T(8,128)(2,1)S(1)}, u32[]{:S(2)}, u32[]{:S(2)}) %collective-permute-start.7) | collective-permute-done | bytes 524320 | tf_op jit(solution)/shard_map/ppermute | solution.py:60
  40.5 2.5 %convolution_convert_fusion.1 = bf16[128,1792]{1,0:T(8,128)(2,1)S(1)} fusion(bf16[1792,2048]{1,0:T(8,128)(2,1)S(1)} %bitcast.21, bf16[64,2048]{1,0:T(8,128)(2,1)S(1)} %get-tuple-element.43, bf16[64,2048]{1,0:T(8,128)(2,1)S(1)} %get-tuple-element.68), kind=kOutput, calls=%fused_computation.6 | convolution fusion | flops 940802048 | bytes 8323072 | tf_op jit(solution)/shard_map/dot_general | solution.py:18
  43.3 7.4 %collective-permute-done.4 = bf16[128,1792]{1,0:T(8,128)(2,1)S(1)} collective-permute-done((bf16[128,1792]{1,0:T(8,128)(2,1)S(1)}, bf16[128,1792]{1,0:T(8,128)(2,1)S(1)}, u32[]{:S(2)}, u32[]{:S(2)}) %collective-permute-start.4) | collective-permute-done | bytes 458784 | tf_op jit(solution)/shard_map/ppermute | solution.py:71
  50.7 0.5 multiply_convert_fusion.2
  51.3 2.6 %fusion.6 = (bf16[128,1792]{1,0:T(8,128)(2,1)S(1)}, f32[128,1792]{1,0:T(8,128)S(1)}) fusion(bf16[128,1792]{1,0:T(8,128)(2,1)S(1)} %collective-permute-done.8, bf16[128,2048]{1,0:T(8,128)(2,1)S(1)} %pad_maximum_fusion.7, bf16[1792,2048]{1,0:T(8,128)(2,1)S(1)} %bitcast.21), kind=kOutput, calls=%fused_computation.33 | convolution fusion | flops 940670976 | bytes 9699328 | tf_op jit(solution)/shard_map/dot_general | solution.py:18
  53.8 1.5 %collective-permute-start.9 = (bf16[128,1792]{1,0:T(8,128)(2,1)S(1)}, bf16[128,1792]{1,0:T(8,128)(2,1)S(1)}, u32[]{:S(2)}, u32[]{:S(2)}) collective-permute-start(bf16[128,1792]{1,0:T(8,128)(2,1)S(1)} %get-tuple-element.65), channel_id=1, source_target_pairs={{0,2},{1,3},{2,0},{3,1},{4,6},{5,7},{6,4},{7,5},{8,10},{9,11},{10,... | collective-permute-start | bytes 1376264 | tf_op jit(solution)/shard_map/ppermute | solution.py:71
  55.5 1.1 convolution_convert_fusion.3
  56.7 0.6 collective-permute-start.6
  57.2 1.2 convolution_convert_fusion.2
  58.4 8.4 %collective-permute-done.9 = bf16[128,1792]{1,0:T(8,128)(2,1)S(1)} collective-permute-done((bf16[128,1792]{1,0:T(8,128)(2,1)S(1)}, bf16[128,1792]{1,0:T(8,128)(2,1)S(1)}, u32[]{:S(2)}, u32[]{:S(2)}) %collective-permute-start.9) | collective-permute-done | bytes 458784 | tf_op jit(solution)/shard_map/ppermute | solution.py:71
  66.9 0.9 multiply_convert_fusion
  68.0 0.5 collective-permute-start.10
  68.5 5.8 %shard_map.94 = bf16[1792,2048]{1,0:T(8,128)(2,1)} custom-call(bf16[256,1792]{1,0:T(8,128)(2,1)S(1)} %pad_maximum_fusion.4.left_ref, bf16[256,2048]{1,0:T(8,128)(2,1)S(1)} %pad_maximum_fusion.1.right_ref), custom_call_target="tpu_custom_call" | custom-call | flops 1879048192 | bytes 9306112 | tf_op jit(solution)/shard_map/pallas_call | solution.py:40
  74.6 2.4 %fusion.10 = f32[128,2048]{1,0:T(8,128)S(1)} fusion(bf16[2048,1792]{1,0:T(8,128)(2,1)S(1)} %bitcast.25, bf16[64,1792]{1,0:T(8,128)(2,1)S(1)} %get-tuple-element.52, bf16[64,1792]{1,0:T(8,128)(2,1)S(1)} %get-tuple-element.50), kind=kOutput, calls=%fused_computation.44 | convolution fusion | flops 940441600 | bytes 8847360 | tf_op jit(solution)/shard_map/dot_general | solution.py:18
  77.0 2.5 %fusion = bf16[128,2048]{1,0:T(8,128)(2,1)S(1)} fusion(f32[128,2048]{1,0:T(8,128)S(1)} %fusion.10, bf16[128,1792]{1,0:T(8,128)(2,1)S(1)} %pad_maximum_fusion.11, bf16[2048,1792]{1,0:T(8,128)(2,1)S(1)} %bitcast.29), kind=kOutput, calls=%fused_computation.2 | convolution fusion | flops 940048384 | bytes 9371648 | tf_op jit(solution)/shard_map/dot_general | solution.py:18
  79.5 0.3 collective-permute-start.18
  79.9 2.4 %fusion.26 = f32[128,2048]{1,0:T(8,128)S(1)} fusion(bf16[128,1792]{1,0:T(8,128)(2,1)S(1)} %pad_maximum_fusion.10, bf16[2048,1792]{1,0:T(8,128)(2,1)S(1)} %bitcast.29), kind=kOutput, calls=%fused_computation.84 | convolution fusion | flops 939524096 | bytes 8847360 | tf_op jit(solution)/shard_map/dot_general | solution.py:18
  82.3 2.5 %fusion.1 = bf16[128,2048]{1,0:T(8,128)(2,1)S(1)} fusion(f32[128,2048]{1,0:T(8,128)S(1)} %fusion.26, bf16[2048,1792]{1,0:T(8,128)(2,1)S(1)} %bitcast.25, bf16[64,1792]{1,0:T(8,128)(2,1)S(1)} %get-tuple-element.51, bf16[64,1792]{1,0:T(8,128)(2,1)S(1)} %get-tuple-element.49), kind=kOutput, calls=%fused_computation.3 | convolution fusion | flops 940965888 | bytes 9371648 | tf_op jit(solution)/shard_map/dot_general | solution.py:18
  85.1 1.8 %collective-permute-start.12 = (bf16[32,2048]{1,0:T(8,128)(2,1)S(1)}, bf16[32,2048]{1,0:T(8,128)(2,1)S(1)}, u32[]{:S(2)}, u32[]{:S(2)}) collective-permute-start(bf16[32,2048]{1,0:T(8,128)(2,1)S(1)} %get-tuple-element.38), channel_id=1, source_target_pairs={{0,4},{4,8},{8,12},{12,0},{1,5},{5,9},{9,13},{13,1},{2,6},{6,10},{... | collective-permute-start | bytes 393224 | tf_op jit(solution)/shard_map/ppermute | solution.py:60
  87.0 2.1 %collective-permute-start.14 = (bf16[32,2048]{1,0:T(8,128)(2,1)S(1)}, bf16[32,2048]{1,0:T(8,128)(2,1)S(1)}, u32[]{:S(2)}, u32[]{:S(2)}) collective-permute-start(bf16[32,2048]{1,0:T(8,128)(2,1)S(1)} %get-tuple-element.39), channel_id=1, source_target_pairs={{0,12},{4,0},{8,4},{12,8},{1,13},{5,1},{9,5},{13,9},{2,14},{6,2},{... | collective-permute-start | bytes 393224 | tf_op jit(solution)/shard_map/ppermute | solution.py:60
  89.1 0.9 collective-permute-start.13
  90.0 6.1 %shard_map.93 = bf16[2048,1792]{1,0:T(8,128)(2,1)} custom-call(bf16[256,2048]{1,0:T(8,128)(2,1)S(1)} %pad_maximum_fusion.left_ref, bf16[256,1792]{1,0:T(8,128)(2,1)S(1)} %pad_maximum_fusion.3.right_ref), custom_call_target="tpu_custom_call" | custom-call | flops 1879048192 | bytes 9306112 | tf_op jit(solution)/shard_map/pallas_call | solution.py:40
  96.1 4.8 %collective-permute-done.13 = bf16[32,2048]{1,0:T(8,128)(2,1)S(1)} collective-permute-done((bf16[32,2048]{1,0:T(8,128)(2,1)S(1)}, bf16[32,2048]{1,0:T(8,128)(2,1)S(1)}, u32[]{:S(2)}, u32[]{:S(2)}) %collective-permute-start.13) | collective-permute-done | bytes 131104 | tf_op jit(solution)/shard_map/ppermute | solution.py:60
  101.1 6.1 %shard_map.92 = bf16[2048,1792]{1,0:T(8,128)(2,1)} custom-call(bf16[256,2048]{1,0:T(8,128)(2,1)S(1)} %pad_maximum_fusion.left_ref, bf16[256,1792]{1,0:T(8,128)(2,1)S(1)} %pad_maximum_fusion.2.right_ref), custom_call_target="tpu_custom_call" | custom-call | flops 1879048192 | bytes 9306112 | tf_op jit(solution)/shard_map/pallas_call | solution.py:40
  107.2 2.2 %collective-permute-start.16 = (bf16[32,2048]{1,0:T(8,128)(2,1)S(1)}, bf16[32,2048]{1,0:T(8,128)(2,1)S(1)}, u32[]{:S(2)}, u32[]{:S(2)}) collective-permute-start(bf16[32,2048]{1,0:T(8,128)(2,1)S(1)} %get-tuple-element.32), channel_id=1, source_target_pairs={{0,8},{4,12},{8,0},{12,4},{1,9},{5,13},{9,1},{13,5},{2,10},{6,14},... | collective-permute-start | bytes 393224 | tf_op jit(solution)/shard_map/ppermute | solution.py:60
  109.4 1.6 %collective-permute-start.17 = (bf16[32,2048]{1,0:T(8,128)(2,1)S(1)}, bf16[32,2048]{1,0:T(8,128)(2,1)S(1)}, u32[]{:S(2)}, u32[]{:S(2)}) collective-permute-start(bf16[32,2048]{1,0:T(8,128)(2,1)S(1)} %get-tuple-element.32), channel_id=1, source_target_pairs={{0,12},{4,0},{8,4},{12,8},{1,13},{5,1},{9,5},{13,9},{2,14},{6,2},{... | collective-permute-start | bytes 393224 | tf_op jit(solution)/shard_map/ppermute | solution.py:60
  111.2 0.6 collective-permute-start.19
  111.8 3.3 %collective-permute-start.21 = (bf16[32,2048]{1,0:T(8,128)(2,1)S(1)}, bf16[32,2048]{1,0:T(8,128)(2,1)S(1)}, u32[]{:S(2)}, u32[]{:S(2)}) collective-permute-start(bf16[32,2048]{1,0:T(8,128)(2,1)S(1)} %get-tuple-element.36), channel_id=1, source_target_pairs={{0,12},{4,0},{8,4},{12,8},{1,13},{5,1},{9,5},{13,9},{2,14},{6,2},{... | collective-permute-start | bytes 393224 | tf_op jit(solution)/shard_map/ppermute | solution.py:60
  115.3 2.9 %collective-permute-done.16 = bf16[32,2048]{1,0:T(8,128)(2,1)S(1)} collective-permute-done((bf16[32,2048]{1,0:T(8,128)(2,1)S(1)}, bf16[32,2048]{1,0:T(8,128)(2,1)S(1)}, u32[]{:S(2)}, u32[]{:S(2)}) %collective-permute-start.16) | collective-permute-done | bytes 131104 | tf_op jit(solution)/shard_map/ppermute | solution.py:60
  118.2 2.8 %collective-permute-done.19 = bf16[32,2048]{1,0:T(8,128)(2,1)S(1)} collective-permute-done((bf16[32,2048]{1,0:T(8,128)(2,1)S(1)}, bf16[32,2048]{1,0:T(8,128)(2,1)S(1)}, u32[]{:S(2)}, u32[]{:S(2)}) %collective-permute-start.19) | collective-permute-done | bytes 131104 | tf_op jit(solution)/shard_map/ppermute | solution.py:60
  121.0 1.1 collective-permute-done.21
  122.1 8.2 %collective-permute-done.20 = bf16[32,2048]{1,0:T(8,128)(2,1)S(1)} collective-permute-done((bf16[32,2048]{1,0:T(8,128)(2,1)S(1)}, bf16[32,2048]{1,0:T(8,128)(2,1)S(1)}, u32[]{:S(2)}, u32[]{:S(2)}) %collective-permute-start.20) | collective-permute-done | bytes 131104 | tf_op jit(solution)/shard_map/ppermute | solution.py:60
  130.6 2.9 %collective-permute-start.23 = (bf16[32,2048]{1,0:T(8,128)(2,1)S(1)}, bf16[32,2048]{1,0:T(8,128)(2,1)S(1)}, u32[]{:S(2)}, u32[]{:S(2)}) collective-permute-start(bf16[32,2048]{1,0:T(8,128)(2,1)S(1)} %get-tuple-element.30), channel_id=1, source_target_pairs={{0,8},{4,12},{8,0},{12,4},{1,9},{5,13},{9,1},{13,5},{2,10},{6,14},... | collective-permute-start | bytes 393224 | tf_op jit(solution)/shard_map/ppermute | solution.py:60
  133.6 1.0 collective-permute-start.24
  134.5 4.3 %collective-permute-done.22 = bf16[32,2048]{1,0:T(8,128)(2,1)S(1)} collective-permute-done((bf16[32,2048]{1,0:T(8,128)(2,1)S(1)}, bf16[32,2048]{1,0:T(8,128)(2,1)S(1)}, u32[]{:S(2)}, u32[]{:S(2)}) %collective-permute-start.22) | collective-permute-done | bytes 131104 | tf_op jit(solution)/shard_map/ppermute | solution.py:60
  138.9 3.8 %collective-permute-done.23 = bf16[32,2048]{1,0:T(8,128)(2,1)S(1)} collective-permute-done((bf16[32,2048]{1,0:T(8,128)(2,1)S(1)}, bf16[32,2048]{1,0:T(8,128)(2,1)S(1)}, u32[]{:S(2)}, u32[]{:S(2)}) %collective-permute-start.23) | collective-permute-done | bytes 131104 | tf_op jit(solution)/shard_map/ppermute | solution.py:60
  142.7 0.8 copy-done
  (85 shorter events, 2.6 us)
Async XLA Ops:
  0.6 15.2 %collective-permute-start = (bf16[128,2048]{1,0:T(8,128)(2,1)}, bf16[128,2048]{1,0:T(8,128)(2,1)S(1)}, u32[]{:S(2)}, u32[]{:S(2)}) collective-permute-start(bf16[128,2048]{1,0:T(8,128)(2,1)} %param.5), channel_id=1, source_target_pairs={{0,16},{16,0},{1,17},{17,1},{2,18},{18,2},{3,19},{19,3},{4,20},{20... | collective-permute-start | bytes 1572872 | tf_op jit(solution)/shard_map/ppermute | solution.py:60
  15.8 6.3 %slice-start.6 = ((s8[7340032]{0:T(1024)(128)(4,1)}), s8[4194304]{0:T(1024)(128)(4,1)S(1)}, s32[]{:S(2)}) async-start(s8[7340032]{0:T(1024)(128)(4,1)} %bitcast.26), calls=%async_computation.6 | async-start | bytes 8388608
  15.8 6.3 %slice-start.7 = ((s8[7340032]{0:T(1024)(128)(4,1)}), s8[3145728]{0:T(1024)(128)(4,1)S(1)}, s32[]{:S(2)}) async-start(s8[7340032]{0:T(1024)(128)(4,1)} %bitcast.26), calls=%async_computation.7 | async-start | bytes 6291456
  20.2 1.9 %collective-permute-start.1 = (bf16[128,1792]{1,0:T(8,128)(2,1)S(1)}, bf16[128,1792]{1,0:T(8,128)(2,1)S(1)}, u32[]{:S(2)}, u32[]{:S(2)}) collective-permute-start(bf16[128,1792]{1,0:T(8,128)(2,1)S(1)} %convolution_convert_fusion.7), channel_id=1, source_target_pairs={{0,1},{1,0},{2,3},{3,2},{4,5},{5,4},{6,7},{7,6},{8,9},{9,8},{10,11... | collective-permute-start | bytes 1376264 | tf_op jit(solution)/shard_map/ppermute | solution.py:65
  20.3 3.8 %slice-start.2 = ((s8[7340032]{0:T(1024)(128)(4,1)}), s8[4194304]{0:T(1024)(128)(4,1)S(1)}, s32[]{:S(2)}) async-start(s8[7340032]{0:T(1024)(128)(4,1)} %bitcast.22), calls=%async_computation.2 | async-start | bytes 8388608
  20.4 3.7 %slice-start.3 = ((s8[7340032]{0:T(1024)(128)(4,1)}), s8[3145728]{0:T(1024)(128)(4,1)S(1)}, s32[]{:S(2)}) async-start(s8[7340032]{0:T(1024)(128)(4,1)} %bitcast.22), calls=%async_computation.3 | async-start | bytes 6291456
  24.1 2.1 %copy-start.2 = (bf16[128,2048]{1,0:T(8,128)(2,1)S(1)}, bf16[128,2048]{1,0:T(8,128)(2,1)}, u32[]{:S(2)}) copy-start(bf16[128,2048]{1,0:T(8,128)(2,1)} %param.9) | copy-start | bytes 1572868
  26.1 3.6 %collective-permute-start.3 = (bf16[128,1792]{1,0:T(8,128)(2,1)}, bf16[128,1792]{1,0:T(8,128)(2,1)S(1)}, u32[]{:S(2)}, u32[]{:S(2)}) collective-permute-start(bf16[128,1792]{1,0:T(8,128)(2,1)} %convolution_convert_fusion.5), channel_id=1, source_target_pairs={{0,1},{1,0},{2,3},{3,2},{4,5},{5,4},{6,7},{7,6},{8,9},{9,8},{10,11... | collective-permute-start | bytes 1376264 | tf_op jit(solution)/shard_map/ppermute | solution.py:65
  26.2 14.2 %collective-permute-start.7 = (bf16[128,2048]{1,0:T(8,128)(2,1)S(1)}, bf16[128,2048]{1,0:T(8,128)(2,1)S(1)}, u32[]{:S(2)}, u32[]{:S(2)}) collective-permute-start(bf16[128,2048]{1,0:T(8,128)(2,1)S(1)} %copy-done.2), channel_id=1, source_target_pairs={{0,16},{16,0},{1,17},{17,1},{2,18},{18,2},{3,19},{19,3},{4,20},{20... | collective-permute-start | bytes 1572872 | tf_op jit(solution)/shard_map/ppermute | solution.py:60
  28.0 12.5 %slice-start = ((s8[7340032]{0:T(1024)(128)(4,1)}), s8[4194304]{0:T(1024)(128)(4,1)S(1)}, s32[]{:S(2)}) async-start(s8[7340032]{0:T(1024)(128)(4,1)} %bitcast.20), calls=%async_computation | async-start | bytes 8388608
  28.0 12.5 %slice-start.1 = ((s8[7340032]{0:T(1024)(128)(4,1)}), s8[3145728]{0:T(1024)(128)(4,1)S(1)}, s32[]{:S(2)}) async-start(s8[7340032]{0:T(1024)(128)(4,1)} %bitcast.20), calls=%async_computation.1 | async-start | bytes 6291456
  28.1 15.3 %collective-permute-start.2 = (bf16[128,1792]{1,0:T(8,128)(2,1)}, bf16[128,1792]{1,0:T(8,128)(2,1)S(1)}, u32[]{:S(2)}, u32[]{:S(2)}) collective-permute-start(bf16[128,1792]{1,0:T(8,128)(2,1)} %get-tuple-element.63), channel_id=1, source_target_pairs={{0,2},{1,3},{2,0},{3,1},{4,6},{5,7},{6,4},{7,5},{8,10},{9,11},{10,... | collective-permute-start | bytes 1376264 | tf_op jit(solution)/shard_map/ppermute | solution.py:71
  34.4 16.3 %collective-permute-start.4 = (bf16[128,1792]{1,0:T(8,128)(2,1)S(1)}, bf16[128,1792]{1,0:T(8,128)(2,1)S(1)}, u32[]{:S(2)}, u32[]{:S(2)}) collective-permute-start(bf16[128,1792]{1,0:T(8,128)(2,1)S(1)} %get-tuple-element.61), channel_id=1, source_target_pairs={{0,2},{1,3},{2,0},{3,1},{4,6},{5,7},{6,4},{7,5},{8,10},{9,11},{10,... | collective-permute-start | bytes 1376264 | tf_op jit(solution)/shard_map/ppermute | solution.py:71
  43.1 8.2 %collective-permute-start.8 = (bf16[128,1792]{1,0:T(8,128)(2,1)S(1)}, bf16[128,1792]{1,0:T(8,128)(2,1)S(1)}, u32[]{:S(2)}, u32[]{:S(2)}) collective-permute-start(bf16[128,1792]{1,0:T(8,128)(2,1)S(1)} %convolution_convert_fusion.1), channel_id=1, source_target_pairs={{0,1},{1,0},{2,3},{3,2},{4,5},{5,4},{6,7},{7,6},{8,9},{9,8},{10,11... | collective-permute-start | bytes 1376264 | tf_op jit(solution)/shard_map/ppermute | solution.py:65
  51.2 4.2 %collective-permute-start.5 = (bf16[128,1792]{1,0:T(8,128)(2,1)S(1)}, bf16[128,1792]{1,0:T(8,128)(2,1)S(1)}, u32[]{:S(2)}, u32[]{:S(2)}) collective-permute-start(bf16[128,1792]{1,0:T(8,128)(2,1)S(1)} %multiply_convert_fusion.2), channel_id=1, source_target_pairs={{0,1},{1,0},{2,3},{3,2},{4,5},{5,4},{6,7},{7,6},{8,9},{9,8},{10,11... | collective-permute-start | bytes 1376264 | tf_op jit(solution)/shard_map/ppermute | solution.py:65
  53.8 13.0 %collective-permute-start.9 = (bf16[128,1792]{1,0:T(8,128)(2,1)S(1)}, bf16[128,1792]{1,0:T(8,128)(2,1)S(1)}, u32[]{:S(2)}, u32[]{:S(2)}) collective-permute-start(bf16[128,1792]{1,0:T(8,128)(2,1)S(1)} %get-tuple-element.65), channel_id=1, source_target_pairs={{0,2},{1,3},{2,0},{3,1},{4,6},{5,7},{6,4},{7,5},{8,10},{9,11},{10,... | collective-permute-start | bytes 1376264 | tf_op jit(solution)/shard_map/ppermute | solution.py:71
  56.7 28.3 %collective-permute-start.6 = (bf16[128,2048]{1,0:T(8,128)(2,1)S(1)}, bf16[128,2048]{1,0:T(8,128)(2,1)S(1)}, u32[]{:S(2)}, u32[]{:S(2)}) collective-permute-start(bf16[128,2048]{1,0:T(8,128)(2,1)S(1)} %convolution_convert_fusion.3), channel_id=1, source_target_pairs={{0,16},{16,0},{1,17},{17,1},{2,18},{18,2},{3,19},{19,3},{4,20},{20... | collective-permute-start | bytes 1572872 | tf_op jit(solution)/shard_map/ppermute | solution.py:60
  67.9 6.6 %collective-permute-start.11 = (bf16[128,1792]{1,0:T(8,128)(2,1)S(1)}, bf16[128,1792]{1,0:T(8,128)(2,1)S(1)}, u32[]{:S(2)}, u32[]{:S(2)}) collective-permute-start(bf16[128,1792]{1,0:T(8,128)(2,1)S(1)} %get-tuple-element.33), channel_id=1, source_target_pairs={{0,1},{1,0},{2,3},{3,2},{4,5},{5,4},{6,7},{7,6},{8,9},{9,8},{10,11... | collective-permute-start | bytes 1376264 | tf_op jit(solution)/shard_map/ppermute | solution.py:65
  67.9 6.6 %slice-start.4 = ((s8[7340032]{0:T(1024)(128)(4,1)}), s8[4194304]{0:T(1024)(128)(4,1)S(1)}, s32[]{:S(2)}) async-start(s8[7340032]{0:T(1024)(128)(4,1)} %bitcast.24), calls=%async_computation.4 | async-start | bytes 8388608
  68.0 6.4 %collective-permute-start.10 = (bf16[128,1792]{1,0:T(8,128)(2,1)S(1)}, bf16[128,1792]{1,0:T(8,128)(2,1)S(1)}, u32[]{:S(2)}, u32[]{:S(2)}) collective-permute-start(bf16[128,1792]{1,0:T(8,128)(2,1)S(1)} %get-tuple-element.34), channel_id=1, source_target_pairs={{0,1},{1,0},{2,3},{3,2},{4,5},{5,4},{6,7},{7,6},{8,9},{9,8},{10,11... | collective-permute-start | bytes 1376264 | tf_op jit(solution)/shard_map/ppermute | solution.py:65
  68.5 6.0 %slice-start.5 = ((s8[7340032]{0:T(1024)(128)(4,1)}), s8[3145728]{0:T(1024)(128)(4,1)S(1)}, s32[]{:S(2)}) async-start(s8[7340032]{0:T(1024)(128)(4,1)} %bitcast.24), calls=%async_computation.5 | async-start | bytes 6291456
  68.5 8.5 %slice-start.8 = ((s8[7340032]{0:T(1024)(128)(4,1)}), s8[4194304]{0:T(1024)(128)(4,1)S(1)}, s32[]{:S(2)}) async-start(s8[7340032]{0:T(1024)(128)(4,1)} %bitcast.28), calls=%async_computation.8 | async-start | bytes 8388608
  74.4 2.6 %slice-start.9 = ((s8[7340032]{0:T(1024)(128)(4,1)}), s8[3145728]{0:T(1024)(128)(4,1)S(1)}, s32[]{:S(2)}) async-start(s8[7340032]{0:T(1024)(128)(4,1)} %bitcast.28), calls=%async_computation.9 | async-start | bytes 6291456
  79.5 31.5 %collective-permute-start.18 = (bf16[128,2048]{1,0:T(8,128)(2,1)S(1)}, bf16[128,2048]{1,0:T(8,128)(2,1)S(1)}, u32[]{:S(2)}, u32[]{:S(2)}) collective-permute-start(bf16[128,2048]{1,0:T(8,128)(2,1)S(1)} %fusion), channel_id=1, source_target_pairs={{0,16},{16,0},{1,17},{17,1},{2,18},{18,2},{3,19},{19,3},{4,20},{20... | collective-permute-start | bytes 1572872 | tf_op jit(solution)/shard_map/ppermute | solution.py:60
  85.1 11.0 %collective-permute-start.12 = (bf16[32,2048]{1,0:T(8,128)(2,1)S(1)}, bf16[32,2048]{1,0:T(8,128)(2,1)S(1)}, u32[]{:S(2)}, u32[]{:S(2)}) collective-permute-start(bf16[32,2048]{1,0:T(8,128)(2,1)S(1)} %get-tuple-element.38), channel_id=1, source_target_pairs={{0,4},{4,8},{8,12},{12,0},{1,5},{5,9},{9,13},{13,1},{2,6},{6,10},{... | collective-permute-start | bytes 393224 | tf_op jit(solution)/shard_map/ppermute | solution.py:60
  87.0 9.1 %collective-permute-start.14 = (bf16[32,2048]{1,0:T(8,128)(2,1)S(1)}, bf16[32,2048]{1,0:T(8,128)(2,1)S(1)}, u32[]{:S(2)}, u32[]{:S(2)}) collective-permute-start(bf16[32,2048]{1,0:T(8,128)(2,1)S(1)} %get-tuple-element.39), channel_id=1, source_target_pairs={{0,12},{4,0},{8,4},{12,8},{1,13},{5,1},{9,5},{13,9},{2,14},{6,2},{... | collective-permute-start | bytes 393224 | tf_op jit(solution)/shard_map/ppermute | solution.py:60
  89.1 11.8 %collective-permute-start.13 = (bf16[32,2048]{1,0:T(8,128)(2,1)S(1)}, bf16[32,2048]{1,0:T(8,128)(2,1)S(1)}, u32[]{:S(2)}, u32[]{:S(2)}) collective-permute-start(bf16[32,2048]{1,0:T(8,128)(2,1)S(1)} %get-tuple-element.40), channel_id=1, source_target_pairs={{0,8},{4,12},{8,0},{12,4},{1,9},{5,13},{9,1},{13,5},{2,10},{6,14},... | collective-permute-start | bytes 393224 | tf_op jit(solution)/shard_map/ppermute | solution.py:60
  101.1 9.9 %collective-permute-start.15 = (bf16[32,2048]{1,0:T(8,128)(2,1)S(1)}, bf16[32,2048]{1,0:T(8,128)(2,1)S(1)}, u32[]{:S(2)}, u32[]{:S(2)}) collective-permute-start(bf16[32,2048]{1,0:T(8,128)(2,1)S(1)} %get-tuple-element.32), channel_id=1, source_target_pairs={{0,4},{4,8},{8,12},{12,0},{1,5},{5,9},{9,13},{13,1},{2,6},{6,10},{... | collective-permute-start | bytes 393224 | tf_op jit(solution)/shard_map/ppermute | solution.py:60
  107.2 11.0 %collective-permute-start.16 = (bf16[32,2048]{1,0:T(8,128)(2,1)S(1)}, bf16[32,2048]{1,0:T(8,128)(2,1)S(1)}, u32[]{:S(2)}, u32[]{:S(2)}) collective-permute-start(bf16[32,2048]{1,0:T(8,128)(2,1)S(1)} %get-tuple-element.32), channel_id=1, source_target_pairs={{0,8},{4,12},{8,0},{12,4},{1,9},{5,13},{9,1},{13,5},{2,10},{6,14},... | collective-permute-start | bytes 393224 | tf_op jit(solution)/shard_map/ppermute | solution.py:60
  109.4 21.2 %collective-permute-start.17 = (bf16[32,2048]{1,0:T(8,128)(2,1)S(1)}, bf16[32,2048]{1,0:T(8,128)(2,1)S(1)}, u32[]{:S(2)}, u32[]{:S(2)}) collective-permute-start(bf16[32,2048]{1,0:T(8,128)(2,1)S(1)} %get-tuple-element.32), channel_id=1, source_target_pairs={{0,12},{4,0},{8,4},{12,8},{1,13},{5,1},{9,5},{13,9},{2,14},{6,2},{... | collective-permute-start | bytes 393224 | tf_op jit(solution)/shard_map/ppermute | solution.py:60
  111.2 9.8 %collective-permute-start.19 = (bf16[32,2048]{1,0:T(8,128)(2,1)S(1)}, bf16[32,2048]{1,0:T(8,128)(2,1)S(1)}, u32[]{:S(2)}, u32[]{:S(2)}) collective-permute-start(bf16[32,2048]{1,0:T(8,128)(2,1)S(1)} %get-tuple-element.35), channel_id=1, source_target_pairs={{0,4},{4,8},{8,12},{12,0},{1,5},{5,9},{9,13},{13,1},{2,6},{6,10},{... | collective-permute-start | bytes 393224 | tf_op jit(solution)/shard_map/ppermute | solution.py:60
  111.8 10.3 %collective-permute-start.21 = (bf16[32,2048]{1,0:T(8,128)(2,1)S(1)}, bf16[32,2048]{1,0:T(8,128)(2,1)S(1)}, u32[]{:S(2)}, u32[]{:S(2)}) collective-permute-start(bf16[32,2048]{1,0:T(8,128)(2,1)S(1)} %get-tuple-element.36), channel_id=1, source_target_pairs={{0,12},{4,0},{8,4},{12,8},{1,13},{5,1},{9,5},{13,9},{2,14},{6,2},{... | collective-permute-start | bytes 393224 | tf_op jit(solution)/shard_map/ppermute | solution.py:60
  115.1 15.3 %collective-permute-start.20 = (bf16[32,2048]{1,0:T(8,128)(2,1)S(1)}, bf16[32,2048]{1,0:T(8,128)(2,1)S(1)}, u32[]{:S(2)}, u32[]{:S(2)}) collective-permute-start(bf16[32,2048]{1,0:T(8,128)(2,1)S(1)} %get-tuple-element.37), channel_id=1, source_target_pairs={{0,8},{4,12},{8,0},{12,4},{1,9},{5,13},{9,1},{13,5},{2,10},{6,14},... | collective-permute-start | bytes 393224 | tf_op jit(solution)/shard_map/ppermute | solution.py:60
  130.5 8.3 %collective-permute-start.22 = (bf16[32,2048]{1,0:T(8,128)(2,1)S(1)}, bf16[32,2048]{1,0:T(8,128)(2,1)S(1)}, u32[]{:S(2)}, u32[]{:S(2)}) collective-permute-start(bf16[32,2048]{1,0:T(8,128)(2,1)S(1)} %get-tuple-element.30), channel_id=1, source_target_pairs={{0,4},{4,8},{8,12},{12,0},{1,5},{5,9},{9,13},{13,1},{2,6},{6,10},{... | collective-permute-start | bytes 393224 | tf_op jit(solution)/shard_map/ppermute | solution.py:60
  130.6 12.1 %copy-start.1 = (bf16[128,2048]{1,0:T(8,128)(2,1)}, bf16[128,2048]{1,0:T(8,128)(2,1)S(1)}, u32[]{:S(2)}) copy-start(bf16[128,2048]{1,0:T(8,128)(2,1)S(1)} %constant_dynamic-update-slice_fusion.4) | copy-start | bytes 1572868
  130.6 12.0 %collective-permute-start.23 = (bf16[32,2048]{1,0:T(8,128)(2,1)S(1)}, bf16[32,2048]{1,0:T(8,128)(2,1)S(1)}, u32[]{:S(2)}, u32[]{:S(2)}) collective-permute-start(bf16[32,2048]{1,0:T(8,128)(2,1)S(1)} %get-tuple-element.30), channel_id=1, source_target_pairs={{0,8},{4,12},{8,0},{12,4},{1,9},{5,13},{9,1},{13,5},{2,10},{6,14},... | collective-permute-start | bytes 393224 | tf_op jit(solution)/shard_map/ppermute | solution.py:60
  133.6 9.1 %collective-permute-start.24 = (bf16[32,2048]{1,0:T(8,128)(2,1)S(1)}, bf16[32,2048]{1,0:T(8,128)(2,1)S(1)}, u32[]{:S(2)}, u32[]{:S(2)}) collective-permute-start(bf16[32,2048]{1,0:T(8,128)(2,1)S(1)} %get-tuple-element.30), channel_id=1, source_target_pairs={{0,12},{4,0},{8,4},{12,8},{1,13},{5,1},{9,5},{13,9},{2,14},{6,2},{... | collective-permute-start | bytes 393224 | tf_op jit(solution)/shard_map/ppermute | solution.py:60
  142.7 0.8 copy-start

commit v4 on v3

--- a/solution.py
+++ b/solution.py
@@ -110,26 +110,31 @@
     total = terms[0].astype(F32)
     for k in range(1, len(terms)):
         total = total + after(shift(terms[k], "gx", -k), *earlier).astype(F32)
-    rows, width = total.shape
+    rows = total.shape[0]
     n = lax.axis_size("gy")
     me = lax.axis_index("gy")
     core = lax.rem(lax.axis_index("gz"), CORES)
-    piece = rows // n
-    total = total.astype(BF16)
-
-    def slot(k):
-        return lax.rem(me + k, n) * piece
-
-    mine = lax.dynamic_slice_in_dim(total, slot(0), piece, 0).astype(F32)
-    for k in range(1, n):
-        mine = mine + shift(lax.dynamic_slice_in_dim(total, slot(k), piece, 0), "gy", k).astype(F32)
-    mine = mine.astype(BF16)
-    result = jnp.zeros((rows, width), BF16)
-    for k in range(n):
-        got = mine if k == 0 else shift(mine, "gy", k)
-        at = lax.rem(slot(n - k) + core * (rows // CORES), rows)
-        result = lax.dynamic_update_slice_in_dim(result, got, at, 0)
-    return result
+    bits = [1 << j for j in range(n.bit_length() - 1)]
+    sides = [lax.rem(me // bit, 2) for bit in bits]
+
+    def swap(x, bit):
+        return lax.ppermute(x, "gy", [(i, i ^ bit) for i in range(n)])
+
+    for bit, side in zip(bits, sides):
+        half = total.shape[0] // 2
+        total_sent = total.astype(BF16)
+        kept = lax.dynamic_slice_in_dim(total_sent, side * half, half, 0)
+        sent = lax.dynamic_slice_in_dim(total_sent, (1 - side) * half, half, 0)
+        total = kept.astype(F32) + swap(sent, bit).astype(F32)
+    result = total.astype(BF16)
+    for bit, side in zip(reversed(bits), reversed(sides)):
+        got = swap(result, bit)
+        first = jnp.where(side == 0, result, got)
+        last = jnp.where(side == 0, got, result)
+        result = jnp.concatenate([first, last], axis=0)
+    return lax.dynamic_slice_in_dim(
+        jnp.concatenate([result, result], axis=0), core * (rows // CORES), rows, 0
+    )
 
 
 def body(tokens, gate_weight, up_weight, down_weight, out_grad):
@@ -158,7 +163,11 @@
         ahead = (terms[k],)
     out_terms = list(terms)
 
-    dhidden = after(dhidden, *ahead)
+    down_grad = weight_grad(
+        jnp.concatenate([hid_mine, hid_other], axis=0),
+        jnp.concatenate([grad_mine, grad_other], axis=0),
+    )
+    dhidden = after(dhidden, down_grad, *ahead)
     dg_mine = (dhidden * upward * sig * (1.0 + gate * (1.0 - sig))).astype(BF16)
     du_mine = (dhidden * gate * sig).astype(BF16)
     dg_other, du_other = other_core(dg_mine), other_core(du_mine)
@@ -175,7 +184,6 @@
         return jnp.concatenate([mine, other], axis=0)
 
     all_tokens = join(tok_mine, tok_other)
-    down_grad = weight_grad(join(hid_mine, hid_other), join(grad_mine, grad_other))
     gate_grad = weight_grad(after(all_tokens, *ahead), join(dg_mine, dg_other))
     up_grad = weight_grad(after(all_tokens, *ahead), join(du_mine, du_other))
     return (output, input_grad, gate_grad, up_grad, down_grad)

time: 144 us -> 136 us (0.944)
  starting transfers between devices: 26.9 us -> 19.3 us
  other arithmetic: 2.54 us -> 5.72 us
  waiting for transfers between devices: 62.1 us -> 59.9 us
    ppermute x0 -> x8, waiting for transfers between devices: none -> 29.8 us  [swap(): return lax.ppermute(x, 'gy', [(i, i ^ bit) for i in range(n)])]
    ppermute x16 -> x4, waiting for transfers between devices: 44.7 us -> 16.7 us  [shift(): return lax.ppermute(x, axis, [(i, (i + step) % n) for i in range(n)])]
    ppermute x16 -> x4, starting transfers between devices: 22.5 us -> 5.72 us  [shift(): return lax.ppermute(x, axis, [(i, (i + step) % n) for i in range(n)])]
    ppermute x0 -> x8, starting transfers between devices: none -> 9.26 us  [swap(): return lax.ppermute(x, 'gy', [(i, i ^ bit) for i in range(n)])]
    ppermute x3, waiting for transfers between devices: 15.7 us -> 9.75 us  [shift_chip(): lax.ppermute(x, 'gz', [(i, (i // CORES + step) % chips * CORES + i % CORE...]
    concatenate x0 -> x6, other arithmetic: none -> 3.26 us  [the longest x2 3.08 us: reduce_terms(): jnp.concatenate([result, result], axis=0)]
    ppermute x6, waiting for transfers between devices: 1.7 us -> 3.62 us  [other_core(): return lax.ppermute(x, 'gz', [(i, i ^ 1) for i in range(n)])]
  transfers between devices with their start and end apart: 25 -> 21, of which waited for: 12 -> 13; matrix products, arithmetic and copies ran while one was open for 18% -> 20% of each run, Pallas kernels for 12% -> 13%
where the time goes in v4:
time: 136 us
  waiting for transfers between devices  59.9 us (44%)
  matrix products  30.3 us (22%)
  starting transfers between devices  19.3 us (14%)
  Pallas kernels  18.1 us (13%)
  other arithmetic  5.72 us (4%)
  local copies, waits for them, and re-layouts  1.52 us (1%)
    ppermute x8, waiting for transfers between devices, swap(): return lax.ppermute(x, 'gy', [(i, i ^ bit) for i in range(n)])  29.8 us
    pallas_call x3, Pallas kernels, weight_grad(): pl.pallas_call(weight_grad_kernel, out_shape=jax.ShapeDtypeStruct((height...  18.1 us
    ppermute x4, waiting for transfers between devices, shift(): return lax.ppermute(x, axis, [(i, (i + step) % n) for i in range(n)])  16.7 us
    dot_general x6, matrix products, dot(): return jnp.dot(left, right, preferred_element_type=F32)  15.3 us
    dot_general x6, matrix products, contract_cols(): lax.dot_general(left, right, (((1,), (1,)), ((), ())), preferred_element_...  14.9 us
    ppermute x3, waiting for transfers between devices, shift_chip(): lax.ppermute(x, 'gz', [(i, (i // CORES + step) % chips * CORES + i % CORE...  9.75 us
    ppermute x8, starting transfers between devices, swap(): return lax.ppermute(x, 'gy', [(i, i ^ bit) for i in range(n)])  9.26 us
    ppermute x4, starting transfers between devices, shift(): return lax.ppermute(x, axis, [(i, (i + step) % n) for i in range(n)])  5.72 us
  transfers between devices with their start and end apart: 21, of which 13 were waited for; matrix products, arithmetic and copies ran while one was open for 20% of the time, Pallas kernels for 13%

profile of v4, /device:TPU:0, one launch (start us, length us, event | category | flops | bytes accessed | tf_op | source)
XLA Modules:
  0.0 136.0 jit_solution(1632055127971163146)
XLA Ops:
  0.6 3.0 %collective-permute-start = (bf16[128,2048]{1,0:T(8,128)(2,1)}, bf16[128,2048]{1,0:T(8,128)(2,1)S(1)}, u32[]{:S(2)}, u32[]{:S(2)}) collective-permute-start(bf16[128,2048]{1,0:T(8,128)(2,1)} %param.5), channel_id=1, source_target_pairs={{0,16},{16,0},{1,17},{17,1},{2,18},{18,2},{3,19},{19,3},{4,20},{20... | collective-permute-start | bytes 1572872 | tf_op jit(solution)/shard_map/ppermute | solution.py:60
  3.7 1.1 constant_dynamic-slice_fusion.9
  4.7 11.1 %collective-permute-done = bf16[128,2048]{1,0:T(8,128)(2,1)S(1)} collective-permute-done((bf16[128,2048]{1,0:T(8,128)(2,1)}, bf16[128,2048]{1,0:T(8,128)(2,1)S(1)}, u32[]{:S(2)}, u32[]{:S(2)}) %collective-permute-start) | collective-permute-done | bytes 524320 | tf_op jit(solution)/shard_map/ppermute | solution.py:60
  15.9 4.4 %convolution_convert_fusion.7 = bf16[128,1792]{1,0:T(8,128)(2,1)S(1)} fusion(bf16[2048,1792]{1,0:T(8,128)(2,1)} %param.6, bf16[64,2048]{1,0:T(8,128)(2,1)S(1)} %get-tuple-element.41, bf16[64,2048]{1,0:T(8,128)(2,1)S(1)} %get-tuple-element.39), kind=kOutput, calls=%fused_computation.13 | convolution fusion | flops 940802048 | bytes 8323072 | tf_op jit(solution)/shard_map/dot_general | solution.py:14
  20.4 1.7 %collective-permute-done.1 = bf16[128,1792]{1,0:T(8,128)(2,1)S(1)} collective-permute-done((bf16[128,1792]{1,0:T(8,128)(2,1)S(1)}, bf16[128,1792]{1,0:T(8,128)(2,1)S(1)}, u32[]{:S(2)}, u32[]{:S(2)}) %collective-permute-start.1) | collective-permute-done | bytes 458784 | tf_op jit(solution)/shard_map/ppermute | solution.py:65
  22.1 2.0 %fusion.4 = (bf16[128,1792]{1,0:T(8,128)(2,1)}, bf16[128,1792]{1,0:T(8,128)(2,1)S(1)}) fusion(bf16[128,1792]{1,0:T(8,128)(2,1)S(1)} %collective-permute-done.1, bf16[128,2048]{1,0:T(8,128)(2,1)S(1)} %pad_maximum_fusion.5, bf16[2048,1792]{1,0:T(8,128)(2,1)S(1)} %bitcast.27), kind=kOutput, calls=%fused_computation.39 | convolution fusion | flops 940670976 | bytes 9240576 | tf_op jit(solution)/shard_map/dot_general | solution.py:14
  24.1 1.9 %convolution_convert_fusion.5 = bf16[128,1792]{1,0:T(8,128)(2,1)} fusion(bf16[128,2048]{1,0:T(8,128)(2,1)S(1)} %pad_maximum_fusion.6, bf16[2048,1792]{1,0:T(8,128)(2,1)S(1)} %bitcast.23), kind=kOutput, calls=%fused_computation.11 | convolution fusion | flops 939753472 | bytes 8323072 | tf_op jit(solution)/shard_map/dot_general | solution.py:14
  26.1 0.1 collective-permute-start.3
  26.2 1.8 %collective-permute-start.7 = (bf16[128,2048]{1,0:T(8,128)(2,1)S(1)}, bf16[128,2048]{1,0:T(8,128)(2,1)S(1)}, u32[]{:S(2)}, u32[]{:S(2)}) collective-permute-start(bf16[128,2048]{1,0:T(8,128)(2,1)S(1)} %copy-done), channel_id=1, source_target_pairs={{0,16},{16,0},{1,17},{17,1},{2,18},{18,2},{3,19},{19,3},{4,20},{20... | collective-permute-start | bytes 1572872 | tf_op jit(solution)/shard_map/ppermute | solution.py:60
  28.1 1.6 %collective-permute-start.2 = (bf16[128,1792]{1,0:T(8,128)(2,1)}, bf16[128,1792]{1,0:T(8,128)(2,1)S(1)}, u32[]{:S(2)}, u32[]{:S(2)}) collective-permute-start(bf16[128,1792]{1,0:T(8,128)(2,1)} %get-tuple-element.61), channel_id=1, source_target_pairs={{0,2},{1,3},{2,0},{3,1},{4,6},{5,7},{6,4},{7,5},{8,10},{9,11},{10,... | collective-permute-start | bytes 1376264 | tf_op jit(solution)/shard_map/ppermute | solution.py:71
  29.6 4.8 %fusion.5 = (bf16[128,1792]{1,0:T(8,128)(2,1)S(1)}, f32[128,1792]{1,0:T(8,128)S(1)}) fusion(bf16[128,1792]{1,0:T(8,128)(2,1)S(1)} %collective-permute-done.3, bf16[128,2048]{1,0:T(8,128)(2,1)S(1)} %pad_maximum_fusion.5, bf16[2048,1792]{1,0:T(8,128)(2,1)} %param.7), kind=kOutput, calls=%fused_computation.40 | convolution fusion | flops 940670976 | bytes 9699328 | tf_op jit(solution)/shard_map/dot_general | solution.py:14
  34.4 0.3 collective-permute-start.4
  34.7 5.7 %collective-permute-done.7 = bf16[128,2048]{1,0:T(8,128)(2,1)S(1)} collective-permute-done((bf16[128,2048]{1,0:T(8,128)(2,1)S(1)}, bf16[128,2048]{1,0:T(8,128)(2,1)S(1)}, u32[]{:S(2)}, u32[]{:S(2)}) %collective-permute-start.7) | collective-permute-done | bytes 524320 | tf_op jit(solution)/shard_map/ppermute | solution.py:60
  40.5 2.5 %convolution_convert_fusion.1 = bf16[128,1792]{1,0:T(8,128)(2,1)S(1)} fusion(bf16[1792,2048]{1,0:T(8,128)(2,1)S(1)} %bitcast.21, bf16[64,2048]{1,0:T(8,128)(2,1)S(1)} %get-tuple-element.37, bf16[64,2048]{1,0:T(8,128)(2,1)S(1)} %get-tuple-element.66), kind=kOutput, calls=%fused_computation.6 | convolution fusion | flops 940802048 | bytes 8323072 | tf_op jit(solution)/shard_map/dot_general | solution.py:18
  43.3 7.4 %collective-permute-done.4 = bf16[128,1792]{1,0:T(8,128)(2,1)S(1)} collective-permute-done((bf16[128,1792]{1,0:T(8,128)(2,1)S(1)}, bf16[128,1792]{1,0:T(8,128)(2,1)S(1)}, u32[]{:S(2)}, u32[]{:S(2)}) %collective-permute-start.4) | collective-permute-done | bytes 458784 | tf_op jit(solution)/shard_map/ppermute | solution.py:71
  50.7 0.5 multiply_convert_fusion.2
  51.3 2.5 %fusion.6 = (bf16[128,1792]{1,0:T(8,128)(2,1)S(1)}, f32[128,1792]{1,0:T(8,128)S(1)}) fusion(bf16[128,1792]{1,0:T(8,128)(2,1)S(1)} %collective-permute-done.8, bf16[128,2048]{1,0:T(8,128)(2,1)S(1)} %pad_maximum_fusion.7, bf16[1792,2048]{1,0:T(8,128)(2,1)S(1)} %bitcast.21), kind=kOutput, calls=%fused_computation.41 | convolution fusion | flops 940670976 | bytes 9699328 | tf_op jit(solution)/shard_map/dot_general | solution.py:18
  53.8 1.6 %collective-permute-start.9 = (bf16[128,1792]{1,0:T(8,128)(2,1)S(1)}, bf16[128,1792]{1,0:T(8,128)(2,1)S(1)}, u32[]{:S(2)}, u32[]{:S(2)}) collective-permute-start(bf16[128,1792]{1,0:T(8,128)(2,1)S(1)} %get-tuple-element.63), channel_id=1, source_target_pairs={{0,2},{1,3},{2,0},{3,1},{4,6},{5,7},{6,4},{7,5},{8,10},{9,11},{10,... | collective-permute-start | bytes 1376264 | tf_op jit(solution)/shard_map/ppermute | solution.py:71
  55.5 1.1 convolution_convert_fusion.3
  56.7 0.6 collective-permute-start.6
  57.3 6.0 %shard_map.92 = bf16[1792,2048]{1,0:T(8,128)(2,1)} custom-call(bf16[256,1792]{1,0:T(8,128)(2,1)S(1)} %pad_maximum_fusion.2.left_ref, bf16[256,2048]{1,0:T(8,128)(2,1)S(1)} %pad_maximum_fusion.right_ref), custom_call_target="tpu_custom_call" | custom-call | flops 1879048192 | bytes 9306112 | tf_op jit(solution)/shard_map/pallas_call | solution.py:40
  63.3 1.1 convolution_convert_fusion.2
  64.4 2.4 %collective-permute-done.9 = bf16[128,1792]{1,0:T(8,128)(2,1)S(1)} collective-permute-done((bf16[128,1792]{1,0:T(8,128)(2,1)S(1)}, bf16[128,1792]{1,0:T(8,128)(2,1)S(1)}, u32[]{:S(2)}, u32[]{:S(2)}) %collective-permute-start.9) | collective-permute-done | bytes 458784 | tf_op jit(solution)/shard_map/ppermute | solution.py:71
  66.9 0.7 multiply_convert_fusion
  67.8 0.5 collective-permute-start.10
  68.3 1.9 %collective-permute-done.10 = bf16[128,1792]{1,0:T(8,128)(2,1)S(1)} collective-permute-done((bf16[128,1792]{1,0:T(8,128)(2,1)S(1)}, bf16[128,1792]{1,0:T(8,128)(2,1)S(1)}, u32[]{:S(2)}, u32[]{:S(2)}) %collective-permute-start.10) | collective-permute-done | bytes 458784 | tf_op jit(solution)/shard_map/ppermute | solution.py:65
  70.4 2.5 %fusion.16 = f32[128,2048]{1,0:T(8,128)S(1)} fusion(bf16[2048,1792]{1,0:T(8,128)(2,1)S(1)} %bitcast.25, bf16[64,1792]{1,0:T(8,128)(2,1)S(1)} %get-tuple-element.46, bf16[64,1792]{1,0:T(8,128)(2,1)S(1)} %get-tuple-element.44), kind=kOutput, calls=%fused_computation.60 | convolution fusion | flops 940441600 | bytes 8847360 | tf_op jit(solution)/shard_map/dot_general | solution.py:18
  72.9 2.5 %fusion = bf16[128,2048]{1,0:T(8,128)(2,1)S(1)} fusion(f32[128,2048]{1,0:T(8,128)S(1)} %fusion.16, bf16[128,1792]{1,0:T(8,128)(2,1)S(1)} %pad_maximum_fusion.11, bf16[2048,1792]{1,0:T(8,128)(2,1)S(1)} %bitcast.29), kind=kOutput, calls=%fused_computation.2 | convolution fusion | flops 940048384 | bytes 9371648 | tf_op jit(solution)/shard_map/dot_general | solution.py:18
  75.4 0.4 collective-permute-start.16
  75.7 2.4 %fusion.32 = f32[128,2048]{1,0:T(8,128)S(1)} fusion(bf16[128,1792]{1,0:T(8,128)(2,1)S(1)} %pad_maximum_fusion.10, bf16[2048,1792]{1,0:T(8,128)(2,1)S(1)} %bitcast.29), kind=kOutput, calls=%fused_computation.100 | convolution fusion | flops 939524096 | bytes 8847360 | tf_op jit(solution)/shard_map/dot_general | solution.py:18
  78.2 2.5 %fusion.1 = bf16[128,2048]{1,0:T(8,128)(2,1)S(1)} fusion(f32[128,2048]{1,0:T(8,128)S(1)} %fusion.32, bf16[2048,1792]{1,0:T(8,128)(2,1)S(1)} %bitcast.25, bf16[64,1792]{1,0:T(8,128)(2,1)S(1)} %get-tuple-element.45, bf16[64,1792]{1,0:T(8,128)(2,1)S(1)} %get-tuple-element.43), kind=kOutput, calls=%fused_computation.3 | convolution fusion | flops 940965888 | bytes 9371648 | tf_op jit(solution)/shard_map/dot_general | solution.py:18
  80.8 0.1 add_convert_fusion.1
  81.0 1.9 %collective-permute-start.12 = (bf16[64,2048]{1,0:T(8,128)(2,1)S(1)}, bf16[64,2048]{1,0:T(8,128)(2,1)S(1)}, u32[]{:S(2)}, u32[]{:S(2)}) collective-permute-start(bf16[64,2048]{1,0:T(8,128)(2,1)S(1)} %constant_dynamic-slice_fusion.3), channel_id=1, source_target_pairs={{0,4},{4,0},{8,12},{12,8},{1,5},{5,1},{9,13},{13,9},{2,6},{6,2},{1... | collective-permute-start | bytes 786440 | tf_op jit(solution)/shard_map/ppermute | solution.py:121
  82.9 6.1 %shard_map.94 = bf16[2048,1792]{1,0:T(8,128)(2,1)} custom-call(bf16[256,2048]{1,0:T(8,128)(2,1)S(1)} %pad_maximum_fusion.1.left_ref, bf16[256,1792]{1,0:T(8,128)(2,1)S(1)} %pad_maximum_fusion.4.right_ref), custom_call_target="tpu_custom_call" | custom-call | flops 1879048192 | bytes 9306112 | tf_op jit(solution)/shard_map/pallas_call | solution.py:40
  88.9 6.1 %shard_map.93 = bf16[2048,1792]{1,0:T(8,128)(2,1)} custom-call(bf16[256,2048]{1,0:T(8,128)(2,1)S(1)} %pad_maximum_fusion.1.left_ref, bf16[256,1792]{1,0:T(8,128)(2,1)S(1)} %pad_maximum_fusion.3.right_ref), custom_call_target="tpu_custom_call" | custom-call | flops 1879048192 | bytes 9306112 | tf_op jit(solution)/shard_map/pallas_call | solution.py:40
  95.1 2.7 %collective-permute-start.13 = (bf16[32,2048]{1,0:T(8,128)(2,1)S(1)}, bf16[32,2048]{1,0:T(8,128)(2,1)S(1)}, u32[]{:S(2)}, u32[]{:S(2)}) collective-permute-start(bf16[32,2048]{1,0:T(8,128)(2,1)S(1)} %constant_dynamic-slice_fusion.2), channel_id=1, source_target_pairs={{0,8},{4,12},{8,0},{12,4},{1,9},{5,13},{9,1},{13,5},{2,10},{6,14},... | collective-permute-start | bytes 393224 | tf_op jit(solution)/shard_map/ppermute | solution.py:121
  97.9 0.5 collective-permute-start.17
  98.4 5.3 %collective-permute-done.13 = bf16[32,2048]{1,0:T(8,128)(2,1)S(1)} collective-permute-done((bf16[32,2048]{1,0:T(8,128)(2,1)S(1)}, bf16[32,2048]{1,0:T(8,128)(2,1)S(1)}, u32[]{:S(2)}, u32[]{:S(2)}) %collective-permute-start.13) | collective-permute-done | bytes 131104 | tf_op jit(solution)/shard_map/ppermute | solution.py:121
  103.8 1.4 %collective-permute-start.14 = (bf16[32,2048]{1,0:T(8,128)(2,1)S(1)}, bf16[32,2048]{1,0:T(8,128)(2,1)S(1)}, u32[]{:S(2)}, u32[]{:S(2)}) collective-permute-start(bf16[32,2048]{1,0:T(8,128)(2,1)S(1)} %add_convert_fusion.5), channel_id=1, source_target_pairs={{0,8},{4,12},{8,0},{12,4},{1,9},{5,13},{9,1},{13,5},{2,10},{6,14},... | collective-permute-start | bytes 393224 | tf_op jit(solution)/shard_map/ppermute | solution.py:121
  105.2 3.2 %collective-permute-done.17 = bf16[64,2048]{1,0:T(8,128)(2,1)S(1)} collective-permute-done((bf16[64,2048]{1,0:T(8,128)(2,1)S(1)}, bf16[64,2048]{1,0:T(8,128)(2,1)S(1)}, u32[]{:S(2)}, u32[]{:S(2)}) %collective-permute-start.17) | collective-permute-done | bytes 262176 | tf_op jit(solution)/shard_map/ppermute | solution.py:121
  108.6 5.1 %collective-permute-done.14 = bf16[32,2048]{1,0:T(8,128)(2,1)S(1)} collective-permute-done((bf16[32,2048]{1,0:T(8,128)(2,1)S(1)}, bf16[32,2048]{1,0:T(8,128)(2,1)S(1)}, u32[]{:S(2)}, u32[]{:S(2)}) %collective-permute-start.14) | collective-permute-done | bytes 131104 | tf_op jit(solution)/shard_map/ppermute | solution.py:121
  113.7 3.9 %collective-permute-done.18 = bf16[32,2048]{1,0:T(8,128)(2,1)S(1)} collective-permute-done((bf16[32,2048]{1,0:T(8,128)(2,1)S(1)}, bf16[32,2048]{1,0:T(8,128)(2,1)S(1)}, u32[]{:S(2)}, u32[]{:S(2)}) %collective-permute-start.18) | collective-permute-done | bytes 131104 | tf_op jit(solution)/shard_map/ppermute | solution.py:121
  117.8 2.6 %collective-permute-start.15 = (bf16[64,2048]{1,0:T(8,128)(2,1)S(1)}, bf16[64,2048]{1,0:T(8,128)(2,1)S(1)}, u32[]{:S(2)}, u32[]{:S(2)}) collective-permute-start(bf16[64,2048]{1,0:T(8,128)(2,1)S(1)} %pad_maximum_fusion.12), channel_id=1, source_target_pairs={{0,4},{4,0},{8,12},{12,8},{1,5},{5,1},{9,13},{13,9},{2,6},{6,2},{1... | collective-permute-start | bytes 786440 | tf_op jit(solution)/shard_map/ppermute | solution.py:121
  120.5 5.0 %collective-permute-done.19 = bf16[32,2048]{1,0:T(8,128)(2,1)S(1)} collective-permute-done((bf16[32,2048]{1,0:T(8,128)(2,1)S(1)}, bf16[32,2048]{1,0:T(8,128)(2,1)S(1)}, u32[]{:S(2)}, u32[]{:S(2)}) %collective-permute-start.19) | collective-permute-done | bytes 131104 | tf_op jit(solution)/shard_map/ppermute | solution.py:121
  125.6 4.0 %collective-permute-done.15 = bf16[64,2048]{1,0:T(8,128)(2,1)S(1)} collective-permute-done((bf16[64,2048]{1,0:T(8,128)(2,1)S(1)}, bf16[64,2048]{1,0:T(8,128)(2,1)S(1)}, u32[]{:S(2)}, u32[]{:S(2)}) %collective-permute-start.15) | collective-permute-done | bytes 262176 | tf_op jit(solution)/shard_map/ppermute | solution.py:121
  129.7 1.5 %fusion.12 = bf16[128,2048]{1,0:T(8,128)(2,1)} fusion(s32[]{:T(128)S(6)} %select_n.93, bf16[64,2048]{1,0:T(8,128)(2,1)S(1)} %get-tuple-element.34, bf16[64,2048]{1,0:T(8,128)(2,1)S(1)} %get-tuple-element.33), kind=kLoop, calls=%fused_computation.47 | loop fusion | flops 2097152 | bytes 1048580 | tf_op jit(solution)/shard_map/concatenate | solution.py:136
  131.2 3.2 %collective-permute-done.20 = bf16[64,2048]{1,0:T(8,128)(2,1)S(1)} collective-permute-done((bf16[64,2048]{1,0:T(8,128)(2,1)S(1)}, bf16[64,2048]{1,0:T(8,128)(2,1)S(1)}, u32[]{:S(2)}, u32[]{:S(2)}) %collective-permute-start.20) | collective-permute-done | bytes 262176 | tf_op jit(solution)/shard_map/ppermute | solution.py:121
  134.5 1.5 %fusion.9 = bf16[128,2048]{1,0:T(8,128)(2,1)} fusion(s32[]{:T(128)S(6)} %select_n.93, bf16[64,2048]{1,0:T(8,128)(2,1)S(1)} %get-tuple-element.32, bf16[64,2048]{1,0:T(8,128)(2,1)S(1)} %get-tuple-element.31), kind=kLoop, calls=%fused_computation.44 | loop fusion | flops 2097152 | bytes 1048580 | tf_op jit(solution)/shard_map/concatenate | solution.py:136
  (77 shorter events, 2.3 us)
Async XLA Ops:
  0.6 15.2 %collective-permute-start = (bf16[128,2048]{1,0:T(8,128)(2,1)}, bf16[128,2048]{1,0:T(8,128)(2,1)S(1)}, u32[]{:S(2)}, u32[]{:S(2)}) collective-permute-start(bf16[128,2048]{1,0:T(8,128)(2,1)} %param.5), channel_id=1, source_target_pairs={{0,16},{16,0},{1,17},{17,1},{2,18},{18,2},{3,19},{19,3},{4,20},{20... | collective-permute-start | bytes 1572872 | tf_op jit(solution)/shard_map/ppermute | solution.py:60
  15.8 6.3 %slice-start.6 = ((s8[7340032]{0:T(1024)(128)(4,1)}), s8[4194304]{0:T(1024)(128)(4,1)S(1)}, s32[]{:S(2)}) async-start(s8[7340032]{0:T(1024)(128)(4,1)} %bitcast.26), calls=%async_computation.6 | async-start | bytes 8388608
  15.8 6.3 %slice-start.7 = ((s8[7340032]{0:T(1024)(128)(4,1)}), s8[3145728]{0:T(1024)(128)(4,1)S(1)}, s32[]{:S(2)}) async-start(s8[7340032]{0:T(1024)(128)(4,1)} %bitcast.26), calls=%async_computation.7 | async-start | bytes 6291456
  20.2 1.9 %collective-permute-start.1 = (bf16[128,1792]{1,0:T(8,128)(2,1)S(1)}, bf16[128,1792]{1,0:T(8,128)(2,1)S(1)}, u32[]{:S(2)}, u32[]{:S(2)}) collective-permute-start(bf16[128,1792]{1,0:T(8,128)(2,1)S(1)} %convolution_convert_fusion.7), channel_id=1, source_target_pairs={{0,1},{1,0},{2,3},{3,2},{4,5},{5,4},{6,7},{7,6},{8,9},{9,8},{10,11... | collective-permute-start | bytes 1376264 | tf_op jit(solution)/shard_map/ppermute | solution.py:65
  20.4 3.8 %slice-start.2 = ((s8[7340032]{0:T(1024)(128)(4,1)}), s8[4194304]{0:T(1024)(128)(4,1)S(1)}, s32[]{:S(2)}) async-start(s8[7340032]{0:T(1024)(128)(4,1)} %bitcast.22), calls=%async_computation.2 | async-start | bytes 8388608
  20.4 3.7 %slice-start.3 = ((s8[7340032]{0:T(1024)(128)(4,1)}), s8[3145728]{0:T(1024)(128)(4,1)S(1)}, s32[]{:S(2)}) async-start(s8[7340032]{0:T(1024)(128)(4,1)} %bitcast.22), calls=%async_computation.3 | async-start | bytes 6291456
  24.1 2.1 %copy-start = (bf16[128,2048]{1,0:T(8,128)(2,1)S(1)}, bf16[128,2048]{1,0:T(8,128)(2,1)}, u32[]{:S(2)}) copy-start(bf16[128,2048]{1,0:T(8,128)(2,1)} %param.9) | copy-start | bytes 1572868
  26.1 3.6 %collective-permute-start.3 = (bf16[128,1792]{1,0:T(8,128)(2,1)}, bf16[128,1792]{1,0:T(8,128)(2,1)S(1)}, u32[]{:S(2)}, u32[]{:S(2)}) collective-permute-start(bf16[128,1792]{1,0:T(8,128)(2,1)} %convolution_convert_fusion.5), channel_id=1, source_target_pairs={{0,1},{1,0},{2,3},{3,2},{4,5},{5,4},{6,7},{7,6},{8,9},{9,8},{10,11... | collective-permute-start | bytes 1376264 | tf_op jit(solution)/shard_map/ppermute | solution.py:65
  26.2 14.2 %collective-permute-start.7 = (bf16[128,2048]{1,0:T(8,128)(2,1)S(1)}, bf16[128,2048]{1,0:T(8,128)(2,1)S(1)}, u32[]{:S(2)}, u32[]{:S(2)}) collective-permute-start(bf16[128,2048]{1,0:T(8,128)(2,1)S(1)} %copy-done), channel_id=1, source_target_pairs={{0,16},{16,0},{1,17},{17,1},{2,18},{18,2},{3,19},{19,3},{4,20},{20... | collective-permute-start | bytes 1572872 | tf_op jit(solution)/shard_map/ppermute | solution.py:60
  28.0 12.4 %slice-start = ((s8[7340032]{0:T(1024)(128)(4,1)}), s8[4194304]{0:T(1024)(128)(4,1)S(1)}, s32[]{:S(2)}) async-start(s8[7340032]{0:T(1024)(128)(4,1)} %bitcast.20), calls=%async_computation | async-start | bytes 8388608
  28.1 12.4 %slice-start.1 = ((s8[7340032]{0:T(1024)(128)(4,1)}), s8[3145728]{0:T(1024)(128)(4,1)S(1)}, s32[]{:S(2)}) async-start(s8[7340032]{0:T(1024)(128)(4,1)} %bitcast.20), calls=%async_computation.1 | async-start | bytes 6291456
  28.1 15.2 %collective-permute-start.2 = (bf16[128,1792]{1,0:T(8,128)(2,1)}, bf16[128,1792]{1,0:T(8,128)(2,1)S(1)}, u32[]{:S(2)}, u32[]{:S(2)}) collective-permute-start(bf16[128,1792]{1,0:T(8,128)(2,1)} %get-tuple-element.61), channel_id=1, source_target_pairs={{0,2},{1,3},{2,0},{3,1},{4,6},{5,7},{6,4},{7,5},{8,10},{9,11},{10,... | collective-permute-start | bytes 1376264 | tf_op jit(solution)/shard_map/ppermute | solution.py:71
  34.4 16.3 %collective-permute-start.4 = (bf16[128,1792]{1,0:T(8,128)(2,1)S(1)}, bf16[128,1792]{1,0:T(8,128)(2,1)S(1)}, u32[]{:S(2)}, u32[]{:S(2)}) collective-permute-start(bf16[128,1792]{1,0:T(8,128)(2,1)S(1)} %get-tuple-element.59), channel_id=1, source_target_pairs={{0,2},{1,3},{2,0},{3,1},{4,6},{5,7},{6,4},{7,5},{8,10},{9,11},{10,... | collective-permute-start | bytes 1376264 | tf_op jit(solution)/shard_map/ppermute | solution.py:71
  43.1 8.2 %collective-permute-start.8 = (bf16[128,1792]{1,0:T(8,128)(2,1)S(1)}, bf16[128,1792]{1,0:T(8,128)(2,1)S(1)}, u32[]{:S(2)}, u32[]{:S(2)}) collective-permute-start(bf16[128,1792]{1,0:T(8,128)(2,1)S(1)} %convolution_convert_fusion.1), channel_id=1, source_target_pairs={{0,1},{1,0},{2,3},{3,2},{4,5},{5,4},{6,7},{7,6},{8,9},{9,8},{10,11... | collective-permute-start | bytes 1376264 | tf_op jit(solution)/shard_map/ppermute | solution.py:65
  51.2 4.2 %collective-permute-start.5 = (bf16[128,1792]{1,0:T(8,128)(2,1)S(1)}, bf16[128,1792]{1,0:T(8,128)(2,1)S(1)}, u32[]{:S(2)}, u32[]{:S(2)}) collective-permute-start(bf16[128,1792]{1,0:T(8,128)(2,1)S(1)} %multiply_convert_fusion.2), channel_id=1, source_target_pairs={{0,1},{1,0},{2,3},{3,2},{4,5},{5,4},{6,7},{7,6},{8,9},{9,8},{10,11... | collective-permute-start | bytes 1376264 | tf_op jit(solution)/shard_map/ppermute | solution.py:65
  53.8 13.0 %collective-permute-start.9 = (bf16[128,1792]{1,0:T(8,128)(2,1)S(1)}, bf16[128,1792]{1,0:T(8,128)(2,1)S(1)}, u32[]{:S(2)}, u32[]{:S(2)}) collective-permute-start(bf16[128,1792]{1,0:T(8,128)(2,1)S(1)} %get-tuple-element.63), channel_id=1, source_target_pairs={{0,2},{1,3},{2,0},{3,1},{4,6},{5,7},{6,4},{7,5},{8,10},{9,11},{10,... | collective-permute-start | bytes 1376264 | tf_op jit(solution)/shard_map/ppermute | solution.py:71
  56.7 24.2 %collective-permute-start.6 = (bf16[128,2048]{1,0:T(8,128)(2,1)S(1)}, bf16[128,2048]{1,0:T(8,128)(2,1)S(1)}, u32[]{:S(2)}, u32[]{:S(2)}) collective-permute-start(bf16[128,2048]{1,0:T(8,128)(2,1)S(1)} %convolution_convert_fusion.3), channel_id=1, source_target_pairs={{0,16},{16,0},{1,17},{17,1},{2,18},{18,2},{3,19},{19,3},{4,20},{20... | collective-permute-start | bytes 1572872 | tf_op jit(solution)/shard_map/ppermute | solution.py:60
  57.3 13.0 %slice-start.4 = ((s8[7340032]{0:T(1024)(128)(4,1)}), s8[4194304]{0:T(1024)(128)(4,1)S(1)}, s32[]{:S(2)}) async-start(s8[7340032]{0:T(1024)(128)(4,1)} %bitcast.24), calls=%async_computation.4 | async-start | bytes 8388608
  63.3 7.1 %slice-start.5 = ((s8[7340032]{0:T(1024)(128)(4,1)}), s8[3145728]{0:T(1024)(128)(4,1)S(1)}, s32[]{:S(2)}) async-start(s8[7340032]{0:T(1024)(128)(4,1)} %bitcast.24), calls=%async_computation.5 | async-start | bytes 6291456
  67.6 5.2 %slice-start.8 = ((s8[7340032]{0:T(1024)(128)(4,1)}), s8[4194304]{0:T(1024)(128)(4,1)S(1)}, s32[]{:S(2)}) async-start(s8[7340032]{0:T(1024)(128)(4,1)} %bitcast.28), calls=%async_computation.8 | async-start | bytes 8388608
  67.7 2.6 %collective-permute-start.11 = (bf16[128,1792]{1,0:T(8,128)(2,1)S(1)}, bf16[128,1792]{1,0:T(8,128)(2,1)S(1)}, u32[]{:S(2)}, u32[]{:S(2)}) collective-permute-start(bf16[128,1792]{1,0:T(8,128)(2,1)S(1)} %get-tuple-element.29), channel_id=1, source_target_pairs={{0,1},{1,0},{2,3},{3,2},{4,5},{5,4},{6,7},{7,6},{8,9},{9,8},{10,11... | collective-permute-start | bytes 1376264 | tf_op jit(solution)/shard_map/ppermute | solution.py:65
  67.8 2.5 %collective-permute-start.10 = (bf16[128,1792]{1,0:T(8,128)(2,1)S(1)}, bf16[128,1792]{1,0:T(8,128)(2,1)S(1)}, u32[]{:S(2)}, u32[]{:S(2)}) collective-permute-start(bf16[128,1792]{1,0:T(8,128)(2,1)S(1)} %get-tuple-element.30), channel_id=1, source_target_pairs={{0,1},{1,0},{2,3},{3,2},{4,5},{5,4},{6,7},{7,6},{8,9},{9,8},{10,11... | collective-permute-start | bytes 1376264 | tf_op jit(solution)/shard_map/ppermute | solution.py:65
  70.4 2.5 %slice-start.9 = ((s8[7340032]{0:T(1024)(128)(4,1)}), s8[3145728]{0:T(1024)(128)(4,1)S(1)}, s32[]{:S(2)}) async-start(s8[7340032]{0:T(1024)(128)(4,1)} %bitcast.28), calls=%async_computation.9 | async-start | bytes 6291456
  75.4 22.4 %collective-permute-start.16 = (bf16[128,2048]{1,0:T(8,128)(2,1)S(1)}, bf16[128,2048]{1,0:T(8,128)(2,1)S(1)}, u32[]{:S(2)}, u32[]{:S(2)}) collective-permute-start(bf16[128,2048]{1,0:T(8,128)(2,1)S(1)} %fusion), channel_id=1, source_target_pairs={{0,16},{16,0},{1,17},{17,1},{2,18},{18,2},{3,19},{19,3},{4,20},{20... | collective-permute-start | bytes 1572872 | tf_op jit(solution)/shard_map/ppermute | solution.py:60
  81.0 14.0 %collective-permute-start.12 = (bf16[64,2048]{1,0:T(8,128)(2,1)S(1)}, bf16[64,2048]{1,0:T(8,128)(2,1)S(1)}, u32[]{:S(2)}, u32[]{:S(2)}) collective-permute-start(bf16[64,2048]{1,0:T(8,128)(2,1)S(1)} %constant_dynamic-slice_fusion.3), channel_id=1, source_target_pairs={{0,4},{4,0},{8,12},{12,8},{1,5},{5,1},{9,13},{13,9},{2,6},{6,2},{1... | collective-permute-start | bytes 786440 | tf_op jit(solution)/shard_map/ppermute | solution.py:121
  95.1 8.7 %collective-permute-start.13 = (bf16[32,2048]{1,0:T(8,128)(2,1)S(1)}, bf16[32,2048]{1,0:T(8,128)(2,1)S(1)}, u32[]{:S(2)}, u32[]{:S(2)}) collective-permute-start(bf16[32,2048]{1,0:T(8,128)(2,1)S(1)} %constant_dynamic-slice_fusion.2), channel_id=1, source_target_pairs={{0,8},{4,12},{8,0},{12,4},{1,9},{5,13},{9,1},{13,5},{2,10},{6,14},... | collective-permute-start | bytes 393224 | tf_op jit(solution)/shard_map/ppermute | solution.py:121
  97.9 10.5 %collective-permute-start.17 = (bf16[64,2048]{1,0:T(8,128)(2,1)S(1)}, bf16[64,2048]{1,0:T(8,128)(2,1)S(1)}, u32[]{:S(2)}, u32[]{:S(2)}) collective-permute-start(bf16[64,2048]{1,0:T(8,128)(2,1)S(1)} %constant_dynamic-slice_fusion.1), channel_id=1, source_target_pairs={{0,4},{4,0},{8,12},{12,8},{1,5},{5,1},{9,13},{13,9},{2,6},{6,2},{1... | collective-permute-start | bytes 786440 | tf_op jit(solution)/shard_map/ppermute | solution.py:121
  103.8 9.9 %collective-permute-start.14 = (bf16[32,2048]{1,0:T(8,128)(2,1)S(1)}, bf16[32,2048]{1,0:T(8,128)(2,1)S(1)}, u32[]{:S(2)}, u32[]{:S(2)}) collective-permute-start(bf16[32,2048]{1,0:T(8,128)(2,1)S(1)} %add_convert_fusion.5), channel_id=1, source_target_pairs={{0,8},{4,12},{8,0},{12,4},{1,9},{5,13},{9,1},{13,5},{2,10},{6,14},... | collective-permute-start | bytes 393224 | tf_op jit(solution)/shard_map/ppermute | solution.py:121
  108.5 9.2 %collective-permute-start.18 = (bf16[32,2048]{1,0:T(8,128)(2,1)S(1)}, bf16[32,2048]{1,0:T(8,128)(2,1)S(1)}, u32[]{:S(2)}, u32[]{:S(2)}) collective-permute-start(bf16[32,2048]{1,0:T(8,128)(2,1)S(1)} %constant_dynamic-slice_fusion), channel_id=1, source_target_pairs={{0,8},{4,12},{8,0},{12,4},{1,9},{5,13},{9,1},{13,5},{2,10},{6,14},... | collective-permute-start | bytes 393224 | tf_op jit(solution)/shard_map/ppermute | solution.py:121
  117.7 7.7 %collective-permute-start.19 = (bf16[32,2048]{1,0:T(8,128)(2,1)S(1)}, bf16[32,2048]{1,0:T(8,128)(2,1)S(1)}, u32[]{:S(2)}, u32[]{:S(2)}) collective-permute-start(bf16[32,2048]{1,0:T(8,128)(2,1)S(1)} %add_convert_fusion.4), channel_id=1, source_target_pairs={{0,8},{4,12},{8,0},{12,4},{1,9},{5,13},{9,1},{13,5},{2,10},{6,14},... | collective-permute-start | bytes 393224 | tf_op jit(solution)/shard_map/ppermute | solution.py:121
  117.8 11.8 %collective-permute-start.15 = (bf16[64,2048]{1,0:T(8,128)(2,1)S(1)}, bf16[64,2048]{1,0:T(8,128)(2,1)S(1)}, u32[]{:S(2)}, u32[]{:S(2)}) collective-permute-start(bf16[64,2048]{1,0:T(8,128)(2,1)S(1)} %pad_maximum_fusion.12), channel_id=1, source_target_pairs={{0,4},{4,0},{8,12},{12,8},{1,5},{5,1},{9,13},{13,9},{2,6},{6,2},{1... | collective-permute-start | bytes 786440 | tf_op jit(solution)/shard_map/ppermute | solution.py:121
  125.5 8.9 %collective-permute-start.20 = (bf16[64,2048]{1,0:T(8,128)(2,1)S(1)}, bf16[64,2048]{1,0:T(8,128)(2,1)S(1)}, u32[]{:S(2)}, u32[]{:S(2)}) collective-permute-start(bf16[64,2048]{1,0:T(8,128)(2,1)S(1)} %pad_maximum_fusion.13), channel_id=1, source_target_pairs={{0,4},{4,0},{8,12},{12,8},{1,5},{5,1},{9,13},{13,9},{2,6},{6,2},{1... | collective-permute-start | bytes 786440 | tf_op jit(solution)/shard_map/ppermute | solution.py:121
